TPU v7x, 32 devices: a whole 2x2x4 slice. The times are simulated.
32 devices in a mesh: region: 8 (over z, y), sub: 4 (over x, core).
Axes of the slice: x: 2, y: 2, z: 4, core: 2. Of those that a mesh axis runs over, the one named last changes fastest.
Arguments:
- modal_state: float32 [9, 56, 4096], P(None, None, ('region', 'sub')), may hold values from -6 to 6
- deriv_stiff: float32 [3, 56, 56], replicated, may hold values from -0.75 to 0.75
- volume_stiff: float32 [3, 56, 56], replicated, may hold values from -0.5 to 0.5
- local_flux: float32 [4, 56, 56], replicated, may hold values from -0.375 to 0.375
- neighbour_flux: float32 [4, 12, 56, 56], replicated, may hold values from -0.375 to 0.375
- star_matrices: float32 [3, 9, 9, 4096], P(None, None, None, ('region', 'sub')), may hold values from -2 to 2
- plus_flux: float32 [4, 9, 9, 4096], P(None, None, None, ('region', 'sub')), may hold values from -2 to 2
- minus_flux: float32 [4, 9, 9, 4096], P(None, None, None, ('region', 'sub')), may hold values from -2 to 2
- cluster_ids: int32 [4096], P(('region', 'sub')), may hold values from 0 to 2
- face_neighbours: int32 [4, 4096], P(None, ('region', 'sub')), may hold values from 0 to 287
- face_orient: int32 [4, 4096], P(None, ('region', 'sub')), may hold values from 0 to 11
- send_lists: int32 [32, 4, 3, 32], P(('region', 'sub')), may hold values from 0 to 127
- sub_lists: int32 [32, 3, 8], P(('region', 'sub')), may hold values from 0 to 127
Outputs:
- new_state: float32 [9, 56, 4096], P(None, None, ('region', 'sub'))
Inputs may be any that keep to these rules, and one draw needn't show every extreme that they name: `face_neighbours`: values below 128 name elements of the same partition, the next 128 name slots received from neighbouring regions, the last 32 slots received from the region's subpartitions. `send_lists`: every slot of every list is used. `sub_lists`: every slot of every list is used.
All inputs are finite; a program needn't handle non-finite values.
Results may differ from a plain program's by a relative error of at most 0.0003.
Values sent between devices are 32-bit elements; how exact they have to be, the bound alone decides.
No kernel may reach another device: no remote copies, remote signals or barrier semaphores. Data moves between devices by JAX's collectives and lax.ppermute only.
A program may use at most 128 MiB of HBM per device.

v0:
```python
import jax
import jax.numpy as jnp
from jax import lax
from jax.sharding import PartitionSpec as P

NDER = 6


base_step = 0.25
offset_table = (-2, -1, 1, 2)


def passed_along(value, axis, steps):
    count = lax.axis_size(axis)
    pairs = [(source, (source + steps) % count) for source in range(count)]
    return lax.ppermute(value, axis, pairs)


def apply_small(matrix, values):
    running = matrix[:, 0, :][None, :, :] * values[:, 0, :][:, None, :]
    for column in range(1, values.shape[1]):
        running = running + matrix[:, column, :][None, :, :] * values[:, column, :][:, None, :]
    return running


def apply_modes(matrix, values):
    mode_in, quant_count, local_count = values.shape
    product = jnp.dot(
        matrix,
        values.reshape(mode_in, quant_count * local_count),
        precision=lax.Precision.HIGHEST,
        preferred_element_type=jnp.float32,
    )
    return product.reshape(matrix.shape[0], quant_count, local_count)


def predict(start_state, stars, deriv_stiff, cluster_count):
    series = [start_state]
    current = start_state
    for deriv_order in range(NDER - 1):
        running = jnp.zeros_like(current)
        for direction in range(3):
            running = running + apply_small(
                stars[direction], apply_modes(deriv_stiff[direction], current)
            )
        current = -running
        series.append(current)
    results = []
    for cluster in range(cluster_count):
        step_width = base_step * 2.0**cluster
        running = jnp.zeros_like(start_state)
        factor = 1.0
        for deriv_order in range(NDER):
            factor = factor * step_width / (deriv_order + 1)
            running = running + factor * series[deriv_order]
        results.append(running)
    return jnp.stack(results)


def local(
    modal_state,
    deriv_stiff,
    volume_stiff,
    local_flux,
    neighbour_flux,
    star_matrices,
    plus_flux,
    minus_flux,
    cluster_ids,
    face_neighbours,
    face_orient,
    send_lists,
    sub_lists,
):
    quant_count, mode_count, local_count = modal_state.shape
    send_table = send_lists[0]
    cluster_count = send_table.shape[1]
    slot_count = send_table.shape[2]
    sub_slots = sub_lists.shape[2]
    orient_count = neighbour_flux.shape[1]
    state_modes = jnp.transpose(modal_state, (1, 0, 2))
    integrals = predict(state_modes, star_matrices, deriv_stiff, cluster_count)

    def pack(rows):
        picked = jnp.stack(
            [
                jnp.take(integrals[cluster], rows[cluster], axis=2)
                for cluster in range(cluster_count)
            ]
        )
        return picked.reshape(-1)

    outgoing = [pack(send_table[block_index]) for block_index in range(4)]
    arriving = []
    for block_index in range(4):
        arriving.append(
            passed_along(outgoing[3 - block_index], "region", -offset_table[block_index])
        )
    sub_flat = pack(sub_lists[0])
    sub_all = lax.all_gather(sub_flat[None], "sub", axis=0, tiled=True)
    sub_count = sub_all.shape[0]
    own_integral = jnp.zeros_like(state_modes)
    for cluster in range(cluster_count):
        own_integral = jnp.where(
            cluster_ids[None, None, :] == cluster, integrals[cluster], own_integral
        )
    result = state_modes
    for direction in range(3):
        result = result + apply_small(
            star_matrices[direction], apply_modes(volume_stiff[direction], own_integral)
        )
    region_ghost = jnp.stack(arriving).reshape(
        4, cluster_count, mode_count, quant_count, slot_count
    )
    region_ghost = region_ghost.transpose(1, 2, 3, 0, 4).reshape(
        cluster_count, mode_count, quant_count, 4 * slot_count
    )
    sub_ghost = sub_all.reshape(sub_count, cluster_count, mode_count, quant_count, sub_slots)
    sub_ghost = sub_ghost.transpose(1, 2, 3, 0, 4).reshape(
        cluster_count, mode_count, quant_count, sub_count * sub_slots
    )
    partner_pool = jnp.concatenate([integrals, region_ghost, sub_ghost], axis=3)
    pool_width = partner_pool.shape[3]
    pool_flat = partner_pool.transpose(1, 2, 0, 3).reshape(
        mode_count, quant_count, cluster_count * pool_width
    )
    orient_range = jnp.arange(orient_count, dtype=jnp.int32)
    for face_index in range(4):
        result = result - apply_small(
            plus_flux[face_index], apply_modes(local_flux[face_index], own_integral)
        )
        pool_index = cluster_ids * pool_width + face_neighbours[face_index]
        partner = jnp.take(pool_flat, pool_index, axis=2)
        mixed = apply_small(minus_flux[face_index], partner)
        stacked = neighbour_flux[face_index].reshape(orient_count * mode_count, mode_count)
        every_orient = apply_modes(stacked, mixed).reshape(
            orient_count, mode_count, quant_count, local_count
        )
        onehot = (face_orient[face_index][None, :] == orient_range[:, None]).astype(jnp.float32)
        selected = jnp.sum(every_orient * onehot[:, None, None, :], axis=0)
        result = result - selected
    return jnp.transpose(result, (1, 0, 2))


def solution(mesh):
    return jax.shard_map(
        local,
        mesh=mesh,
        in_specs=(
            P(None, None, ("region", "sub")),
            P(),
            P(),
            P(),
            P(),
            P(None, None, None, ("region", "sub")),
            P(None, None, None, ("region", "sub")),
            P(None, None, None, ("region", "sub")),
            P(("region", "sub")),
            P(None, ("region", "sub")),
            P(None, ("region", "sub")),
            P(("region", "sub"), None, None, None),
            P(("region", "sub"), None, None),
        ),
        out_specs=P(None, None, ("region", "sub")),
        check_vma=False,
    )
```

profile of v0, /device:TPU:0, one launch (start us, length us, event | category | flops | bytes accessed | tf_op | source)
XLA Modules:
  0.0 449.3 jit_solution(5600216009484618728)
XLA Ops:
  25.9 9.0 %add_negate_fusion.4 = f32[56,9,128]{0,1,2:T(8,128)S(1)} fusion(f32[56,128]{0,1:T(8,128)} %copy.308, f32[9,128]{0,1:T(8,128)S(1)} %bitcast.1155, f32[56,128]{0,1:T(8,128)} %copy.306, f32[9,128]{0,1:T(8,128)S(1)} %bitcast.1150, f32[56,128]{0,1:T(8,128)} %copy.304, f32[9,128]{0,1:T(8,128)S(1)} %bitcast.1145, f32[56,128]{0,1:T(8,128)} %copy.302, ...), kind=kLoop, calls=%fused_computation.74 | loop fusion | flops 3483648 | bytes 1156608 | tf_op jit(solution)/shard_map/neg | solution.py:46
  53.2 8.8 %add_negate_fusion.3 = f32[56,9,128]{0,1,2:T(8,128)S(1)} fusion(f32[56,128]{0,1:T(8,128)} %copy.336, f32[56,128]{0,1:T(8,128)} %copy.335, f32[56,128]{0,1:T(8,128)} %copy.334, f32[56,128]{0,1:T(8,128)} %copy.333, f32[56,128]{0,1:T(8,128)} %copy.332, f32[56,128]{0,1:T(8,128)} %copy.331, f32[56,128]{0,1:T(8,128)} %copy.330, f32[56,128]{0,1:T(8,128)} %copy.329, ...), kind=kLoop, calls=%fused_computation.73 | loop fusion | flops 3483648 | bytes 1156608 | tf_op jit(solution)/shard_map/neg | solution.py:46
  80.2 9.2 %add_negate_fusion.2 = f32[56,9,128]{0,1,2:T(8,128)S(1)} fusion(f32[56,128]{0,1:T(8,128)} %copy.364, f32[56,128]{0,1:T(8,128)} %copy.363, f32[56,128]{0,1:T(8,128)} %copy.362, f32[56,128]{0,1:T(8,128)} %copy.361, f32[56,128]{0,1:T(8,128)} %copy.360, f32[56,128]{0,1:T(8,128)} %copy.359, f32[56,128]{0,1:T(8,128)} %copy.358, f32[56,128]{0,1:T(8,128)} %copy.357, ...), kind=kLoop, calls=%fused_computation.72 | loop fusion | flops 3483648 | bytes 1156608 | tf_op jit(solution)/shard_map/neg | solution.py:46
  109.2 8.8 %add_negate_fusion.1 = f32[56,9,128]{0,1,2:T(8,128)S(1)} fusion(f32[56,128]{0,1:T(8,128)} %copy.392, f32[56,128]{0,1:T(8,128)} %copy.391, f32[56,128]{0,1:T(8,128)} %copy.390, f32[56,128]{0,1:T(8,128)} %copy.389, f32[56,128]{0,1:T(8,128)} %copy.388, f32[56,128]{0,1:T(8,128)} %copy.387, f32[56,128]{0,1:T(8,128)} %copy.386, f32[56,128]{0,1:T(8,128)} %copy.385, ...), kind=kLoop, calls=%fused_computation.71 | loop fusion | flops 3483648 | bytes 1156608 | tf_op jit(solution)/shard_map/neg | solution.py:46
  146.3 27.5 %select_select_fusion = (f32[56,9,128]{0,1,2:T(8,128)}, f32[56,9,128]{0,1,2:T(8,128)S(1)}, f32[56,9,128]{0,1,2:T(8,128)S(1)}, f32[56,9,128]{0,1,2:T(8,128)S(1)}) fusion(pred[128]{0:T(512)(128)(4,1)S(1)} %get-tuple-element.436, pred[128]{0:T(512)(128)(4,1)S(1)} %get-tuple-element.434, pred[128]{0:T(512)(128)(4,1)S(1)} %get-tuple-element.435, ...), kind=kLoop, calls=%fused_computation.69 | loop fusion | flops 19676160 | bytes 5285760 | tf_op jit(solution)/shard_map/jit(_where)/select_n | solution.py:104
  220.6 3.2 collective-permute-start.2
  274.0 6.3 %all-gather = f32[4,1,12096]{2,1,0:T(1,128)} all-gather(f32[1,1,12096]{2,1,0:T(1,128)S(1)} %reshape.9552), channel_id=1, replica_groups=mesh['region'=8,'sub'=4] {'sub'}, dimensions={0}, use_global_device_ids=true | all-gather | bytes 241920 | tf_op jit(solution)/shard_map/all_gather | solution.py:100
  282.4 4.7 %reshape.9375 = f32[4,3,56,9,8]{4,3,2,1,0:T(8,128)} reshape(f32[4,12096]{1,0:T(4,128)} %reduce) | data formatting | bytes 387072 | tf_op jit(solution)/shard_map/reshape | solution.py:118
  287.1 3.9 copy.438
  362.3 5.9 %copy.490 = f32[56,9,3,288]{0,1,3,2:T(8,128)} copy(f32[56,9,3,288]{3,0,1,2:T(8,128)S(1)} %maximum_bitcast_fusion) | data formatting | bytes 3483648 | tf_op jit(solution)/shard_map/reshape | solution.py:124
  368.2 3.8 gather_fusion.15
  372.0 3.8 gather_fusion.16
  378.7 3.6 convolution_bitcast_fusion.3
  385.3 3.8 fusion.121
  390.9 3.6 convolution_bitcast_fusion.2
  397.6 3.8 gather_fusion.17
  401.4 3.8 gather_fusion.18
  408.1 3.6 convolution_bitcast_fusion.1
  414.7 4.2 fusion.123
  420.7 4.3 convolution_bitcast_fusion
  425.0 5.0 %reshape_reshape.15 = f32[12,56,9,128]{3,2,1,0:T(8,128)} reshape(f32[672,1152]{1,0:T(8,128)} %convolution_bitcast_fusion) | data formatting | bytes 6193152 | tf_op jit(solution)/shard_map/reshape;reshape | solution.py:136
  430.0 3.2 multiply_reduce_fusion.3
  433.3 3.9 multiply_reduce_fusion.2
  439.8 8.5 %bitcast_subtract_fusion = f32[9,56,128]{2,0,1:T(8,128)S(1)} fusion(f32[56,9,128]{2,1,0:T(8,128)S(1)} %multiply_reduce_fusion, f32[56,9,128]{2,1,0:T(8,128)S(1)} %multiply_reduce_fusion.1, f32[56,9,128]{2,1,0:T(8,128)S(1)} %multiply_reduce_fusion.2, f32[56,9,128]{2,1,0:T(8,128)S(1)} %multiply_reduce_fusion.3, f32[9,56,128]{2,1,0:T(8,128)S(1)} %copy-done, ...), kind=kLoop, calls=%fused_computation.79 | loop fusion | flops 8386560 | bytes 3644928 | tf_op jit(solution)/shard_map/sub | solution.py:141
  (912 shorter events, 299.5 us)
Async XLA Ops:
  5.7 103.2 %copy-start.1 = (f32[9,1,128]{0,2,1:T(8,128)}, f32[9,1,128]{0,2,1:T(8,128)S(1)}, u32[]{:S(2)}) copy-start(f32[9,1,128]{0,2,1:T(8,128)S(1)} %copy.604) | copy-start | bytes 13828
  5.8 103.1 %copy-start.2 = (f32[9,1,128]{0,2,1:T(8,128)}, f32[9,1,128]{0,2,1:T(8,128)S(1)}, u32[]{:S(2)}) copy-start(f32[9,1,128]{0,2,1:T(8,128)S(1)} %copy.605) | copy-start | bytes 13828
  5.9 103.0 %copy-start.3 = (f32[9,1,128]{0,2,1:T(8,128)}, f32[9,1,128]{0,2,1:T(8,128)S(1)}, u32[]{:S(2)}) copy-start(f32[9,1,128]{0,2,1:T(8,128)S(1)} %copy.606) | copy-start | bytes 13828
  6.0 102.9 %copy-start.4 = (f32[9,1,128]{0,2,1:T(8,128)}, f32[9,1,128]{0,2,1:T(8,128)S(1)}, u32[]{:S(2)}) copy-start(f32[9,1,128]{0,2,1:T(8,128)S(1)} %copy.607) | copy-start | bytes 13828
  6.2 102.8 %copy-start.5 = (f32[9,1,128]{0,2,1:T(8,128)}, f32[9,1,128]{0,2,1:T(8,128)S(1)}, u32[]{:S(2)}) copy-start(f32[9,1,128]{0,2,1:T(8,128)S(1)} %copy.608) | copy-start | bytes 13828
  6.3 102.7 %copy-start.6 = (f32[9,1,128]{0,2,1:T(8,128)}, f32[9,1,128]{0,2,1:T(8,128)S(1)}, u32[]{:S(2)}) copy-start(f32[9,1,128]{0,2,1:T(8,128)S(1)} %copy.609) | copy-start | bytes 13828
  6.4 102.6 %copy-start.7 = (f32[9,1,128]{0,2,1:T(8,128)}, f32[9,1,128]{0,2,1:T(8,128)S(1)}, u32[]{:S(2)}) copy-start(f32[9,1,128]{0,2,1:T(8,128)S(1)} %copy.610) | copy-start | bytes 13828
  6.7 102.3 %copy-start.8 = (f32[9,1,128]{0,2,1:T(8,128)}, f32[9,1,128]{0,2,1:T(8,128)S(1)}, u32[]{:S(2)}) copy-start(f32[9,1,128]{0,2,1:T(8,128)S(1)} %copy.611) | copy-start | bytes 13828
  6.8 102.2 %copy-start.9 = (f32[9,1,128]{0,2,1:T(8,128)}, f32[9,1,128]{0,2,1:T(8,128)S(1)}, u32[]{:S(2)}) copy-start(f32[9,1,128]{0,2,1:T(8,128)S(1)} %copy.612) | copy-start | bytes 13828
  6.9 102.1 %copy-start.10 = (f32[9,1,128]{0,2,1:T(8,128)}, f32[9,1,128]{0,2,1:T(8,128)S(1)}, u32[]{:S(2)}) copy-start(f32[9,1,128]{0,2,1:T(8,128)S(1)} %copy.613) | copy-start | bytes 13828
  7.0 102.0 %copy-start.11 = (f32[9,1,128]{0,2,1:T(8,128)}, f32[9,1,128]{0,2,1:T(8,128)S(1)}, u32[]{:S(2)}) copy-start(f32[9,1,128]{0,2,1:T(8,128)S(1)} %copy.614) | copy-start | bytes 13828
  7.1 101.9 %copy-start.12 = (f32[9,1,128]{0,2,1:T(8,128)}, f32[9,1,128]{0,2,1:T(8,128)S(1)}, u32[]{:S(2)}) copy-start(f32[9,1,128]{0,2,1:T(8,128)S(1)} %copy.615) | copy-start | bytes 13828
  7.2 101.8 %copy-start.13 = (f32[9,1,128]{0,2,1:T(8,128)}, f32[9,1,128]{0,2,1:T(8,128)S(1)}, u32[]{:S(2)}) copy-start(f32[9,1,128]{0,2,1:T(8,128)S(1)} %copy.616) | copy-start | bytes 13828
  7.4 101.7 %copy-start.14 = (f32[9,1,128]{0,2,1:T(8,128)}, f32[9,1,128]{0,2,1:T(8,128)S(1)}, u32[]{:S(2)}) copy-start(f32[9,1,128]{0,2,1:T(8,128)S(1)} %copy.617) | copy-start | bytes 13828
  7.5 101.5 %copy-start.15 = (f32[9,1,128]{0,2,1:T(8,128)}, f32[9,1,128]{0,2,1:T(8,128)S(1)}, u32[]{:S(2)}) copy-start(f32[9,1,128]{0,2,1:T(8,128)S(1)} %copy.618) | copy-start | bytes 13828
  7.6 101.4 %copy-start.16 = (f32[9,1,128]{0,2,1:T(8,128)}, f32[9,1,128]{0,2,1:T(8,128)S(1)}, u32[]{:S(2)}) copy-start(f32[9,1,128]{0,2,1:T(8,128)S(1)} %copy.619) | copy-start | bytes 13828
  8.4 100.6 %copy-start.17 = (f32[9,1,128]{0,2,1:T(8,128)}, f32[9,1,128]{0,2,1:T(8,128)S(1)}, u32[]{:S(2)}) copy-start(f32[9,1,128]{0,2,1:T(8,128)S(1)} %copy.620) | copy-start | bytes 13828
  8.8 100.2 %copy-start.18 = (f32[9,1,128]{0,2,1:T(8,128)}, f32[9,1,128]{0,2,1:T(8,128)S(1)}, u32[]{:S(2)}) copy-start(f32[9,1,128]{0,2,1:T(8,128)S(1)} %copy.621) | copy-start | bytes 13828
  9.0 100.1 %copy-start.19 = (f32[9,1,128]{0,2,1:T(8,128)}, f32[9,1,128]{0,2,1:T(8,128)S(1)}, u32[]{:S(2)}) copy-start(f32[9,1,128]{0,2,1:T(8,128)S(1)} %copy.622) | copy-start | bytes 13828
  9.1 100.0 %copy-start.20 = (f32[9,1,128]{0,2,1:T(8,128)}, f32[9,1,128]{0,2,1:T(8,128)S(1)}, u32[]{:S(2)}) copy-start(f32[9,1,128]{0,2,1:T(8,128)S(1)} %copy.623) | copy-start | bytes 13828
  189.6 163.8 %collective-permute-start = (f32[48384]{0:T(1024)}, f32[48384]{0:T(1024)}, u32[]{:S(2)}, u32[]{:S(2)}) collective-permute-start(f32[48384]{0:T(1024)} %reshape.9370), channel_id=1, source_target_pairs={{0,8},{4,12},{8,16},{12,20},{16,24},{20,28},{24,0},{28,4},{1,9},{5... | collective-permute-start | bytes 580616 | tf_op jit(solution)/shard_map/ppermute | solution.py:16
  205.9 149.1 %collective-permute-start.1 = (f32[48384]{0:T(1024)}, f32[48384]{0:T(1024)}, u32[]{:S(2)}, u32[]{:S(2)}) collective-permute-start(f32[48384]{0:T(1024)} %reshape.9371), channel_id=1, source_target_pairs={{0,4},{4,8},{8,12},{12,16},{16,20},{20,24},{24,28},{28,0},{1,5},{5... | collective-permute-start | bytes 580616 | tf_op jit(solution)/shard_map/ppermute | solution.py:16
  220.6 136.0 %collective-permute-start.2 = (f32[48384]{0:T(1024)}, f32[48384]{0:T(1024)}, u32[]{:S(2)}, u32[]{:S(2)}) collective-permute-start(f32[48384]{0:T(1024)} %reshape.9372), channel_id=1, source_target_pairs={{0,28},{4,0},{8,4},{12,8},{16,12},{20,16},{24,20},{28,24},{1,29},{... | collective-permute-start | bytes 580616 | tf_op jit(solution)/shard_map/ppermute | solution.py:16
  237.1 121.1 %collective-permute-start.3 = (f32[48384]{0:T(1024)}, f32[48384]{0:T(1024)}, u32[]{:S(2)}, u32[]{:S(2)}) collective-permute-start(f32[48384]{0:T(1024)} %reshape.9373), channel_id=1, source_target_pairs={{0,24},{4,28},{8,0},{12,4},{16,8},{20,12},{24,16},{28,20},{1,25},{... | collective-permute-start | bytes 580616 | tf_op jit(solution)/shard_map/ppermute | solution.py:16
  (193 other events, 2162.4 us)
where the time goes:
time: 455 us; the launch traced here: 449 us
  local copies, waits for them, and re-layouts  274 us (60%)
  other arithmetic  118 us (26%)
  matrix products  38.8 us (9%)
  starting transfers between devices  8.03 us (2%)
  blocking collectives  6.26 us (1%)
    mul x152, local copies, waits for them, and re-layouts, apply_small(): matrix[:, column, :][None, :, :] * values[:, column, :][:, None, :]  70.7 us
    unnamed x545, local copies, waits for them, and re-layouts  66.1 us
    dot_general x26, matrix products, apply_modes(): jnp.dot(matrix, values.reshape(mode_in, quant_count * local_count), preci...  38.8 us
    neg x4, other arithmetic, predict(): current = -running  35.9 us
    select_n x1, other arithmetic, local(): jnp.where(cluster_ids[None, None, :] == cluster, integrals[cluster], own_...  27.5 us
    another operation x20, other arithmetic, pack(): jnp.stack([jnp.take(integrals[cluster], rows[cluster], axis=2) for cluste...  21.2 us
    gather x15, local copies, waits for them, and re-layouts, pack(): jnp.take(integrals[cluster], rows[cluster], axis=2)  18 us
    slice x34, local copies, waits for them, and re-layouts, apply_small(): running = matrix[:, 0, :][None, :, :] * values[:, 0, :][:, None, :]  17.7 us
  transfers between devices with their start and end apart: 4, of which 0 were waited for; matrix products, arithmetic and copies ran while one was open for 34% of the time, Pallas kernels for 0%

commit v1 on v0

v1 whole, which is shorter than its diff:
```python
import jax
import jax.numpy as jnp
from jax import lax
from jax.experimental import pallas as pl
from jax.experimental.pallas import tpu as pltpu
from jax.sharding import PartitionSpec as P

NDER = 6
BASE_STEP = 0.25
OFFSETS = (-2, -1, 1, 2)
BLOCKS = 4
LANES = 128
QUARTER = 32
F32 = jnp.float32
BF16 = jnp.bfloat16


def split_rows(values):
    high = values.astype(BF16).astype(F32)
    low = values - high
    blank = jnp.zeros((8, values.shape[1]), F32)
    return jnp.concatenate([high, high, low, blank], axis=0).astype(BF16)


def split_columns(matrix):
    high = matrix.astype(BF16).astype(F32)
    low = matrix - high
    blank = jnp.zeros((matrix.shape[0], 8), F32)
    return jnp.concatenate([high, low, high, blank], axis=1).astype(BF16)


def odd_and_high(shape):
    quarter = lax.broadcasted_iota(jnp.int32, shape, 1) // QUARTER
    return quarter % 2 == 1, quarter >= 2


def turned(odd, high, rows):
    pairs = [jnp.where(odd, rows[(k + 1) % BLOCKS], rows[k]) for k in range(BLOCKS)]
    return [
        jnp.where(high, pairs[(2 - i) % BLOCKS], pairs[(-i) % BLOCKS]) for i in range(BLOCKS)
    ]


def lane_gather(values, index):
    return jnp.take_along_axis(values, index, axis=1)


def groups(count):
    return (count + BLOCKS - 1) // BLOCKS


def taylor_factors(clusters):
    factors = []
    for cluster in range(clusters):
        width = BASE_STEP * 2.0**cluster
        factor = 1.0
        row = []
        for order in range(NDER):
            factor = factor * width / (order + 1)
            row.append(factor)
        factors.append(row)
    return factors


def pairing_blocks(region):
    second = region // 2 % 2
    odd = region % 2
    return [3 * second, 1 + odd, 3 - 3 * second, 2 - odd]


def predict_kernel(
    state_hbm,
    stiff_hbm,
    star_hbm,
    send_hbm,
    sub_hbm,
    cluster_hbm,
    face_hbm,
    orient_hbm,
    region_index_ref,
    sub_index_ref,
    integral_hbm,
    table_hbm,
    region_hbm0,
    region_hbm1,
    region_hbm2,
    region_hbm3,
    within_hbm0,
    within_hbm1,
    within_hbm2,
    stiff_ref,
    star_ref,
    send_ref,
    sub_ref,
    cluster_ref,
    face_ref,
    orient_ref,
    series_ref,
    product_ref,
    integral_ref,
    table_ref,
    region_ref,
    within_ref,
    arrived,
    sent,
):
    region_hbms = (region_hbm0, region_hbm1, region_hbm2, region_hbm3)
    quants, modes, lanes = state_hbm.shape
    clusters = integral_hbm.shape[0]
    dims = stiff_hbm.shape[0]
    copies = [
        pltpu.make_async_copy(source, target, arrived.at[place])
        for place, (source, target) in enumerate(
            [
                (stiff_hbm, stiff_ref),
                (state_hbm, series_ref.at[0]),
                (star_hbm, star_ref),
                (send_hbm, send_ref),
                (sub_hbm, sub_ref),
                (cluster_hbm, cluster_ref),
                (face_hbm, face_ref),
                (orient_hbm, orient_ref),
            ]
        )
    ]
    for copy in copies:
        copy.start()
    copies[0].wait()
    stacked = jnp.concatenate([stiff_ref[d] for d in range(dims)], axis=0)
    lhs = split_columns(-stacked)
    copies[1].wait()
    block = 3
    blocks = [range(first, min(first + block, quants)) for first in range(0, quants, block)]

    def multiply(slot, rows, values):
        product = jnp.dot(
            lhs, split_rows(jnp.concatenate(values, axis=1)), preferred_element_type=F32
        )
        for place, row in enumerate(rows):
            product_ref[slot, row] = product[:, place * lanes : (place + 1) * lanes]

    for rows in blocks:
        multiply(0, rows, [series_ref[0, row] for row in rows])
    for copy in copies[2:]:
        copy.wait()
    for order in range(1, NDER):
        slot = (order - 1) % 2
        for rows in blocks:
            sums = [None for _ in rows]
            for column in range(quants):
                for d in range(dims):
                    value = product_ref[slot, column, pl.ds(d * modes, modes), :]
                    for place, row in enumerate(rows):
                        term = star_ref[row, column, pl.ds(d, 1), :] * value
                        sums[place] = term if sums[place] is None else sums[place] + term
            for place, row in enumerate(rows):
                series_ref[order, row] = sums[place]
            if order < NDER - 1:
                multiply(1 - slot, rows, sums)

    factors = taylor_factors(clusters)
    per_quant = modes // 8
    count = quants * per_quant
    odd, high = odd_and_high((8, lanes))
    lists = pairing_blocks(region_index_ref[0])
    index = []
    for cluster in range(clusters):
        base = jnp.concatenate(
            [send_ref[0, cluster, pl.ds(lists[s], 1), :] for s in range(BLOCKS)], axis=1
        )
        base = jnp.broadcast_to(base, (8, lanes))
        index.append([base] + [pltpu.roll(base, QUARTER * i, 1) for i in range(1, BLOCKS)])
    sub_slots = sub_ref.shape[2]
    blank = jnp.zeros((1, QUARTER - clusters * sub_slots), jnp.int32)
    row = jnp.concatenate([sub_ref[c] for c in range(clusters)] + [blank], axis=1)
    sub_index = jnp.broadcast_to(jnp.concatenate([row] * BLOCKS, axis=1), (8, lanes))
    owner = lax.broadcasted_iota(jnp.int32, (8, lanes), 1) % QUARTER // sub_slots
    chunk = 4
    leaving = []
    here = sub_index_ref[0]
    brought = pairing_blocks(region_index_ref[0])
    cluster_row = cluster_ref[...]
    for face in range(face_ref.shape[0]):
        entry = face_ref[pl.ds(face, 1), :]
        place = entry - lanes
        sub_place = place - BLOCKS * QUARTER
        block = place // QUARTER
        slot = sum(jnp.where(block == brought[p], p, 0) for p in range(BLOCKS))
        source = (sub_place // sub_slots) ^ here
        for i in range(BLOCKS):
            region = ((slot + i) & (BLOCKS - 1)) * QUARTER + (place & (QUARTER - 1))
            within = ((source + i) & (BLOCKS - 1)) * QUARTER + cluster_row * sub_slots
            within = within + (sub_place & (sub_slots - 1))
            table_ref[face, pl.ds(i, 1), :] = region & (lanes - 1)
            table_ref[face, pl.ds(BLOCKS + i, 1), :] = within & (lanes - 1)
        table_ref[face, pl.ds(2 * BLOCKS + 2, 1), :] = entry & (lanes - 1)
        table_ref[face, pl.ds(2 * BLOCKS + 3, 1), :] = cluster_row
        kind = jnp.where(place < 0, -1, jnp.where(sub_place < 0, cluster_row, clusters))
        table_ref[face, pl.ds(2 * BLOCKS, 1), :] = kind
        table_ref[face, pl.ds(2 * BLOCKS + 1, 1), :] = orient_ref[pl.ds(face, 1), :]

    for group in range(groups(count)):
        picked = [[] for _ in range(clusters)]
        shared = []
        for member in range(BLOCKS):
            at = group * BLOCKS + member
            if at >= count:
                for cluster in range(clusters):
                    picked[cluster].append(picked[cluster][-1])
                shared.append(shared[-1])
                continue
            quant, rows = at // per_quant, pl.ds(at % per_quant * 8, 8)
            series = [series_ref[order, quant, rows, :] for order in range(NDER)]
            for cluster in range(clusters):
                total = factors[cluster][0] * series[0]
                for order in range(1, NDER):
                    total = total + factors[cluster][order] * series[order]
                integral_ref[cluster, at] = total
                picked[cluster].append(lane_gather(total, index[cluster][member]))
                other = lane_gather(total, sub_index)
                within = other if cluster == 0 else jnp.where(owner == cluster, other, within)
            shared.append(within)
        for cluster in range(clusters):
            for b, packed in enumerate(turned(odd, high, picked[cluster])):
                region_ref[b, cluster, group] = packed
        for k, packed in enumerate(turned(odd, high, shared)):
            within_ref[(0, 2, 1, 3)[k], group] = packed
        if (group + 1) % chunk == 0:
            part = pl.ds(group + 1 - chunk, chunk)
            leaving += [
                pltpu.make_async_copy(
                    region_ref.at[b, :, part],
                    region_hbms[b].at[:, part],
                    sent.at[len(leaving) + b],
                )
                for b in range(BLOCKS)
            ]
            for copy in leaving[-BLOCKS:]:
                copy.start()
    for source, target in (
        (within_ref.at[pl.ds(2, 2)], within_hbm1),
        (within_ref.at[0], within_hbm0),
        (within_ref.at[pl.ds(1, 1)], within_hbm2),
        (integral_ref, integral_hbm),
        (table_ref, table_hbm),
    ):
        leaving.append(pltpu.make_async_copy(source, target, sent.at[len(leaving)]))
        leaving[-1].start()
    for copy in leaving:
        copy.wait()


def near_kernel(table_ref, integral_ref, partner_ref):
    clusters, quants, modes, lanes = integral_ref.shape

    def one_face(face, _):
        index = jnp.broadcast_to(table_ref[face, pl.ds(2 * BLOCKS + 2, 1), :], (modes, lanes))
        cluster_row = table_ref[face, pl.ds(2 * BLOCKS + 3, 1), :]
        for quant in range(quants):
            total = lane_gather(integral_ref[0, quant], index)
            for cluster in range(1, clusters):
                other = lane_gather(integral_ref[cluster, quant], index)
                total = jnp.where(cluster_row == cluster, other, total)
            partner_ref[face, quant] = total
        return 0

    lax.fori_loop(0, table_ref.shape[0], one_face, 0)


def own_kernel(
    table_ref,
    volume_ref,
    local_ref,
    integral_ref,
    state_ref,
    star_ref,
    plus_ref,
    neighbour_ref,
    result_ref,
    flux_ref,
    lhs_ref,
    product_ref,
):
    quants, modes, lanes = state_ref.shape
    clusters = integral_ref.shape[0]
    dims = volume_ref.shape[0]
    faces, orients = neighbour_ref.shape[:2]
    cluster_row = table_ref[0, pl.ds(2 * BLOCKS + 3, 1), :]

    stacked = jnp.concatenate(
        [volume_ref[d] for d in range(dims)] + [-local_ref[f] for f in range(faces)], axis=0
    )
    lhs_ref[...] = split_columns(stacked)
    for quant in range(quants):
        own = integral_ref[0, quant]
        for cluster in range(1, clusters):
            own = jnp.where(cluster_row == cluster, integral_ref[cluster, quant], own)
        product_ref[quant] = jnp.dot(lhs_ref[...], split_rows(own), preferred_element_type=F32)

    def own_row(row, _):
        total = state_ref[row]
        for column in range(quants):
            for part in range(dims + faces):
                value = product_ref[column, pl.ds(part * modes, modes), :]
                if part < dims:
                    matrix = star_ref[row, column, pl.ds(part, 1), :]
                else:
                    matrix = plus_ref[row, column, pl.ds(part - dims, 1), :]
                total = total + matrix * value
        result_ref[row] = total
        return 0

    lax.fori_loop(0, quants, own_row, 0)

    def one_face(face, _):
        stack = jnp.concatenate([-neighbour_ref[face, o] for o in range(orients)], axis=0)
        flux_ref[face] = split_columns(stack)
        return 0

    lax.fori_loop(0, faces, one_face, 0)


def neighbour_kernel(
    region_refs,
    first_ref,
    beside_ref,
    across_ref,
    table_ref,
    near_ref,
    minus_ref,
    flux_ref,
    own_ref,
    result_ref,
    pool_ref,
    sub_pool_ref,
    partner_ref,
):
    quants, modes, lanes = own_ref.shape
    faces = flux_ref.shape[0]
    clusters = region_refs[0].shape[0]
    orients = flux_ref.shape[1] // modes
    per_quant = modes // 8
    count = quants * per_quant
    odd, high = odd_and_high((8, lanes))

    def spread(face, row):
        return jnp.broadcast_to(table_ref[face, pl.ds(row, 1), :], (8, lanes))

    def unpack(group):
        for cluster in range(clusters):
            pools = turned(odd, high, [region_refs[b][cluster, group] for b in range(BLOCKS)])
            for member, pool in enumerate(pools):
                if group * BLOCKS + member < count:
                    pool_ref[cluster, group * BLOCKS + member] = pool
        within = [first_ref[group], beside_ref[0, group], across_ref[0, group], across_ref[1, group]]
        pools = turned(odd, high, within)
        for member, pool in enumerate(pools):
            if group * BLOCKS + member < count:
                sub_pool_ref[group * BLOCKS + member] = pool

    def gather(face, ats):
        kind = spread(face, 2 * BLOCKS)
        hits = [kind == cluster for cluster in range(clusters + 1)]
        for at in ats:
            rows = pl.ds(at % per_quant * 8, 8)
            region_index = spread(face, at % BLOCKS)
            sub_index = spread(face, BLOCKS + at % BLOCKS)
            total = near_ref[face, at // per_quant, rows, :]
            for cluster in range(clusters):
                other = lane_gather(pool_ref[cluster, at], region_index)
                total = jnp.where(hits[cluster], other, total)
            other = lane_gather(sub_pool_ref[at], sub_index)
            partner_ref[face, at // per_quant, rows, :] = jnp.where(hits[clusters], other, total)

    block = 2
    blocks = [range(first, min(first + block, quants)) for first in range(0, quants, block)]

    def flux(face, rows):
        orient = table_ref[face, pl.ds(2 * BLOCKS + 1, 1), :]
        mixed = [None for _ in rows]
        for column in range(quants):
            value = partner_ref[face, column]
            for place, row in enumerate(rows):
                term = minus_ref[row, column, pl.ds(face, 1), :] * value
                mixed[place] = term if mixed[place] is None else mixed[place] + term
        every = jnp.dot(
            flux_ref[face], split_rows(jnp.concatenate(mixed, axis=1)), preferred_element_type=F32
        )
        for place, row in enumerate(rows):
            part = every[:, place * lanes : (place + 1) * lanes]
            selected = part[0:modes]
            for o in range(1, orients):
                selected = jnp.where(orient == o, part[o * modes : (o + 1) * modes], selected)
            if face == 0:
                result_ref[row] = own_ref[row] + selected
            else:
                result_ref[row] += selected

    for group in range(groups(count)):
        unpack(group)
    gather(0, range(count))
    for face in range(faces):
        step = (count + len(blocks) - 1) // len(blocks)
        for place, rows in enumerate(blocks):
            flux(face, rows)
            if face + 1 < faces:
                gather(face + 1, range(place * step, min((place + 1) * step, count)))


def whole(count):
    return [pl.BlockSpec(memory_space=pltpu.VMEM) for _ in range(count)]


def far(count):
    return [pl.BlockSpec(memory_space=pltpu.HBM) for _ in range(count)]


def paired(value, axis, pairing):
    count = lax.axis_size(axis)
    pairs = []
    for source in range(count):
        offset = OFFSETS[pairing_blocks(source)[pairing]]
        pairs.append((source, (source + offset) % count))
    return lax.ppermute(value, axis, pairs)


def swapped(value, axis, bit):
    return lax.ppermute(value, axis, [(s, s ^ bit) for s in range(lax.axis_size(axis))])


def local(
    modal_state,
    deriv_stiff,
    volume_stiff,
    local_flux,
    neighbour_flux,
    star_matrices,
    plus_flux,
    minus_flux,
    cluster_ids,
    face_neighbours,
    face_orient,
    send_lists,
    sub_lists,
):
    quants, modes, lanes = modal_state.shape
    clusters = send_lists.shape[2]
    faces, orients = neighbour_flux.shape[:2]
    dims = deriv_stiff.shape[0]
    depth = 3 * modes + 8
    count = quants * modes // 8
    fours = groups(count)
    near_params = pltpu.CompilerParams(vmem_limit_bytes=40 * 1024 * 1024)
    params = pltpu.CompilerParams(vmem_limit_bytes=60 * 1024 * 1024)
    shape = jax.ShapeDtypeStruct
    stars, plus, minus = (
        jnp.transpose(matrix, (1, 2, 0, 3)) for matrix in (star_matrices, plus_flux, minus_flux)
    )
    sends = jnp.transpose(send_lists, (0, 2, 1, 3))
    subs = jnp.transpose(sub_lists, (1, 0, 2))

    here = lax.axis_index("sub").astype(jnp.int32).reshape(1)
    region = lax.axis_index("region").astype(jnp.int32).reshape(1)

    integrals, table, *packed = pl.pallas_call(
        predict_kernel,
        out_shape=(
            shape((clusters, count, 8, lanes), F32),
            shape((faces, 2 * BLOCKS + 8, lanes), jnp.int32),
            *[shape((clusters, fours, 8, lanes), F32)] * BLOCKS,
            shape((fours, 8, lanes), F32),
            shape((2, fours, 8, lanes), F32),
            shape((1, fours, 8, lanes), F32),
        ),
        in_specs=far(8) + [pl.BlockSpec(memory_space=pltpu.SMEM)] * 2,
        out_specs=tuple(far(5 + BLOCKS)),
        scratch_shapes=[
            pltpu.VMEM(deriv_stiff.shape, F32),
            pltpu.VMEM(stars.shape, F32),
            pltpu.VMEM(sends.shape, jnp.int32),
            pltpu.VMEM(subs.shape, jnp.int32),
            pltpu.VMEM((1, lanes), jnp.int32),
            pltpu.VMEM(face_neighbours.shape, jnp.int32),
            pltpu.VMEM(face_orient.shape, jnp.int32),
            pltpu.VMEM((NDER, quants, modes, lanes), F32),
            pltpu.VMEM((2, quants, dims * modes, lanes), F32),
            pltpu.VMEM((clusters, count, 8, lanes), F32),
            pltpu.VMEM((faces, 2 * BLOCKS + 8, lanes), jnp.int32),
            pltpu.VMEM((BLOCKS, clusters, fours, 8, lanes), F32),
            pltpu.VMEM((BLOCKS, fours, 8, lanes), F32),
            pltpu.SemaphoreType.DMA((8,)),
            pltpu.SemaphoreType.DMA((fours + 5,)),
        ],
        compiler_params=params,
        name="predict",
    )(
        modal_state,
        deriv_stiff,
        stars,
        sends,
        subs,
        cluster_ids.reshape(1, lanes),
        face_neighbours,
        face_orient,
        region,
        here,
    )

    arrived = [paired(packed[p], "region", p) for p in range(BLOCKS)]
    first, beside, across = packed[BLOCKS:]
    beside = swapped(beside, "sub", 1)
    across = swapped(jnp.concatenate([across, beside[1:]], axis=0), "sub", 2)
    integrals = integrals.reshape(clusters, quants, modes, lanes)
    near_partner = pl.pallas_call(
        near_kernel,
        out_shape=shape((faces, quants, modes, lanes), F32),
        in_specs=whole(2),
        out_specs=whole(1)[0],
        compiler_params=near_params,
        cost_estimate=pl.CostEstimate(
            flops=4_000_000_000, bytes_accessed=8_000_000, transcendentals=0
        ),
        name="near",
    )(table, integrals)

    own, flux = pl.pallas_call(
        own_kernel,
        out_shape=(
            shape((quants, modes, lanes), F32),
            shape((faces, orients * modes, depth), BF16),
        ),
        in_specs=whole(8),
        out_specs=tuple(whole(2)),
        scratch_shapes=[
            pltpu.VMEM(((dims + faces) * modes, depth), BF16),
            pltpu.VMEM((quants, (dims + faces) * modes, lanes), F32),
        ],
        compiler_params=near_params,
        cost_estimate=pl.CostEstimate(
            flops=4_000_000_000, bytes_accessed=8_000_000, transcendentals=0
        ),
        name="own",
    )(
        table,
        volume_stiff,
        local_flux,
        integrals,
        modal_state,
        stars,
        plus,
        neighbour_flux,
    )

    return pl.pallas_call(
        neighbour_kernel,
        out_shape=shape((quants, modes, lanes), F32),
        in_specs=[whole(BLOCKS), *whole(8)],
        out_specs=whole(1)[0],
        scratch_shapes=[
            pltpu.VMEM((clusters, count, 8, lanes), F32),
            pltpu.VMEM((count, 8, lanes), F32),
            pltpu.VMEM((faces, quants, modes, lanes), F32),
        ],
        compiler_params=near_params,
        name="neighbour",
    )(arrived, first, beside, across, table, near_partner, minus, flux, own)


def solution(mesh):
    return jax.shard_map(
        local,
        mesh=mesh,
        in_specs=(
            P(None, None, ("region", "sub")),
            P(),
            P(),
            P(),
            P(),
            P(None, None, None, ("region", "sub")),
            P(None, None, None, ("region", "sub")),
            P(None, None, None, ("region", "sub")),
            P(("region", "sub")),
            P(None, ("region", "sub")),
            P(None, ("region", "sub")),
            P(("region", "sub"), None, None, None),
            P(("region", "sub"), None, None),
        ),
        out_specs=P(None, None, ("region", "sub")),
        check_vma=False,
    )
```

time: 455 us -> 31.2 us (0.07); the launches traced: 449 us -> 31 us
  local copies, waits for them, and re-layouts: 274 us -> 1.94 us
  other arithmetic: 118 us -> 0.01 us
  matrix products: 38.8 us -> 0 us
  Pallas kernels: 0 us -> 15.3 us
  blocking collectives: 6.26 us -> 0 us
    mul x174 -> x0, local copies, waits for them, and re-layouts: 78.7 us -> none  [the longest x152 70.7 us: apply_small(): matrix[:, column, :][None, :, :] * values[:, column, :][:, None, :]]
    unnamed x545 -> x24, local copies, waits for them, and re-layouts: 66.1 us -> 1.94 us
    dot_general x26 -> x0, matrix products: 38.8 us -> none  [apply_modes(): jnp.dot(matrix, values.reshape(mode_in, quant_count * local_count), preci...]
    another operation x20 -> x0, local copies, waits for them, and re-layouts: 37.5 us -> none  [the longest x5 14.1 us: pack(): jnp.stack([jnp.take(integrals[cluster], rows[cluster], axis=2) for cluste...]
    neg x4 -> x0, other arithmetic: 35.9 us -> none  [predict(): current = -running]
    gather x19 -> x0, local copies, waits for them, and re-layouts: 33.1 us -> none  [the longest x15 18 us: pack(): jnp.take(integrals[cluster], rows[cluster], axis=2)]
    select_n x3 -> x0, other arithmetic: 30.2 us -> none  [the longest x1 27.5 us: local(): jnp.where(cluster_ids[None, None, :] == cluster, integrals[cluster], own_...]
    reshape x27 -> x0, local copies, waits for them, and re-layouts: 26.1 us -> none  [the longest x4 9.14 us: pack(): return picked.reshape(-1)]
  transfers between devices with their start and end apart: 4 -> 6, of which waited for: 0 -> 2; matrix products, arithmetic and copies ran while one was open for 34% -> 0% of each run, Pallas kernels for 0% -> 12%
where the time goes in v1:
time: 31.2 us; the launch traced here: 31 us
  Pallas kernels  15.3 us (49%)
  starting transfers between devices  9.73 us (31%)
  waiting for transfers between devices  3.81 us (12%)
  local copies, waits for them, and re-layouts  1.94 us (6%)
    ppermute x4, starting transfers between devices, paired(): return lax.ppermute(value, axis, pairs)  7.65 us
    pallas_call x1, Pallas kernels, local(): pl.pallas_call(predict_kernel, out_shape=(shape((clusters, count, 8, lane...  6.89 us
    pallas_call x1, Pallas kernels, local(): pl.pallas_call(neighbour_kernel, out_shape=shape((quants, modes, lanes),...  4.57 us
    ppermute x4, waiting for transfers between devices, paired(): return lax.ppermute(value, axis, pairs)  3.8 us
    pallas_call x1, Pallas kernels, local(): pl.pallas_call(own_kernel, out_shape=(shape((quants, modes, lanes), F32),...  2.76 us
    ppermute x2, starting transfers between devices, swapped(): lax.ppermute(value, axis, [(s, s ^ bit) for s in range(lax.axis_size(axis...  2.08 us
    unnamed x24, local copies, waits for them, and re-layouts  1.94 us
    pallas_call x1, Pallas kernels, local(): pl.pallas_call(near_kernel, out_shape=shape((faces, quants, modes, lanes)...  1.08 us
  transfers between devices with their start and end apart: 6, of which 2 were waited for; matrix products, arithmetic and copies ran while one was open for 0% of the time, Pallas kernels for 12%

profile of v1, /device:TPU:0, one launch (start us, length us, event | category | flops | bytes accessed | tf_op | source)
XLA Modules:
  0.0 31.0 jit_solution(17525644288181578688)
XLA Ops:
  0.0 6.9 %predict.1 = (f32[3,63,8,128]{3,2,1,0:T(8,128)}, s32[4,16,128]{2,1,0:T(8,128)}, f32[3,16,8,128]{3,2,1,0:T(8,128)}, f32[3,16,8,128]{3,2,1,0:T(8,128)}, f32[3,16,8...) custom-call(f32[9,56,128]{2,1,0:T(8,128)} %state_ref.1, ...), custom_call_target="tpu_custom_call" | custom-call | tf_op jit(solution)/shard_map/predict/pallas_call | solution.py:465
  6.9 0.5 %collective-permute-start.4 = (f32[2,16,8,128]{3,2,1,0:T(8,128)}, f32[2,16,8,128]{3,2,1,0:T(8,128)S(1)}, u32[]{:S(2)}, u32[]{:S(2)}) collective-permute-start(f32[2,16,8,128]{3,2,1,0:T(8,128)} %get-tuple-element.21), channel_id=1, source_target_pairs={{0,1},{1,0},{2,3},{3,2},{4,5},{5,4},{6,7},{7,6},{8,9},{9,8},{10,11... | collective-permute-start | bytes 393224 | tf_op jit(solution)/shard_map/ppermute | solution.py:428
  7.4 4.7 %collective-permute-start = (f32[3,16,8,128]{3,2,1,0:T(8,128)}, f32[3,16,8,128]{3,2,1,0:T(8,128)S(1)}, u32[]{:S(2)}, u32[]{:S(2)}) collective-permute-start(f32[3,16,8,128]{3,2,1,0:T(8,128)} %get-tuple-element.16), channel_id=1, source_target_pairs={{0,24},{4,28},{8,16},{12,20},{16,8},{20,12},{24,0},{28,4},{1,25},{... | collective-permute-start | bytes 589832 | tf_op jit(solution)/shard_map/ppermute | solution.py:424
  12.1 1.2 %collective-permute-start.1 = (f32[3,16,8,128]{3,2,1,0:T(8,128)}, f32[3,16,8,128]{3,2,1,0:T(8,128)S(1)}, u32[]{:S(2)}, u32[]{:S(2)}) collective-permute-start(f32[3,16,8,128]{3,2,1,0:T(8,128)} %get-tuple-element.17), channel_id=1, source_target_pairs={{0,28},{4,8},{8,4},{12,16},{16,12},{20,24},{24,20},{28,0},{1,29},{... | collective-permute-start | bytes 589832 | tf_op jit(solution)/shard_map/ppermute | solution.py:424
  13.3 1.8 %collective-permute-start.2 = (f32[3,16,8,128]{3,2,1,0:T(8,128)}, f32[3,16,8,128]{3,2,1,0:T(8,128)S(1)}, u32[]{:S(2)}, u32[]{:S(2)}) collective-permute-start(f32[3,16,8,128]{3,2,1,0:T(8,128)} %get-tuple-element.18), channel_id=1, source_target_pairs={{0,8},{4,12},{8,0},{12,4},{16,24},{20,28},{24,16},{28,20},{1,9},{5... | collective-permute-start | bytes 589832 | tf_op jit(solution)/shard_map/ppermute | solution.py:424
  15.1 0.0 collective-permute-start.3
  15.1 0.8 %copy-done.4 = s32[4,16,128]{2,1,0:T(8,128)S(1)} copy-done((s32[4,16,128]{2,1,0:T(8,128)S(1)}, s32[4,16,128]{2,1,0:T(8,128)}, u32[]{:S(2)}) %copy-start.4) | copy-done | bytes 32792
  15.8 1.1 %copy-done.7 = f32[3,63,8,128]{3,2,1,0:T(8,128)S(1)} copy-done((f32[3,63,8,128]{3,2,1,0:T(8,128)S(1)}, f32[3,63,8,128]{3,2,1,0:T(8,128)}, u32[]{:S(2)}) %copy-start.7) | copy-done | bytes 774168
  17.0 0.0 copy-start.6
  17.0 0.0 copy-start.8
  17.0 0.0 copy-start.9
  17.0 0.0 copy-start.10
  17.0 1.1 %near.1.near_ref = f32[4,9,56,128]{3,2,1,0:T(8,128)S(1)} custom-call(s32[4,16,128]{2,1,0:T(8,128)S(1)} %copy-done.4, f32[3,9,56,128]{3,2,1,0:T(8,128)S(1)} %bitcast.12), custom_call_target="tpu_custom_call" | custom-call | flops 4000000000 | bytes 8000000 | tf_op jit(solution)/shard_map/near/pallas_call | solution.py:514
  18.1 0.0 collective-permute-done.4.beside_ref
  18.2 1.6 %collective-permute-start.5 = (f32[2,16,8,128]{3,2,1,0:T(8,128)S(1)}, f32[2,16,8,128]{3,2,1,0:T(8,128)S(1)}, u32[]{:S(2)}, u32[]{:S(2)}) collective-permute-start(f32[2,16,8,128]{3,2,1,0:T(8,128)S(1)} %pad_maximum_fusion), channel_id=1, source_target_pairs={{0,2},{1,3},{2,0},{3,1},{4,6},{5,7},{6,4},{7,5},{8,10},{9,11},{10,... | collective-permute-start | bytes 393224 | tf_op jit(solution)/shard_map/ppermute | solution.py:428
  19.7 0.0 copy-done.5
  19.8 0.0 copy-start.1
  19.8 2.8 %own.1 = (f32[9,56,128]{2,1,0:T(8,128)S(1)}, bf16[4,672,176]{2,1,0:T(8,128)(2,1)S(1)}) custom-call(s32[4,16,128]{2,1,0:T(8,128)S(1)} %copy-done.5, f32[3,56,56]{2,1,0:T(8,128)S(1)} %copy-done.10, f32[4,56,56]{2,1,0:T(8,128)S(1)} %copy-done.9, f32[3,9,56,128]{3,2,1,0:T(8,128)S(1)} %bitcast.13, f32[9,56,128]{2,1,0:T(8,128)S(1)} %copy-done, ...), custom_call_target="tpu_custom_call" | custom-call | flops 4000000000 | bytes 8000000 | tf_op jit(solution)/shard_map/own/pallas_call | solution.py:526
  22.6 0.0 collective-permute-done.region_refs_0_
  22.6 0.9 %collective-permute-done.1.region_refs_1_ = f32[3,16,8,128]{3,2,1,0:T(8,128)S(1)} collective-permute-done((f32[3,16,8,128]{3,2,1,0:T(8,128)}, f32[3,16,8,128]{3,2,1,0:T(8,128)S(1)}, u32[]{:S(2)}, u32[]{:S(2)}) %collective-permute-start.1) | collective-permute-done | bytes 196640 | tf_op jit(solution)/shard_map/ppermute | solution.py:424
  23.5 2.9 %collective-permute-done.2.region_refs_2_ = f32[3,16,8,128]{3,2,1,0:T(8,128)S(1)} collective-permute-done((f32[3,16,8,128]{3,2,1,0:T(8,128)}, f32[3,16,8,128]{3,2,1,0:T(8,128)S(1)}, u32[]{:S(2)}, u32[]{:S(2)}) %collective-permute-start.2) | collective-permute-done | bytes 196640 | tf_op jit(solution)/shard_map/ppermute | solution.py:424
  26.4 0.0 collective-permute-done.3.region_refs_3_
  26.4 0.0 collective-permute-done.5.across_ref
  26.4 4.6 %neighbour.1 = f32[9,56,128]{2,1,0:T(8,128)} custom-call(f32[3,16,8,128]{3,2,1,0:T(8,128)S(1)} %collective-permute-done.region_refs_0_, f32[3,16,8,128]{3,2,1,0:T(8,128)S(1)} %collective-permute-done.1.region_refs_1_, f32[3,16,8,128]{3,2,1,0:T(8,128)S(1)} %collective-permute-done.2.region_refs_2_, ...), custom_call_target="tpu_custom_call" | custom-call | tf_op jit(solution)/shard_map/neighbour/pallas_call | solution.py:554
  (18 shorter events, 0.0 us)
Async XLA Ops:
  6.9 11.2 %collective-permute-start.4 = (f32[2,16,8,128]{3,2,1,0:T(8,128)}, f32[2,16,8,128]{3,2,1,0:T(8,128)S(1)}, u32[]{:S(2)}, u32[]{:S(2)}) collective-permute-start(f32[2,16,8,128]{3,2,1,0:T(8,128)} %get-tuple-element.21), channel_id=1, source_target_pairs={{0,1},{1,0},{2,3},{3,2},{4,5},{5,4},{6,7},{7,6},{8,9},{9,8},{10,11... | collective-permute-start | bytes 393224 | tf_op jit(solution)/shard_map/ppermute | solution.py:428
  7.4 15.1 %collective-permute-start = (f32[3,16,8,128]{3,2,1,0:T(8,128)}, f32[3,16,8,128]{3,2,1,0:T(8,128)S(1)}, u32[]{:S(2)}, u32[]{:S(2)}) collective-permute-start(f32[3,16,8,128]{3,2,1,0:T(8,128)} %get-tuple-element.16), channel_id=1, source_target_pairs={{0,24},{4,28},{8,16},{12,20},{16,8},{20,12},{24,0},{28,4},{1,25},{... | collective-permute-start | bytes 589832 | tf_op jit(solution)/shard_map/ppermute | solution.py:424
  12.1 11.4 %collective-permute-start.1 = (f32[3,16,8,128]{3,2,1,0:T(8,128)}, f32[3,16,8,128]{3,2,1,0:T(8,128)S(1)}, u32[]{:S(2)}, u32[]{:S(2)}) collective-permute-start(f32[3,16,8,128]{3,2,1,0:T(8,128)} %get-tuple-element.17), channel_id=1, source_target_pairs={{0,28},{4,8},{8,4},{12,16},{16,12},{20,24},{24,20},{28,0},{1,29},{... | collective-permute-start | bytes 589832 | tf_op jit(solution)/shard_map/ppermute | solution.py:424
  13.3 13.1 %collective-permute-start.2 = (f32[3,16,8,128]{3,2,1,0:T(8,128)}, f32[3,16,8,128]{3,2,1,0:T(8,128)S(1)}, u32[]{:S(2)}, u32[]{:S(2)}) collective-permute-start(f32[3,16,8,128]{3,2,1,0:T(8,128)} %get-tuple-element.18), channel_id=1, source_target_pairs={{0,8},{4,12},{8,0},{12,4},{16,24},{20,28},{24,16},{28,20},{1,9},{5... | collective-permute-start | bytes 589832 | tf_op jit(solution)/shard_map/ppermute | solution.py:424
  15.1 11.3 %collective-permute-start.3 = (f32[3,16,8,128]{3,2,1,0:T(8,128)}, f32[3,16,8,128]{3,2,1,0:T(8,128)S(1)}, u32[]{:S(2)}, u32[]{:S(2)}) collective-permute-start(f32[3,16,8,128]{3,2,1,0:T(8,128)} %get-tuple-element.19), channel_id=1, source_target_pairs={{0,4},{4,0},{8,12},{12,8},{16,20},{20,16},{24,28},{28,24},{1,5},{5... | collective-permute-start | bytes 589832 | tf_op jit(solution)/shard_map/ppermute | solution.py:424
  15.1 0.8 %copy-start.4 = (s32[4,16,128]{2,1,0:T(8,128)S(1)}, s32[4,16,128]{2,1,0:T(8,128)}, u32[]{:S(2)}) copy-start(s32[4,16,128]{2,1,0:T(8,128)} %get-tuple-element.23.table_ref) | copy-start | bytes 98308
  15.8 1.1 %copy-start.7 = (f32[3,63,8,128]{3,2,1,0:T(8,128)S(1)}, f32[3,63,8,128]{3,2,1,0:T(8,128)}, u32[]{:S(2)}) copy-start(f32[3,63,8,128]{3,2,1,0:T(8,128)} %get-tuple-element.24) | copy-start | bytes 2322436
  17.0 1.2 %copy-start.11 = (f32[1,16,8,128]{3,2,1,0:T(8,128)S(1)}, f32[1,16,8,128]{3,2,1,0:T(8,128)}, u32[]{:S(2)}) copy-start(f32[1,16,8,128]{3,2,1,0:T(8,128)} %get-tuple-element.22) | copy-start | bytes 196612
  17.0 2.8 %copy-start = (f32[9,56,128]{2,1,0:T(8,128)S(1)}, f32[9,56,128]{2,1,0:T(8,128)}, u32[]{:S(2)}) copy-start(f32[9,56,128]{2,1,0:T(8,128)} %state_ref.1) | copy-start | bytes 774148
  17.0 2.8 %copy-start.2 = (f32[3,9,9,128]{3,0,2,1:T(4,128)S(1)}, f32[3,9,9,128]{3,0,2,1:T(4,128)}, u32[]{:S(2)}) copy-start(f32[3,9,9,128]{3,0,2,1:T(4,128)} %param.18) | copy-start | bytes 373252
  17.0 2.8 %copy-start.5 = (s32[4,16,128]{2,1,0:T(8,128)S(1)}, s32[4,16,128]{2,1,0:T(8,128)}, u32[]{:S(2)}) copy-start(s32[4,16,128]{2,1,0:T(8,128)} %get-tuple-element.23.table_ref) | copy-start | bytes 98308
  17.0 2.8 %copy-start.6 = (f32[4,12,56,56]{3,2,1,0:T(8,128)S(1)}, f32[4,12,56,56]{3,2,1,0:T(8,128)}, u32[]{:S(2)}) copy-start(f32[4,12,56,56]{3,2,1,0:T(8,128)} %neighbour_ref.1) | copy-start | bytes 1806340
  17.0 2.8 %copy-start.8 = (f32[4,9,9,128]{3,0,2,1:T(4,128)S(1)}, f32[4,9,9,128]{3,0,2,1:T(4,128)}, u32[]{:S(2)}) copy-start(f32[4,9,9,128]{3,0,2,1:T(4,128)} %param.19) | copy-start | bytes 497668
  17.0 2.8 %copy-start.9 = (f32[4,56,56]{2,1,0:T(8,128)S(1)}, f32[4,56,56]{2,1,0:T(8,128)}, u32[]{:S(2)}) copy-start(f32[4,56,56]{2,1,0:T(8,128)} %local_ref.1) | copy-start | bytes 150532
  17.0 2.8 %copy-start.10 = (f32[3,56,56]{2,1,0:T(8,128)S(1)}, f32[3,56,56]{2,1,0:T(8,128)}, u32[]{:S(2)}) copy-start(f32[3,56,56]{2,1,0:T(8,128)} %volume_ref.1) | copy-start | bytes 112900
  18.2 8.2 %collective-permute-start.5 = (f32[2,16,8,128]{3,2,1,0:T(8,128)S(1)}, f32[2,16,8,128]{3,2,1,0:T(8,128)S(1)}, u32[]{:S(2)}, u32[]{:S(2)}) collective-permute-start(f32[2,16,8,128]{3,2,1,0:T(8,128)S(1)} %pad_maximum_fusion), channel_id=1, source_target_pairs={{0,2},{1,3},{2,0},{3,1},{4,6},{5,7},{6,4},{7,5},{8,10},{9,11},{10,... | collective-permute-start | bytes 393224 | tf_op jit(solution)/shard_map/ppermute | solution.py:428
  19.8 6.6 %copy-start.1 = (f32[4,9,9,128]{3,0,2,1:T(4,128)S(1)}, f32[4,9,9,128]{3,0,2,1:T(4,128)}, u32[]{:S(2)}) copy-start(f32[4,9,9,128]{3,0,2,1:T(4,128)} %param.20) | copy-start | bytes 497668
  19.8 6.6 %copy-start.3 = (f32[16,8,128]{2,1,0:T(8,128)S(1)}, f32[16,8,128]{2,1,0:T(8,128)}, u32[]{:S(2)}) copy-start(f32[16,8,128]{2,1,0:T(8,128)} %get-tuple-element.20.first_ref) | copy-start | bytes 196612

commit v2 on v1

--- a/solution.py
+++ b/solution.py
@@ -42,7 +42,20 @@
 
 
 def lane_gather(values, index):
-    return jnp.take_along_axis(values, index, axis=1)
+    numbers = lax.GatherDimensionNumbers(
+        offset_dims=(),
+        collapsed_slice_dims=(1,),
+        start_index_map=(1,),
+        operand_batching_dims=(0,),
+        start_indices_batching_dims=(0,),
+    )
+    return lax.gather(
+        values,
+        index[:, :, None],
+        dimension_numbers=numbers,
+        slice_sizes=(1, 1),
+        mode=lax.GatherScatterMode.PROMISE_IN_BOUNDS,
+    )
 
 
 def groups(count):
@@ -62,10 +75,9 @@
     return factors
 
 
-def pairing_blocks(region):
-    second = region // 2 % 2
-    odd = region % 2
-    return [3 * second, 1 + odd, 3 - 3 * second, 2 - odd]
+def brought_blocks(sub):
+    odd = sub % 2
+    return [0, BLOCKS - 1, 1 + odd, 2 - odd]
 
 
 def predict_kernel(
@@ -77,7 +89,6 @@
     cluster_hbm,
     face_hbm,
     orient_hbm,
-    region_index_ref,
     sub_index_ref,
     integral_hbm,
     table_hbm,
@@ -162,7 +173,7 @@
     per_quant = modes // 8
     count = quants * per_quant
     odd, high = odd_and_high((8, lanes))
-    lists = pairing_blocks(region_index_ref[0])
+    lists = [BLOCKS - 1 - block for block in brought_blocks(sub_index_ref[0])]
     index = []
     for cluster in range(clusters):
         base = jnp.concatenate(
@@ -178,7 +189,7 @@
     chunk = 4
     leaving = []
     here = sub_index_ref[0]
-    brought = pairing_blocks(region_index_ref[0])
+    brought = brought_blocks(sub_index_ref[0])
     cluster_row = cluster_ref[...]
     for face in range(face_ref.shape[0]):
         entry = face_ref[pl.ds(face, 1), :]
@@ -252,16 +263,19 @@
 
 def near_kernel(table_ref, integral_ref, partner_ref):
     clusters, quants, modes, lanes = integral_ref.shape
+    chosen = jnp.broadcast_to(table_ref[0, pl.ds(2 * BLOCKS + 3, 1), :], (8, lanes))
+    masks = [chosen == cluster for cluster in range(clusters)]
 
     def one_face(face, _):
-        index = jnp.broadcast_to(table_ref[face, pl.ds(2 * BLOCKS + 2, 1), :], (modes, lanes))
-        cluster_row = table_ref[face, pl.ds(2 * BLOCKS + 3, 1), :]
+        index = jnp.broadcast_to(table_ref[face, pl.ds(2 * BLOCKS + 2, 1), :], (8, lanes))
         for quant in range(quants):
-            total = lane_gather(integral_ref[0, quant], index)
-            for cluster in range(1, clusters):
-                other = lane_gather(integral_ref[cluster, quant], index)
-                total = jnp.where(cluster_row == cluster, other, total)
-            partner_ref[face, quant] = total
+            for first in range(0, modes, 8):
+                rows = pl.ds(first, 8)
+                total = lane_gather(integral_ref[0, quant, rows, :], index)
+                for cluster in range(1, clusters):
+                    other = lane_gather(integral_ref[cluster, quant, rows, :], index)
+                    total = jnp.where(masks[cluster], other, total)
+                partner_ref[face, quant, rows, :] = total
         return 0
 
     lax.fori_loop(0, table_ref.shape[0], one_face, 0)
@@ -285,17 +299,24 @@
     clusters = integral_ref.shape[0]
     dims = volume_ref.shape[0]
     faces, orients = neighbour_ref.shape[:2]
-    cluster_row = table_ref[0, pl.ds(2 * BLOCKS + 3, 1), :]
+    chosen = jnp.broadcast_to(table_ref[0, pl.ds(2 * BLOCKS + 3, 1), :], (8, lanes))
+    masks = [chosen == cluster for cluster in range(clusters)]
 
     stacked = jnp.concatenate(
         [volume_ref[d] for d in range(dims)] + [-local_ref[f] for f in range(faces)], axis=0
     )
     lhs_ref[...] = split_columns(stacked)
     for quant in range(quants):
-        own = integral_ref[0, quant]
-        for cluster in range(1, clusters):
-            own = jnp.where(cluster_row == cluster, integral_ref[cluster, quant], own)
-        product_ref[quant] = jnp.dot(lhs_ref[...], split_rows(own), preferred_element_type=F32)
+        parts = []
+        for first in range(0, modes, 8):
+            rows = pl.ds(first, 8)
+            own = integral_ref[0, quant, rows, :]
+            for cluster in range(1, clusters):
+                own = jnp.where(masks[cluster], integral_ref[cluster, quant, rows, :], own)
+            parts.append(own)
+        product_ref[quant] = jnp.dot(
+            lhs_ref[...], split_rows(jnp.concatenate(parts, axis=0)), preferred_element_type=F32
+        )
 
     def own_row(row, _):
         total = state_ref[row]
@@ -361,22 +382,23 @@
     def gather(face, ats):
         kind = spread(face, 2 * BLOCKS)
         hits = [kind == cluster for cluster in range(clusters + 1)]
+        region_index = [spread(face, i) for i in range(BLOCKS)]
+        sub_index = [spread(face, BLOCKS + i) for i in range(BLOCKS)]
         for at in ats:
             rows = pl.ds(at % per_quant * 8, 8)
-            region_index = spread(face, at % BLOCKS)
-            sub_index = spread(face, BLOCKS + at % BLOCKS)
             total = near_ref[face, at // per_quant, rows, :]
             for cluster in range(clusters):
-                other = lane_gather(pool_ref[cluster, at], region_index)
+                other = lane_gather(pool_ref[cluster, at], region_index[at % BLOCKS])
                 total = jnp.where(hits[cluster], other, total)
-            other = lane_gather(sub_pool_ref[at], sub_index)
+            other = lane_gather(sub_pool_ref[at], sub_index[at % BLOCKS])
             partner_ref[face, at // per_quant, rows, :] = jnp.where(hits[clusters], other, total)
 
     block = 2
     blocks = [range(first, min(first + block, quants)) for first in range(0, quants, block)]
 
     def flux(face, rows):
-        orient = table_ref[face, pl.ds(2 * BLOCKS + 1, 1), :]
+        orient = spread(face, 2 * BLOCKS + 1)
+        masks = [orient == o for o in range(orients)]
         mixed = [None for _ in rows]
         for column in range(quants):
             value = partner_ref[face, column]
@@ -387,14 +409,18 @@
             flux_ref[face], split_rows(jnp.concatenate(mixed, axis=1)), preferred_element_type=F32
         )
         for place, row in enumerate(rows):
-            part = every[:, place * lanes : (place + 1) * lanes]
-            selected = part[0:modes]
-            for o in range(1, orients):
-                selected = jnp.where(orient == o, part[o * modes : (o + 1) * modes], selected)
-            if face == 0:
-                result_ref[row] = own_ref[row] + selected
-            else:
-                result_ref[row] += selected
+            for first in range(0, modes, 8):
+                columns = slice(place * lanes, (place + 1) * lanes)
+                total = every[first : first + 8, columns]
+                for o in range(1, orients):
+                    at = o * modes + first
+                    total = jnp.where(masks[o], every[at : at + 8, columns], total)
+                where = pl.ds(first, 8)
+                if face == 0:
+                    total = total + own_ref[row, where, :]
+                else:
+                    total = total + result_ref[row, where, :]
+                result_ref[row, where, :] = total
 
     for group in range(groups(count)):
         unpack(group)
@@ -415,13 +441,14 @@
     return [pl.BlockSpec(memory_space=pltpu.HBM) for _ in range(count)]
 
 
-def paired(value, axis, pairing):
-    count = lax.axis_size(axis)
+def exchanged(value, place):
+    regions, subs = lax.axis_size("region"), lax.axis_size("sub")
     pairs = []
-    for source in range(count):
-        offset = OFFSETS[pairing_blocks(source)[pairing]]
-        pairs.append((source, (source + offset) % count))
-    return lax.ppermute(value, axis, pairs)
+    for region in range(regions):
+        for sub in range(subs):
+            target = (region - OFFSETS[brought_blocks(sub)[place]]) % regions
+            pairs.append((region * subs + sub, target * subs + sub))
+    return lax.ppermute(value, ("region", "sub"), pairs)
 
 
 def swapped(value, axis, bit):
@@ -460,7 +487,6 @@
     subs = jnp.transpose(sub_lists, (1, 0, 2))
 
     here = lax.axis_index("sub").astype(jnp.int32).reshape(1)
-    region = lax.axis_index("region").astype(jnp.int32).reshape(1)
 
     integrals, table, *packed = pl.pallas_call(
         predict_kernel,
@@ -472,7 +498,7 @@
             shape((2, fours, 8, lanes), F32),
             shape((1, fours, 8, lanes), F32),
         ),
-        in_specs=far(8) + [pl.BlockSpec(memory_space=pltpu.SMEM)] * 2,
+        in_specs=far(8) + [pl.BlockSpec(memory_space=pltpu.SMEM)],
         out_specs=tuple(far(5 + BLOCKS)),
         scratch_shapes=[
             pltpu.VMEM(deriv_stiff.shape, F32),
@@ -502,11 +528,10 @@
         cluster_ids.reshape(1, lanes),
         face_neighbours,
         face_orient,
-        region,
         here,
     )
 
-    arrived = [paired(packed[p], "region", p) for p in range(BLOCKS)]
+    arrived = [exchanged(packed[p], p) for p in range(BLOCKS)]
     first, beside, across = packed[BLOCKS:]
     beside = swapped(beside, "sub", 1)
     across = swapped(jnp.concatenate([across, beside[1:]], axis=0), "sub", 2)

time: 31.2 us -> 31.9 us (1.022)
  starting transfers between devices: 9.73 us -> 11.7 us
  waiting for transfers between devices: 3.81 us -> 2.7 us
    ppermute x4, starting transfers between devices: 7.65 us -> 9.47 us  [exchanged(): return lax.ppermute(value, ('region', 'sub'), pairs)]
    ppermute x4, waiting for transfers between devices: 3.8 us -> 2.69 us  [exchanged(): return lax.ppermute(value, ('region', 'sub'), pairs)]
  transfers between devices with their start and end apart: 6 -> 6, of which waited for: 2 -> 1; matrix products, arithmetic and copies ran while one was open for 0% -> 0% of each run, Pallas kernels for 12% -> 12%
where the time goes in v2:
time: 31.9 us; the launch traced here: 31.7 us
  Pallas kernels  15.2 us (48%)
  starting transfers between devices  11.7 us (37%)
  waiting for transfers between devices  2.7 us (8%)
  local copies, waits for them, and re-layouts  1.94 us (6%)
    ppermute x4, starting transfers between devices, exchanged(): return lax.ppermute(value, ('region', 'sub'), pairs)  9.47 us
    pallas_call x1, Pallas kernels, local(): pl.pallas_call(predict_kernel, out_shape=(shape((clusters, count, 8, lane...  6.89 us
    pallas_call x1, Pallas kernels, local(): pl.pallas_call(neighbour_kernel, out_shape=shape((quants, modes, lanes),...  4.44 us
    pallas_call x1, Pallas kernels, local(): pl.pallas_call(own_kernel, out_shape=(shape((quants, modes, lanes), F32),...  2.78 us
    ppermute x4, waiting for transfers between devices, exchanged(): return lax.ppermute(value, ('region', 'sub'), pairs)  2.69 us
    ppermute x2, starting transfers between devices, swapped(): lax.ppermute(value, axis, [(s, s ^ bit) for s in range(lax.axis_size(axis...  2.21 us
    unnamed x24, local copies, waits for them, and re-layouts  1.93 us
    pallas_call x1, Pallas kernels, local(): pl.pallas_call(near_kernel, out_shape=shape((faces, quants, modes, lanes)...  1.08 us
  transfers between devices with their start and end apart: 6, of which 1 were waited for; matrix products, arithmetic and copies ran while one was open for 0% of the time, Pallas kernels for 12%

profile of v2, /device:TPU:0, one launch (start us, length us, event | category | flops | bytes accessed | tf_op | source)
XLA Modules:
  0.0 31.7 jit_solution(4070193182233714227)
XLA Ops:
  0.0 6.9 %predict.1 = (f32[3,63,8,128]{3,2,1,0:T(8,128)}, s32[4,16,128]{2,1,0:T(8,128)}, f32[3,16,8,128]{3,2,1,0:T(8,128)}, f32[3,16,8,128]{3,2,1,0:T(8,128)}, f32[3,16,8...) custom-call(f32[9,56,128]{2,1,0:T(8,128)} %state_ref.1, ...), custom_call_target="tpu_custom_call" | custom-call | tf_op jit(solution)/shard_map/predict/pallas_call | solution.py:491
  6.9 0.5 %collective-permute-start.4 = (f32[2,16,8,128]{3,2,1,0:T(8,128)}, f32[2,16,8,128]{3,2,1,0:T(8,128)S(1)}, u32[]{:S(2)}, u32[]{:S(2)}) collective-permute-start(f32[2,16,8,128]{3,2,1,0:T(8,128)} %get-tuple-element.21), channel_id=1, source_target_pairs={{0,1},{1,0},{2,3},{3,2},{4,5},{5,4},{6,7},{7,6},{8,9},{9,8},{10,11... | collective-permute-start | bytes 393224 | tf_op jit(solution)/shard_map/ppermute | solution.py:455
  7.4 2.6 %collective-permute-start = (f32[3,16,8,128]{3,2,1,0:T(8,128)}, f32[3,16,8,128]{3,2,1,0:T(8,128)S(1)}, u32[]{:S(2)}, u32[]{:S(2)}) collective-permute-start(f32[3,16,8,128]{3,2,1,0:T(8,128)} %get-tuple-element.16), channel_id=1, source_target_pairs={{0,8},{1,9},{2,10},{3,11},{4,12},{5,13},{6,14},{7,15},{8,16},{9,17... | collective-permute-start | bytes 589832 | tf_op jit(solution)/shard_map/ppermute | solution.py:451
  10.1 2.1 %collective-permute-start.1 = (f32[3,16,8,128]{3,2,1,0:T(8,128)}, f32[3,16,8,128]{3,2,1,0:T(8,128)S(1)}, u32[]{:S(2)}, u32[]{:S(2)}) collective-permute-start(f32[3,16,8,128]{3,2,1,0:T(8,128)} %get-tuple-element.17), channel_id=1, source_target_pairs={{0,24},{1,25},{2,26},{3,27},{4,28},{5,29},{6,30},{7,31},{8,0},{9,1... | collective-permute-start | bytes 589832 | tf_op jit(solution)/shard_map/ppermute | solution.py:451
  12.2 1.7 %collective-permute-start.2 = (f32[3,16,8,128]{3,2,1,0:T(8,128)}, f32[3,16,8,128]{3,2,1,0:T(8,128)S(1)}, u32[]{:S(2)}, u32[]{:S(2)}) collective-permute-start(f32[3,16,8,128]{3,2,1,0:T(8,128)} %get-tuple-element.18), channel_id=1, source_target_pairs={{0,4},{1,29},{2,6},{3,31},{4,8},{5,1},{6,10},{7,3},{8,12},{9,5},{1... | collective-permute-start | bytes 589832 | tf_op jit(solution)/shard_map/ppermute | solution.py:451
  13.8 3.1 %collective-permute-start.3 = (f32[3,16,8,128]{3,2,1,0:T(8,128)}, f32[3,16,8,128]{3,2,1,0:T(8,128)S(1)}, u32[]{:S(2)}, u32[]{:S(2)}) collective-permute-start(f32[3,16,8,128]{3,2,1,0:T(8,128)} %get-tuple-element.19), channel_id=1, source_target_pairs={{0,28},{1,5},{2,30},{3,7},{4,0},{5,9},{6,2},{7,11},{8,4},{9,13},{1... | collective-permute-start | bytes 589832 | tf_op jit(solution)/shard_map/ppermute | solution.py:451
  16.9 0.8 %copy-done.4 = s32[4,16,128]{2,1,0:T(8,128)S(1)} copy-done((s32[4,16,128]{2,1,0:T(8,128)S(1)}, s32[4,16,128]{2,1,0:T(8,128)}, u32[]{:S(2)}) %copy-start.4) | copy-done | bytes 32792
  17.6 1.1 %copy-done.6 = f32[3,63,8,128]{3,2,1,0:T(8,128)S(1)} copy-done((f32[3,63,8,128]{3,2,1,0:T(8,128)S(1)}, f32[3,63,8,128]{3,2,1,0:T(8,128)}, u32[]{:S(2)}) %copy-start.6) | copy-done | bytes 774168
  18.8 0.0 copy-start.7
  18.8 0.0 copy-start.8
  18.8 0.0 copy-start.9
  18.8 0.0 copy-start.10
  18.8 1.1 %near.1.near_ref = f32[4,9,56,128]{3,2,1,0:T(8,128)S(1)} custom-call(s32[4,16,128]{2,1,0:T(8,128)S(1)} %copy-done.4, f32[3,9,56,128]{3,2,1,0:T(8,128)S(1)} %bitcast.11), custom_call_target="tpu_custom_call" | custom-call | flops 4000000000 | bytes 8000000 | tf_op jit(solution)/shard_map/near/pallas_call | solution.py:539
  19.9 0.0 collective-permute-done.4.beside_ref
  20.0 1.7 %collective-permute-start.5 = (f32[2,16,8,128]{3,2,1,0:T(8,128)S(1)}, f32[2,16,8,128]{3,2,1,0:T(8,128)S(1)}, u32[]{:S(2)}, u32[]{:S(2)}) collective-permute-start(f32[2,16,8,128]{3,2,1,0:T(8,128)S(1)} %pad_maximum_fusion), channel_id=1, source_target_pairs={{0,2},{1,3},{2,0},{3,1},{4,6},{5,7},{6,4},{7,5},{8,10},{9,11},{10,... | collective-permute-start | bytes 393224 | tf_op jit(solution)/shard_map/ppermute | solution.py:455
  21.7 0.0 copy-done.2
  21.7 0.0 copy-start.1
  21.7 2.8 %own.1 = (f32[9,56,128]{2,1,0:T(8,128)S(1)}, bf16[4,672,176]{2,1,0:T(8,128)(2,1)S(1)}) custom-call(s32[4,16,128]{2,1,0:T(8,128)S(1)} %copy-done.4, f32[3,56,56]{2,1,0:T(8,128)S(1)} %copy-done.10, f32[4,56,56]{2,1,0:T(8,128)S(1)} %copy-done.9, f32[3,9,56,128]{3,2,1,0:T(8,128)S(1)} %bitcast.12, f32[9,56,128]{2,1,0:T(8,128)S(1)} %copy-done, ...), custom_call_target="tpu_custom_call" | custom-call | flops 4000000000 | bytes 8000000 | tf_op jit(solution)/shard_map/own/pallas_call | solution.py:551
  24.5 0.0 collective-permute-done.region_refs_0_
  24.5 0.0 collective-permute-done.1.region_refs_1_
  24.5 2.7 %collective-permute-done.2.region_refs_2_ = f32[3,16,8,128]{3,2,1,0:T(8,128)S(1)} collective-permute-done((f32[3,16,8,128]{3,2,1,0:T(8,128)}, f32[3,16,8,128]{3,2,1,0:T(8,128)S(1)}, u32[]{:S(2)}, u32[]{:S(2)}) %collective-permute-start.2) | collective-permute-done | bytes 196640 | tf_op jit(solution)/shard_map/ppermute | solution.py:451
  27.2 0.0 collective-permute-done.3.region_refs_3_
  27.2 0.0 collective-permute-done.5.across_ref
  27.2 4.4 %neighbour.1 = f32[9,56,128]{2,1,0:T(8,128)} custom-call(f32[3,16,8,128]{3,2,1,0:T(8,128)S(1)} %collective-permute-done.region_refs_0_, f32[3,16,8,128]{3,2,1,0:T(8,128)S(1)} %collective-permute-done.1.region_refs_1_, f32[3,16,8,128]{3,2,1,0:T(8,128)S(1)} %collective-permute-done.2.region_refs_2_, ...), custom_call_target="tpu_custom_call" | custom-call | tf_op jit(solution)/shard_map/neighbour/pallas_call | solution.py:579
  (18 shorter events, 0.0 us)
Async XLA Ops:
  6.9 13.0 %collective-permute-start.4 = (f32[2,16,8,128]{3,2,1,0:T(8,128)}, f32[2,16,8,128]{3,2,1,0:T(8,128)S(1)}, u32[]{:S(2)}, u32[]{:S(2)}) collective-permute-start(f32[2,16,8,128]{3,2,1,0:T(8,128)} %get-tuple-element.21), channel_id=1, source_target_pairs={{0,1},{1,0},{2,3},{3,2},{4,5},{5,4},{6,7},{7,6},{8,9},{9,8},{10,11... | collective-permute-start | bytes 393224 | tf_op jit(solution)/shard_map/ppermute | solution.py:455
  7.4 17.1 %collective-permute-start = (f32[3,16,8,128]{3,2,1,0:T(8,128)}, f32[3,16,8,128]{3,2,1,0:T(8,128)S(1)}, u32[]{:S(2)}, u32[]{:S(2)}) collective-permute-start(f32[3,16,8,128]{3,2,1,0:T(8,128)} %get-tuple-element.16), channel_id=1, source_target_pairs={{0,8},{1,9},{2,10},{3,11},{4,12},{5,13},{6,14},{7,15},{8,16},{9,17... | collective-permute-start | bytes 589832 | tf_op jit(solution)/shard_map/ppermute | solution.py:451
  10.1 14.5 %collective-permute-start.1 = (f32[3,16,8,128]{3,2,1,0:T(8,128)}, f32[3,16,8,128]{3,2,1,0:T(8,128)S(1)}, u32[]{:S(2)}, u32[]{:S(2)}) collective-permute-start(f32[3,16,8,128]{3,2,1,0:T(8,128)} %get-tuple-element.17), channel_id=1, source_target_pairs={{0,24},{1,25},{2,26},{3,27},{4,28},{5,29},{6,30},{7,31},{8,0},{9,1... | collective-permute-start | bytes 589832 | tf_op jit(solution)/shard_map/ppermute | solution.py:451
  12.2 15.1 %collective-permute-start.2 = (f32[3,16,8,128]{3,2,1,0:T(8,128)}, f32[3,16,8,128]{3,2,1,0:T(8,128)S(1)}, u32[]{:S(2)}, u32[]{:S(2)}) collective-permute-start(f32[3,16,8,128]{3,2,1,0:T(8,128)} %get-tuple-element.18), channel_id=1, source_target_pairs={{0,4},{1,29},{2,6},{3,31},{4,8},{5,1},{6,10},{7,3},{8,12},{9,5},{1... | collective-permute-start | bytes 589832 | tf_op jit(solution)/shard_map/ppermute | solution.py:451
  13.8 13.4 %collective-permute-start.3 = (f32[3,16,8,128]{3,2,1,0:T(8,128)}, f32[3,16,8,128]{3,2,1,0:T(8,128)S(1)}, u32[]{:S(2)}, u32[]{:S(2)}) collective-permute-start(f32[3,16,8,128]{3,2,1,0:T(8,128)} %get-tuple-element.19), channel_id=1, source_target_pairs={{0,28},{1,5},{2,30},{3,7},{4,0},{5,9},{6,2},{7,11},{8,4},{9,13},{1... | collective-permute-start | bytes 589832 | tf_op jit(solution)/shard_map/ppermute | solution.py:451
  16.9 0.8 %copy-start.4 = (s32[4,16,128]{2,1,0:T(8,128)S(1)}, s32[4,16,128]{2,1,0:T(8,128)}, u32[]{:S(2)}) copy-start(s32[4,16,128]{2,1,0:T(8,128)} %get-tuple-element.23.table_ref) | copy-start | bytes 98308
  17.6 1.1 %copy-start.6 = (f32[3,63,8,128]{3,2,1,0:T(8,128)S(1)}, f32[3,63,8,128]{3,2,1,0:T(8,128)}, u32[]{:S(2)}) copy-start(f32[3,63,8,128]{3,2,1,0:T(8,128)} %get-tuple-element.24) | copy-start | bytes 2322436
  18.8 1.2 %copy-start.11 = (f32[1,16,8,128]{3,2,1,0:T(8,128)S(1)}, f32[1,16,8,128]{3,2,1,0:T(8,128)}, u32[]{:S(2)}) copy-start(f32[1,16,8,128]{3,2,1,0:T(8,128)} %get-tuple-element.22) | copy-start | bytes 196612
  18.8 2.9 %copy-start = (f32[9,56,128]{2,1,0:T(8,128)S(1)}, f32[9,56,128]{2,1,0:T(8,128)}, u32[]{:S(2)}) copy-start(f32[9,56,128]{2,1,0:T(8,128)} %state_ref.1) | copy-start | bytes 774148
  18.8 2.9 %copy-start.2 = (f32[3,9,9,128]{3,0,2,1:T(4,128)S(1)}, f32[3,9,9,128]{3,0,2,1:T(4,128)}, u32[]{:S(2)}) copy-start(f32[3,9,9,128]{3,0,2,1:T(4,128)} %param.18) | copy-start | bytes 373252
  18.8 2.9 %copy-start.5 = (f32[4,12,56,56]{3,2,1,0:T(8,128)S(1)}, f32[4,12,56,56]{3,2,1,0:T(8,128)}, u32[]{:S(2)}) copy-start(f32[4,12,56,56]{3,2,1,0:T(8,128)} %neighbour_ref.1) | copy-start | bytes 1806340
  18.8 2.9 %copy-start.7 = (f32[3,63,8,128]{3,2,1,0:T(8,128)S(1)}, f32[3,63,8,128]{3,2,1,0:T(8,128)}, u32[]{:S(2)}) copy-start(f32[3,63,8,128]{3,2,1,0:T(8,128)} %get-tuple-element.24) | copy-start | bytes 2322436
  18.8 2.9 %copy-start.8 = (f32[4,9,9,128]{3,0,2,1:T(4,128)S(1)}, f32[4,9,9,128]{3,0,2,1:T(4,128)}, u32[]{:S(2)}) copy-start(f32[4,9,9,128]{3,0,2,1:T(4,128)} %param.19) | copy-start | bytes 497668
  18.8 2.9 %copy-start.9 = (f32[4,56,56]{2,1,0:T(8,128)S(1)}, f32[4,56,56]{2,1,0:T(8,128)}, u32[]{:S(2)}) copy-start(f32[4,56,56]{2,1,0:T(8,128)} %local_ref.1) | copy-start | bytes 150532
  18.8 2.9 %copy-start.10 = (f32[3,56,56]{2,1,0:T(8,128)S(1)}, f32[3,56,56]{2,1,0:T(8,128)}, u32[]{:S(2)}) copy-start(f32[3,56,56]{2,1,0:T(8,128)} %volume_ref.1) | copy-start | bytes 112900
  20.0 7.3 %collective-permute-start.5 = (f32[2,16,8,128]{3,2,1,0:T(8,128)S(1)}, f32[2,16,8,128]{3,2,1,0:T(8,128)S(1)}, u32[]{:S(2)}, u32[]{:S(2)}) collective-permute-start(f32[2,16,8,128]{3,2,1,0:T(8,128)S(1)} %pad_maximum_fusion), channel_id=1, source_target_pairs={{0,2},{1,3},{2,0},{3,1},{4,6},{5,7},{6,4},{7,5},{8,10},{9,11},{10,... | collective-permute-start | bytes 393224 | tf_op jit(solution)/shard_map/ppermute | solution.py:455
  21.7 5.5 %copy-start.1 = (f32[4,9,9,128]{3,0,2,1:T(4,128)S(1)}, f32[4,9,9,128]{3,0,2,1:T(4,128)}, u32[]{:S(2)}) copy-start(f32[4,9,9,128]{3,0,2,1:T(4,128)} %param.20) | copy-start | bytes 497668
  21.7 5.5 %copy-start.3 = (f32[16,8,128]{2,1,0:T(8,128)S(1)}, f32[16,8,128]{2,1,0:T(8,128)}, u32[]{:S(2)}) copy-start(f32[16,8,128]{2,1,0:T(8,128)} %get-tuple-element.20.first_ref) | copy-start | bytes 196612

commit v3 on v2

--- a/solution.py
+++ b/solution.py
@@ -75,9 +75,10 @@
     return factors
 
 
-def brought_blocks(sub):
-    odd = sub % 2
-    return [0, BLOCKS - 1, 1 + odd, 2 - odd]
+def pairing_blocks(region):
+    second = region // 2 % 2
+    odd = region % 2
+    return [3 * second, 1 + odd, 3 - 3 * second, 2 - odd]
 
 
 def predict_kernel(
@@ -89,6 +90,7 @@
     cluster_hbm,
     face_hbm,
     orient_hbm,
+    region_index_ref,
     sub_index_ref,
     integral_hbm,
     table_hbm,
@@ -140,7 +142,7 @@
     stacked = jnp.concatenate([stiff_ref[d] for d in range(dims)], axis=0)
     lhs = split_columns(-stacked)
     copies[1].wait()
-    block = 3
+    block = 5
     blocks = [range(first, min(first + block, quants)) for first in range(0, quants, block)]
 
     def multiply(slot, rows, values):
@@ -173,7 +175,7 @@
     per_quant = modes // 8
     count = quants * per_quant
     odd, high = odd_and_high((8, lanes))
-    lists = [BLOCKS - 1 - block for block in brought_blocks(sub_index_ref[0])]
+    lists = pairing_blocks(region_index_ref[0])
     index = []
     for cluster in range(clusters):
         base = jnp.concatenate(
@@ -188,8 +190,13 @@
     owner = lax.broadcasted_iota(jnp.int32, (8, lanes), 1) % QUARTER // sub_slots
     chunk = 4
     leaving = []
+
+    def leave(source, target):
+        leaving.append(pltpu.make_async_copy(source, target, sent.at[len(leaving)]))
+        leaving[-1].start()
+
     here = sub_index_ref[0]
-    brought = brought_blocks(sub_index_ref[0])
+    brought = pairing_blocks(region_index_ref[0])
     cluster_row = cluster_ref[...]
     for face in range(face_ref.shape[0]):
         entry = face_ref[pl.ds(face, 1), :]
@@ -209,6 +216,7 @@
         kind = jnp.where(place < 0, -1, jnp.where(sub_place < 0, cluster_row, clusters))
         table_ref[face, pl.ds(2 * BLOCKS, 1), :] = kind
         table_ref[face, pl.ds(2 * BLOCKS + 1, 1), :] = orient_ref[pl.ds(face, 1), :]
+    leave(table_ref, table_hbm)
 
     for group in range(groups(count)):
         picked = [[] for _ in range(clusters)]
@@ -238,25 +246,14 @@
             within_ref[(0, 2, 1, 3)[k], group] = packed
         if (group + 1) % chunk == 0:
             part = pl.ds(group + 1 - chunk, chunk)
-            leaving += [
-                pltpu.make_async_copy(
-                    region_ref.at[b, :, part],
-                    region_hbms[b].at[:, part],
-                    sent.at[len(leaving) + b],
-                )
-                for b in range(BLOCKS)
-            ]
-            for copy in leaving[-BLOCKS:]:
-                copy.start()
-    for source, target in (
-        (within_ref.at[pl.ds(2, 2)], within_hbm1),
-        (within_ref.at[0], within_hbm0),
-        (within_ref.at[pl.ds(1, 1)], within_hbm2),
-        (integral_ref, integral_hbm),
-        (table_ref, table_hbm),
-    ):
-        leaving.append(pltpu.make_async_copy(source, target, sent.at[len(leaving)]))
-        leaving[-1].start()
+            for b in range(BLOCKS):
+                leave(region_ref.at[b, :, part], region_hbms[b].at[:, part])
+            first = (group + 1 - chunk) * BLOCKS
+            done = pl.ds(first, min(chunk * BLOCKS, count - first))
+            leave(integral_ref.at[:, done], integral_hbm.at[:, done])
+    leave(within_ref.at[pl.ds(2, 2)], within_hbm1)
+    leave(within_ref.at[0], within_hbm0)
+    leave(within_ref.at[pl.ds(1, 1)], within_hbm2)
     for copy in leaving:
         copy.wait()
 
@@ -441,14 +438,13 @@
     return [pl.BlockSpec(memory_space=pltpu.HBM) for _ in range(count)]
 
 
-def exchanged(value, place):
-    regions, subs = lax.axis_size("region"), lax.axis_size("sub")
+def paired(value, axis, pairing):
+    count = lax.axis_size(axis)
     pairs = []
-    for region in range(regions):
-        for sub in range(subs):
-            target = (region - OFFSETS[brought_blocks(sub)[place]]) % regions
-            pairs.append((region * subs + sub, target * subs + sub))
-    return lax.ppermute(value, ("region", "sub"), pairs)
+    for source in range(count):
+        offset = OFFSETS[pairing_blocks(source)[pairing]]
+        pairs.append((source, (source + offset) % count))
+    return lax.ppermute(value, axis, pairs)
 
 
 def swapped(value, axis, bit):
@@ -487,6 +483,7 @@
     subs = jnp.transpose(sub_lists, (1, 0, 2))
 
     here = lax.axis_index("sub").astype(jnp.int32).reshape(1)
+    region = lax.axis_index("region").astype(jnp.int32).reshape(1)
 
     integrals, table, *packed = pl.pallas_call(
         predict_kernel,
@@ -498,7 +495,7 @@
             shape((2, fours, 8, lanes), F32),
             shape((1, fours, 8, lanes), F32),
         ),
-        in_specs=far(8) + [pl.BlockSpec(memory_space=pltpu.SMEM)],
+        in_specs=far(8) + [pl.BlockSpec(memory_space=pltpu.SMEM)] * 2,
         out_specs=tuple(far(5 + BLOCKS)),
         scratch_shapes=[
             pltpu.VMEM(deriv_stiff.shape, F32),
@@ -515,7 +512,7 @@
             pltpu.VMEM((BLOCKS, clusters, fours, 8, lanes), F32),
             pltpu.VMEM((BLOCKS, fours, 8, lanes), F32),
             pltpu.SemaphoreType.DMA((8,)),
-            pltpu.SemaphoreType.DMA((fours + 5,)),
+            pltpu.SemaphoreType.DMA((fours + 8,)),
         ],
         compiler_params=params,
         name="predict",
@@ -528,10 +525,11 @@
         cluster_ids.reshape(1, lanes),
         face_neighbours,
         face_orient,
+        region,
         here,
     )
 
-    arrived = [exchanged(packed[p], p) for p in range(BLOCKS)]
+    arrived = [paired(packed[p], "region", p) for p in range(BLOCKS)]
     first, beside, across = packed[BLOCKS:]
     beside = swapped(beside, "sub", 1)
     across = swapped(jnp.concatenate([across, beside[1:]], axis=0), "sub", 2)

time: 31.9 us -> 31 us (0.972)
  starting transfers between devices: 11.7 us -> 9.73 us
  waiting for transfers between devices: 2.7 us -> 3.81 us
    ppermute x4, starting transfers between devices: 9.47 us -> 7.65 us  [paired(): return lax.ppermute(value, axis, pairs)]
    ppermute x4, waiting for transfers between devices: 2.69 us -> 3.81 us  [paired(): return lax.ppermute(value, axis, pairs)]
  transfers between devices with their start and end apart: 6 -> 6, of which waited for: 1 -> 2; matrix products, arithmetic and copies ran while one was open for 0% -> 0% of each run, Pallas kernels for 12% -> 12%
where the time goes in v3:
time: 31 us; the launch traced here: 30.8 us
  Pallas kernels  15.1 us (49%)
  starting transfers between devices  9.73 us (31%)
  waiting for transfers between devices  3.81 us (12%)
  local copies, waits for them, and re-layouts  1.94 us (6%)
    ppermute x4, starting transfers between devices, paired(): return lax.ppermute(value, axis, pairs)  7.65 us
    pallas_call x1, Pallas kernels, local(): pl.pallas_call(predict_kernel, out_shape=(shape((clusters, count, 8, lane...  6.84 us
    pallas_call x1, Pallas kernels, local(): pl.pallas_call(neighbour_kernel, out_shape=shape((quants, modes, lanes),...  4.45 us
    ppermute x4, waiting for transfers between devices, paired(): return lax.ppermute(value, axis, pairs)  3.81 us
    pallas_call x1, Pallas kernels, local(): pl.pallas_call(own_kernel, out_shape=(shape((quants, modes, lanes), F32),...  2.76 us
    ppermute x2, starting transfers between devices, swapped(): lax.ppermute(value, axis, [(s, s ^ bit) for s in range(lax.axis_size(axis...  2.08 us
    unnamed x24, local copies, waits for them, and re-layouts  1.94 us
    pallas_call x1, Pallas kernels, local(): pl.pallas_call(near_kernel, out_shape=shape((faces, quants, modes, lanes)...  1.08 us
  transfers between devices with their start and end apart: 6, of which 2 were waited for; matrix products, arithmetic and copies ran while one was open for 0% of the time, Pallas kernels for 12%

profile of v3, /device:TPU:0, one launch (start us, length us, event | category | flops | bytes accessed | tf_op | source)
XLA Modules:
  0.0 30.8 jit_solution(1859208450537938748)
XLA Ops:
  0.0 6.8 %predict.1 = (f32[3,63,8,128]{3,2,1,0:T(8,128)}, s32[4,16,128]{2,1,0:T(8,128)}, f32[3,16,8,128]{3,2,1,0:T(8,128)}, f32[3,16,8,128]{3,2,1,0:T(8,128)}, f32[3,16,8...) custom-call(f32[9,56,128]{2,1,0:T(8,128)} %state_ref.1, ...), custom_call_target="tpu_custom_call" | custom-call | tf_op jit(solution)/shard_map/predict/pallas_call | solution.py:488
  6.8 0.5 %collective-permute-start.4 = (f32[2,16,8,128]{3,2,1,0:T(8,128)}, f32[2,16,8,128]{3,2,1,0:T(8,128)S(1)}, u32[]{:S(2)}, u32[]{:S(2)}) collective-permute-start(f32[2,16,8,128]{3,2,1,0:T(8,128)} %get-tuple-element.21), channel_id=1, source_target_pairs={{0,1},{1,0},{2,3},{3,2},{4,5},{5,4},{6,7},{7,6},{8,9},{9,8},{10,11... | collective-permute-start | bytes 393224 | tf_op jit(solution)/shard_map/ppermute | solution.py:451
  7.4 4.7 %collective-permute-start = (f32[3,16,8,128]{3,2,1,0:T(8,128)}, f32[3,16,8,128]{3,2,1,0:T(8,128)S(1)}, u32[]{:S(2)}, u32[]{:S(2)}) collective-permute-start(f32[3,16,8,128]{3,2,1,0:T(8,128)} %get-tuple-element.16), channel_id=1, source_target_pairs={{0,24},{4,28},{8,16},{12,20},{16,8},{20,12},{24,0},{28,4},{1,25},{... | collective-permute-start | bytes 589832 | tf_op jit(solution)/shard_map/ppermute | solution.py:447
  12.0 1.2 %collective-permute-start.1 = (f32[3,16,8,128]{3,2,1,0:T(8,128)}, f32[3,16,8,128]{3,2,1,0:T(8,128)S(1)}, u32[]{:S(2)}, u32[]{:S(2)}) collective-permute-start(f32[3,16,8,128]{3,2,1,0:T(8,128)} %get-tuple-element.17), channel_id=1, source_target_pairs={{0,28},{4,8},{8,4},{12,16},{16,12},{20,24},{24,20},{28,0},{1,29},{... | collective-permute-start | bytes 589832 | tf_op jit(solution)/shard_map/ppermute | solution.py:447
  13.2 1.8 %collective-permute-start.2 = (f32[3,16,8,128]{3,2,1,0:T(8,128)}, f32[3,16,8,128]{3,2,1,0:T(8,128)S(1)}, u32[]{:S(2)}, u32[]{:S(2)}) collective-permute-start(f32[3,16,8,128]{3,2,1,0:T(8,128)} %get-tuple-element.18), channel_id=1, source_target_pairs={{0,8},{4,12},{8,0},{12,4},{16,24},{20,28},{24,16},{28,20},{1,9},{5... | collective-permute-start | bytes 589832 | tf_op jit(solution)/shard_map/ppermute | solution.py:447
  15.0 0.0 collective-permute-start.3
  15.0 0.8 %copy-done.4 = s32[4,16,128]{2,1,0:T(8,128)S(1)} copy-done((s32[4,16,128]{2,1,0:T(8,128)S(1)}, s32[4,16,128]{2,1,0:T(8,128)}, u32[]{:S(2)}) %copy-start.4) | copy-done | bytes 32792
  15.8 1.1 %copy-done.7 = f32[3,63,8,128]{3,2,1,0:T(8,128)S(1)} copy-done((f32[3,63,8,128]{3,2,1,0:T(8,128)S(1)}, f32[3,63,8,128]{3,2,1,0:T(8,128)}, u32[]{:S(2)}) %copy-start.7) | copy-done | bytes 774168
  16.9 0.0 copy-start.6
  16.9 0.0 copy-start.8
  17.0 0.0 copy-start.9
  17.0 0.0 copy-start.10
  17.0 1.1 %near.1.near_ref = f32[4,9,56,128]{3,2,1,0:T(8,128)S(1)} custom-call(s32[4,16,128]{2,1,0:T(8,128)S(1)} %copy-done.4, f32[3,9,56,128]{3,2,1,0:T(8,128)S(1)} %bitcast.12), custom_call_target="tpu_custom_call" | custom-call | flops 4000000000 | bytes 8000000 | tf_op jit(solution)/shard_map/near/pallas_call | solution.py:537
  18.1 0.0 collective-permute-done.4.beside_ref
  18.1 1.6 %collective-permute-start.5 = (f32[2,16,8,128]{3,2,1,0:T(8,128)S(1)}, f32[2,16,8,128]{3,2,1,0:T(8,128)S(1)}, u32[]{:S(2)}, u32[]{:S(2)}) collective-permute-start(f32[2,16,8,128]{3,2,1,0:T(8,128)S(1)} %pad_maximum_fusion), channel_id=1, source_target_pairs={{0,2},{1,3},{2,0},{3,1},{4,6},{5,7},{6,4},{7,5},{8,10},{9,11},{10,... | collective-permute-start | bytes 393224 | tf_op jit(solution)/shard_map/ppermute | solution.py:451
  19.7 0.0 copy-done.5
  19.7 0.0 copy-start.1
  19.7 2.8 %own.1 = (f32[9,56,128]{2,1,0:T(8,128)S(1)}, bf16[4,672,176]{2,1,0:T(8,128)(2,1)S(1)}) custom-call(s32[4,16,128]{2,1,0:T(8,128)S(1)} %copy-done.5, f32[3,56,56]{2,1,0:T(8,128)S(1)} %copy-done.10, f32[4,56,56]{2,1,0:T(8,128)S(1)} %copy-done.9, f32[3,9,56,128]{3,2,1,0:T(8,128)S(1)} %bitcast.13, f32[9,56,128]{2,1,0:T(8,128)S(1)} %copy-done, ...), custom_call_target="tpu_custom_call" | custom-call | flops 4000000000 | bytes 8000000 | tf_op jit(solution)/shard_map/own/pallas_call | solution.py:549
  22.5 0.0 collective-permute-done.region_refs_0_
  22.5 0.9 %collective-permute-done.1.region_refs_1_ = f32[3,16,8,128]{3,2,1,0:T(8,128)S(1)} collective-permute-done((f32[3,16,8,128]{3,2,1,0:T(8,128)}, f32[3,16,8,128]{3,2,1,0:T(8,128)S(1)}, u32[]{:S(2)}, u32[]{:S(2)}) %collective-permute-start.1) | collective-permute-done | bytes 196640 | tf_op jit(solution)/shard_map/ppermute | solution.py:447
  23.5 2.9 %collective-permute-done.2.region_refs_2_ = f32[3,16,8,128]{3,2,1,0:T(8,128)S(1)} collective-permute-done((f32[3,16,8,128]{3,2,1,0:T(8,128)}, f32[3,16,8,128]{3,2,1,0:T(8,128)S(1)}, u32[]{:S(2)}, u32[]{:S(2)}) %collective-permute-start.2) | collective-permute-done | bytes 196640 | tf_op jit(solution)/shard_map/ppermute | solution.py:447
  26.3 0.0 collective-permute-done.3.region_refs_3_
  26.3 0.0 collective-permute-done.5.across_ref
  26.3 4.5 %neighbour.1 = f32[9,56,128]{2,1,0:T(8,128)} custom-call(f32[3,16,8,128]{3,2,1,0:T(8,128)S(1)} %collective-permute-done.region_refs_0_, f32[3,16,8,128]{3,2,1,0:T(8,128)S(1)} %collective-permute-done.1.region_refs_1_, f32[3,16,8,128]{3,2,1,0:T(8,128)S(1)} %collective-permute-done.2.region_refs_2_, ...), custom_call_target="tpu_custom_call" | custom-call | tf_op jit(solution)/shard_map/neighbour/pallas_call | solution.py:577
  (18 shorter events, 0.0 us)
Async XLA Ops:
  6.8 11.2 %collective-permute-start.4 = (f32[2,16,8,128]{3,2,1,0:T(8,128)}, f32[2,16,8,128]{3,2,1,0:T(8,128)S(1)}, u32[]{:S(2)}, u32[]{:S(2)}) collective-permute-start(f32[2,16,8,128]{3,2,1,0:T(8,128)} %get-tuple-element.21), channel_id=1, source_target_pairs={{0,1},{1,0},{2,3},{3,2},{4,5},{5,4},{6,7},{7,6},{8,9},{9,8},{10,11... | collective-permute-start | bytes 393224 | tf_op jit(solution)/shard_map/ppermute | solution.py:451
  7.4 15.1 %collective-permute-start = (f32[3,16,8,128]{3,2,1,0:T(8,128)}, f32[3,16,8,128]{3,2,1,0:T(8,128)S(1)}, u32[]{:S(2)}, u32[]{:S(2)}) collective-permute-start(f32[3,16,8,128]{3,2,1,0:T(8,128)} %get-tuple-element.16), channel_id=1, source_target_pairs={{0,24},{4,28},{8,16},{12,20},{16,8},{20,12},{24,0},{28,4},{1,25},{... | collective-permute-start | bytes 589832 | tf_op jit(solution)/shard_map/ppermute | solution.py:447
  12.0 11.4 %collective-permute-start.1 = (f32[3,16,8,128]{3,2,1,0:T(8,128)}, f32[3,16,8,128]{3,2,1,0:T(8,128)S(1)}, u32[]{:S(2)}, u32[]{:S(2)}) collective-permute-start(f32[3,16,8,128]{3,2,1,0:T(8,128)} %get-tuple-element.17), channel_id=1, source_target_pairs={{0,28},{4,8},{8,4},{12,16},{16,12},{20,24},{24,20},{28,0},{1,29},{... | collective-permute-start | bytes 589832 | tf_op jit(solution)/shard_map/ppermute | solution.py:447
  13.2 13.1 %collective-permute-start.2 = (f32[3,16,8,128]{3,2,1,0:T(8,128)}, f32[3,16,8,128]{3,2,1,0:T(8,128)S(1)}, u32[]{:S(2)}, u32[]{:S(2)}) collective-permute-start(f32[3,16,8,128]{3,2,1,0:T(8,128)} %get-tuple-element.18), channel_id=1, source_target_pairs={{0,8},{4,12},{8,0},{12,4},{16,24},{20,28},{24,16},{28,20},{1,9},{5... | collective-permute-start | bytes 589832 | tf_op jit(solution)/shard_map/ppermute | solution.py:447
  15.0 11.3 %collective-permute-start.3 = (f32[3,16,8,128]{3,2,1,0:T(8,128)}, f32[3,16,8,128]{3,2,1,0:T(8,128)S(1)}, u32[]{:S(2)}, u32[]{:S(2)}) collective-permute-start(f32[3,16,8,128]{3,2,1,0:T(8,128)} %get-tuple-element.19), channel_id=1, source_target_pairs={{0,4},{4,0},{8,12},{12,8},{16,20},{20,16},{24,28},{28,24},{1,5},{5... | collective-permute-start | bytes 589832 | tf_op jit(solution)/shard_map/ppermute | solution.py:447
  15.0 0.8 %copy-start.4 = (s32[4,16,128]{2,1,0:T(8,128)S(1)}, s32[4,16,128]{2,1,0:T(8,128)}, u32[]{:S(2)}) copy-start(s32[4,16,128]{2,1,0:T(8,128)} %get-tuple-element.23.table_ref) | copy-start | bytes 98308
  15.8 1.1 %copy-start.7 = (f32[3,63,8,128]{3,2,1,0:T(8,128)S(1)}, f32[3,63,8,128]{3,2,1,0:T(8,128)}, u32[]{:S(2)}) copy-start(f32[3,63,8,128]{3,2,1,0:T(8,128)} %get-tuple-element.24) | copy-start | bytes 2322436
  16.9 1.2 %copy-start.11 = (f32[1,16,8,128]{3,2,1,0:T(8,128)S(1)}, f32[1,16,8,128]{3,2,1,0:T(8,128)}, u32[]{:S(2)}) copy-start(f32[1,16,8,128]{3,2,1,0:T(8,128)} %get-tuple-element.22) | copy-start | bytes 196612
  16.9 2.8 %copy-start = (f32[9,56,128]{2,1,0:T(8,128)S(1)}, f32[9,56,128]{2,1,0:T(8,128)}, u32[]{:S(2)}) copy-start(f32[9,56,128]{2,1,0:T(8,128)} %state_ref.1) | copy-start | bytes 774148
  16.9 2.8 %copy-start.2 = (f32[3,9,9,128]{3,0,2,1:T(4,128)S(1)}, f32[3,9,9,128]{3,0,2,1:T(4,128)}, u32[]{:S(2)}) copy-start(f32[3,9,9,128]{3,0,2,1:T(4,128)} %param.18) | copy-start | bytes 373252
  16.9 2.8 %copy-start.5 = (s32[4,16,128]{2,1,0:T(8,128)S(1)}, s32[4,16,128]{2,1,0:T(8,128)}, u32[]{:S(2)}) copy-start(s32[4,16,128]{2,1,0:T(8,128)} %get-tuple-element.23.table_ref) | copy-start | bytes 98308
  16.9 2.8 %copy-start.6 = (f32[4,12,56,56]{3,2,1,0:T(8,128)S(1)}, f32[4,12,56,56]{3,2,1,0:T(8,128)}, u32[]{:S(2)}) copy-start(f32[4,12,56,56]{3,2,1,0:T(8,128)} %neighbour_ref.1) | copy-start | bytes 1806340
  16.9 2.7 %copy-start.8 = (f32[4,9,9,128]{3,0,2,1:T(4,128)S(1)}, f32[4,9,9,128]{3,0,2,1:T(4,128)}, u32[]{:S(2)}) copy-start(f32[4,9,9,128]{3,0,2,1:T(4,128)} %param.19) | copy-start | bytes 497668
  17.0 2.7 %copy-start.9 = (f32[4,56,56]{2,1,0:T(8,128)S(1)}, f32[4,56,56]{2,1,0:T(8,128)}, u32[]{:S(2)}) copy-start(f32[4,56,56]{2,1,0:T(8,128)} %local_ref.1) | copy-start | bytes 150532
  17.0 2.7 %copy-start.10 = (f32[3,56,56]{2,1,0:T(8,128)S(1)}, f32[3,56,56]{2,1,0:T(8,128)}, u32[]{:S(2)}) copy-start(f32[3,56,56]{2,1,0:T(8,128)} %volume_ref.1) | copy-start | bytes 112900
  18.1 8.2 %collective-permute-start.5 = (f32[2,16,8,128]{3,2,1,0:T(8,128)S(1)}, f32[2,16,8,128]{3,2,1,0:T(8,128)S(1)}, u32[]{:S(2)}, u32[]{:S(2)}) collective-permute-start(f32[2,16,8,128]{3,2,1,0:T(8,128)S(1)} %pad_maximum_fusion), channel_id=1, source_target_pairs={{0,2},{1,3},{2,0},{3,1},{4,6},{5,7},{6,4},{7,5},{8,10},{9,11},{10,... | collective-permute-start | bytes 393224 | tf_op jit(solution)/shard_map/ppermute | solution.py:451
  19.7 6.6 %copy-start.1 = (f32[4,9,9,128]{3,0,2,1:T(4,128)S(1)}, f32[4,9,9,128]{3,0,2,1:T(4,128)}, u32[]{:S(2)}) copy-start(f32[4,9,9,128]{3,0,2,1:T(4,128)} %param.20) | copy-start | bytes 497668
  19.7 6.6 %copy-start.3 = (f32[16,8,128]{2,1,0:T(8,128)S(1)}, f32[16,8,128]{2,1,0:T(8,128)}, u32[]{:S(2)}) copy-start(f32[16,8,128]{2,1,0:T(8,128)} %get-tuple-element.20.first_ref) | copy-start | bytes 196612

commit v4 on v3

--- a/solution.py
+++ b/solution.py
@@ -109,6 +109,7 @@
     face_ref,
     orient_ref,
     series_ref,
+    spread_ref,
     product_ref,
     integral_ref,
     table_ref,
@@ -142,6 +143,9 @@
     stacked = jnp.concatenate([stiff_ref[d] for d in range(dims)], axis=0)
     lhs = split_columns(-stacked)
     copies[1].wait()
+    factors = taylor_factors(clusters)
+    per_quant = modes // 8
+    count = quants * per_quant
     block = 5
     blocks = [range(first, min(first + block, quants)) for first in range(0, quants, block)]
 
@@ -150,30 +154,41 @@
             lhs, split_rows(jnp.concatenate(values, axis=1)), preferred_element_type=F32
         )
         for place, row in enumerate(rows):
-            product_ref[slot, row] = product[:, place * lanes : (place + 1) * lanes]
+            part = product[:, place * lanes : (place + 1) * lanes]
+            product_ref[slot, row] = part.reshape(dims, per_quant, 8, lanes)
 
     for rows in blocks:
         multiply(0, rows, [series_ref[0, row] for row in rows])
     for copy in copies[2:]:
         copy.wait()
+    for row in range(quants):
+        for column in range(quants):
+            for d in range(dims):
+                spread_ref[row, column, d] = jnp.broadcast_to(
+                    star_ref[row, column, pl.ds(d, 1), :], (8, lanes)
+                )
     for order in range(1, NDER):
         slot = (order - 1) % 2
         for rows in blocks:
             sums = [None for _ in rows]
             for column in range(quants):
                 for d in range(dims):
-                    value = product_ref[slot, column, pl.ds(d * modes, modes), :]
+                    value = product_ref[slot, column, d]
                     for place, row in enumerate(rows):
-                        term = star_ref[row, column, pl.ds(d, 1), :] * value
+                        term = spread_ref[row, column, d][None] * value
                         sums[place] = term if sums[place] is None else sums[place] + term
+            if order < NDER - 1:
+                multiply(1 - slot, rows, [total.reshape(modes, lanes) for total in sums])
             for place, row in enumerate(rows):
-                series_ref[order, row] = sums[place]
-            if order < NDER - 1:
-                multiply(1 - slot, rows, sums)
-
-    factors = taylor_factors(clusters)
-    per_quant = modes // 8
-    count = quants * per_quant
+                for cluster in range(clusters):
+                    term = factors[cluster][order] * sums[place]
+                    if order == 1:
+                        start = series_ref[0, row].reshape(per_quant, 8, lanes)
+                        term = term + factors[cluster][0] * start
+                    else:
+                        term = term + integral_ref[cluster, pl.ds(row * per_quant, per_quant)]
+                    integral_ref[cluster, pl.ds(row * per_quant, per_quant)] = term
+
     odd, high = odd_and_high((8, lanes))
     lists = pairing_blocks(region_index_ref[0])
     index = []
@@ -228,13 +243,8 @@
                     picked[cluster].append(picked[cluster][-1])
                 shared.append(shared[-1])
                 continue
-            quant, rows = at // per_quant, pl.ds(at % per_quant * 8, 8)
-            series = [series_ref[order, quant, rows, :] for order in range(NDER)]
             for cluster in range(clusters):
-                total = factors[cluster][0] * series[0]
-                for order in range(1, NDER):
-                    total = total + factors[cluster][order] * series[order]
-                integral_ref[cluster, at] = total
+                total = integral_ref[cluster, at]
                 picked[cluster].append(lane_gather(total, index[cluster][member]))
                 other = lane_gather(total, sub_index)
                 within = other if cluster == 0 else jnp.where(owner == cluster, other, within)
@@ -286,9 +296,11 @@
     state_ref,
     star_ref,
     plus_ref,
+    minus_ref,
     neighbour_ref,
     result_ref,
     flux_ref,
+    spread_ref,
     lhs_ref,
     product_ref,
 ):
@@ -331,6 +343,11 @@
     lax.fori_loop(0, quants, own_row, 0)
 
     def one_face(face, _):
+        for row in range(quants):
+            for column in range(quants):
+                spread_ref[face, row, column] = jnp.broadcast_to(
+                    minus_ref[row, column, pl.ds(face, 1), :], (8, lanes)
+                )
         stack = jnp.concatenate([-neighbour_ref[face, o] for o in range(orients)], axis=0)
         flux_ref[face] = split_columns(stack)
         return 0
@@ -398,10 +415,11 @@
         masks = [orient == o for o in range(orients)]
         mixed = [None for _ in rows]
         for column in range(quants):
-            value = partner_ref[face, column]
+            value = partner_ref[face, column].reshape(per_quant, 8, lanes)
             for place, row in enumerate(rows):
-                term = minus_ref[row, column, pl.ds(face, 1), :] * value
+                term = minus_ref[face, row, column][None] * value
                 mixed[place] = term if mixed[place] is None else mixed[place] + term
+        mixed = [total.reshape(modes, lanes) for total in mixed]
         every = jnp.dot(
             flux_ref[face], split_rows(jnp.concatenate(mixed, axis=1)), preferred_element_type=F32
         )
@@ -505,8 +523,9 @@
             pltpu.VMEM((1, lanes), jnp.int32),
             pltpu.VMEM(face_neighbours.shape, jnp.int32),
             pltpu.VMEM(face_orient.shape, jnp.int32),
-            pltpu.VMEM((NDER, quants, modes, lanes), F32),
-            pltpu.VMEM((2, quants, dims * modes, lanes), F32),
+            pltpu.VMEM((1, quants, modes, lanes), F32),
+            pltpu.VMEM((quants, quants, dims, 8, lanes), F32),
+            pltpu.VMEM((2, quants, dims, modes // 8, 8, lanes), F32),
             pltpu.VMEM((clusters, count, 8, lanes), F32),
             pltpu.VMEM((faces, 2 * BLOCKS + 8, lanes), jnp.int32),
             pltpu.VMEM((BLOCKS, clusters, fours, 8, lanes), F32),
@@ -546,14 +565,15 @@
         name="near",
     )(table, integrals)
 
-    own, flux = pl.pallas_call(
+    own, flux, minus_spread = pl.pallas_call(
         own_kernel,
         out_shape=(
             shape((quants, modes, lanes), F32),
             shape((faces, orients * modes, depth), BF16),
+            shape((faces, quants, quants, 8, lanes), F32),
         ),
-        in_specs=whole(8),
-        out_specs=tuple(whole(2)),
+        in_specs=whole(9),
+        out_specs=tuple(whole(3)),
         scratch_shapes=[
             pltpu.VMEM(((dims + faces) * modes, depth), BF16),
             pltpu.VMEM((quants, (dims + faces) * modes, lanes), F32),
@@ -571,6 +591,7 @@
         modal_state,
         stars,
         plus,
+        minus,
         neighbour_flux,
     )
 
@@ -586,7 +607,7 @@
         ],
         compiler_params=near_params,
         name="neighbour",
-    )(arrived, first, beside, across, table, near_partner, minus, flux, own)
+    )(arrived, first, beside, across, table, near_partner, minus_spread, flux, own)
 
 
 def solution(mesh):

time: 31 us -> 31.4 us (1.013)
  Pallas kernels: 15.1 us -> 15.6 us
    unnamed x24 -> x26, local copies, waits for them, and re-layouts: 1.94 us -> 1.94 us
  transfers between devices with their start and end apart: 6 -> 6, of which waited for: 2 -> 2; matrix products, arithmetic and copies ran while one was open for 0% -> 0% of each run, Pallas kernels for 12% -> 13%
where the time goes in v4:
time: 31.4 us; the launch traced here: 31.1 us
  Pallas kernels  15.6 us (50%)
  starting transfers between devices  9.73 us (31%)
  waiting for transfers between devices  3.7 us (12%)
  local copies, waits for them, and re-layouts  1.95 us (6%)
    ppermute x4, starting transfers between devices, paired(): return lax.ppermute(value, axis, pairs)  7.66 us
    pallas_call x1, Pallas kernels, local(): pl.pallas_call(predict_kernel, out_shape=(shape((clusters, count, 8, lane...  7.1 us
    pallas_call x1, Pallas kernels, local(): pl.pallas_call(neighbour_kernel, out_shape=shape((quants, modes, lanes),...  4.54 us
    ppermute x4, waiting for transfers between devices, paired(): return lax.ppermute(value, axis, pairs)  3.7 us
    pallas_call x1, Pallas kernels, local(): pl.pallas_call(own_kernel, out_shape=(shape((quants, modes, lanes), F32),...  2.84 us
    ppermute x2, starting transfers between devices, swapped(): lax.ppermute(value, axis, [(s, s ^ bit) for s in range(lax.axis_size(axis...  2.07 us
    unnamed x26, local copies, waits for them, and re-layouts  1.94 us
    pallas_call x1, Pallas kernels, local(): pl.pallas_call(near_kernel, out_shape=shape((faces, quants, modes, lanes)...  1.08 us
  transfers between devices with their start and end apart: 6, of which 2 were waited for; matrix products, arithmetic and copies ran while one was open for 0% of the time, Pallas kernels for 13%

profile of v4, /device:TPU:0, one launch (start us, length us, event | category | flops | bytes accessed | tf_op | source)
XLA Modules:
  0.0 31.1 jit_solution(18082941231068378948)
XLA Ops:
  0.0 7.1 %predict.1 = (f32[3,63,8,128]{3,2,1,0:T(8,128)}, s32[4,16,128]{2,1,0:T(8,128)}, f32[3,16,8,128]{3,2,1,0:T(8,128)}, f32[3,16,8,128]{3,2,1,0:T(8,128)}, f32[3,16,8...) custom-call(f32[9,56,128]{2,1,0:T(8,128)} %state_ref.1, ...), custom_call_target="tpu_custom_call" | custom-call | tf_op jit(solution)/shard_map/predict/pallas_call | solution.py:506
  7.1 0.5 %collective-permute-start.4 = (f32[2,16,8,128]{3,2,1,0:T(8,128)}, f32[2,16,8,128]{3,2,1,0:T(8,128)S(1)}, u32[]{:S(2)}, u32[]{:S(2)}) collective-permute-start(f32[2,16,8,128]{3,2,1,0:T(8,128)} %get-tuple-element.22), channel_id=1, source_target_pairs={{0,1},{1,0},{2,3},{3,2},{4,5},{5,4},{6,7},{7,6},{8,9},{9,8},{10,11... | collective-permute-start | bytes 393224 | tf_op jit(solution)/shard_map/ppermute | solution.py:469
  7.6 4.7 %collective-permute-start = (f32[3,16,8,128]{3,2,1,0:T(8,128)}, f32[3,16,8,128]{3,2,1,0:T(8,128)S(1)}, u32[]{:S(2)}, u32[]{:S(2)}) collective-permute-start(f32[3,16,8,128]{3,2,1,0:T(8,128)} %get-tuple-element.17), channel_id=1, source_target_pairs={{0,24},{4,28},{8,16},{12,20},{16,8},{20,12},{24,0},{28,4},{1,25},{... | collective-permute-start | bytes 589832 | tf_op jit(solution)/shard_map/ppermute | solution.py:465
  12.3 1.2 %collective-permute-start.1 = (f32[3,16,8,128]{3,2,1,0:T(8,128)}, f32[3,16,8,128]{3,2,1,0:T(8,128)S(1)}, u32[]{:S(2)}, u32[]{:S(2)}) collective-permute-start(f32[3,16,8,128]{3,2,1,0:T(8,128)} %get-tuple-element.18), channel_id=1, source_target_pairs={{0,28},{4,8},{8,4},{12,16},{16,12},{20,24},{24,20},{28,0},{1,29},{... | collective-permute-start | bytes 589832 | tf_op jit(solution)/shard_map/ppermute | solution.py:465
  13.5 1.8 %collective-permute-start.2 = (f32[3,16,8,128]{3,2,1,0:T(8,128)}, f32[3,16,8,128]{3,2,1,0:T(8,128)S(1)}, u32[]{:S(2)}, u32[]{:S(2)}) collective-permute-start(f32[3,16,8,128]{3,2,1,0:T(8,128)} %get-tuple-element.19), channel_id=1, source_target_pairs={{0,8},{4,12},{8,0},{12,4},{16,24},{20,28},{24,16},{28,20},{1,9},{5... | collective-permute-start | bytes 589832 | tf_op jit(solution)/shard_map/ppermute | solution.py:465
  15.3 0.0 collective-permute-start.3
  15.3 0.8 %copy-done.3 = s32[4,16,128]{2,1,0:T(8,128)S(1)} copy-done((s32[4,16,128]{2,1,0:T(8,128)S(1)}, s32[4,16,128]{2,1,0:T(8,128)}, u32[]{:S(2)}) %copy-start.3) | copy-done | bytes 32792
  16.1 1.1 %copy-done.6 = f32[3,63,8,128]{3,2,1,0:T(8,128)S(1)} copy-done((f32[3,63,8,128]{3,2,1,0:T(8,128)S(1)}, f32[3,63,8,128]{3,2,1,0:T(8,128)}, u32[]{:S(2)}) %copy-start.6) | copy-done | bytes 774168
  17.2 0.0 copy-start.5
  17.2 0.0 copy-start.8
  17.2 0.0 copy-start.9
  17.2 0.0 copy-start.10
  17.2 0.0 copy-start.11
  17.3 1.1 %near.1.near_ref = f32[4,9,56,128]{3,2,1,0:T(8,128)S(1)} custom-call(s32[4,16,128]{2,1,0:T(8,128)S(1)} %copy-done.3, f32[3,9,56,128]{3,2,1,0:T(8,128)S(1)} %bitcast.11), custom_call_target="tpu_custom_call" | custom-call | flops 4000000000 | bytes 8000000 | tf_op jit(solution)/shard_map/near/pallas_call | solution.py:556
  18.3 0.0 collective-permute-done.4.beside_ref
  18.4 1.6 %collective-permute-start.5 = (f32[2,16,8,128]{3,2,1,0:T(8,128)S(1)}, f32[2,16,8,128]{3,2,1,0:T(8,128)S(1)}, u32[]{:S(2)}, u32[]{:S(2)}) collective-permute-start(f32[2,16,8,128]{3,2,1,0:T(8,128)S(1)} %pad_maximum_fusion), channel_id=1, source_target_pairs={{0,2},{1,3},{2,0},{3,1},{4,6},{5,7},{6,4},{7,5},{8,10},{9,11},{10,... | collective-permute-start | bytes 393224 | tf_op jit(solution)/shard_map/ppermute | solution.py:469
  20.0 0.0 copy-done
  20.0 2.8 %own.1 = (f32[9,56,128]{2,1,0:T(8,128)S(1)}, bf16[4,672,176]{2,1,0:T(8,128)(2,1)S(1)}, f32[4,9,9,8,128]{4,3,2,1,0:T(8,128)S(1)}) custom-call(s32[4,16,128]{2,1,0:T(8,128)S(1)} %copy-done.4, f32[3,56,56]{2,1,0:T(8,128)S(1)} %copy-done.11, f32[4,56,56]{2,1,0:T(8,128)S(1)} %copy-done.10, f32[3,9,56,128]{3,2,1,0:T(8,128)S(1)} %bitcast.12, ...), custom_call_target="tpu_custom_call" | custom-call | flops 4000000000 | bytes 8000000 | tf_op jit(solution)/shard_map/own/pallas_call | solution.py:568
  22.9 0.0 collective-permute-done.region_refs_0_
  22.9 0.8 %collective-permute-done.1.region_refs_1_ = f32[3,16,8,128]{3,2,1,0:T(8,128)S(1)} collective-permute-done((f32[3,16,8,128]{3,2,1,0:T(8,128)}, f32[3,16,8,128]{3,2,1,0:T(8,128)S(1)}, u32[]{:S(2)}, u32[]{:S(2)}) %collective-permute-start.1) | collective-permute-done | bytes 196640 | tf_op jit(solution)/shard_map/ppermute | solution.py:465
  23.7 2.9 %collective-permute-done.2.region_refs_2_ = f32[3,16,8,128]{3,2,1,0:T(8,128)S(1)} collective-permute-done((f32[3,16,8,128]{3,2,1,0:T(8,128)}, f32[3,16,8,128]{3,2,1,0:T(8,128)S(1)}, u32[]{:S(2)}, u32[]{:S(2)}) %collective-permute-start.2) | collective-permute-done | bytes 196640 | tf_op jit(solution)/shard_map/ppermute | solution.py:465
  26.6 0.0 collective-permute-done.3.region_refs_3_
  26.6 0.0 collective-permute-done.5.across_ref
  26.6 4.5 %neighbour.1 = f32[9,56,128]{2,1,0:T(8,128)} custom-call(f32[3,16,8,128]{3,2,1,0:T(8,128)S(1)} %collective-permute-done.region_refs_0_, f32[3,16,8,128]{3,2,1,0:T(8,128)S(1)} %collective-permute-done.1.region_refs_1_, f32[3,16,8,128]{3,2,1,0:T(8,128)S(1)} %collective-permute-done.2.region_refs_2_, ...), custom_call_target="tpu_custom_call" | custom-call | tf_op jit(solution)/shard_map/neighbour/pallas_call | solution.py:598
  (20 shorter events, 0.1 us)
Async XLA Ops:
  7.1 11.2 %collective-permute-start.4 = (f32[2,16,8,128]{3,2,1,0:T(8,128)}, f32[2,16,8,128]{3,2,1,0:T(8,128)S(1)}, u32[]{:S(2)}, u32[]{:S(2)}) collective-permute-start(f32[2,16,8,128]{3,2,1,0:T(8,128)} %get-tuple-element.22), channel_id=1, source_target_pairs={{0,1},{1,0},{2,3},{3,2},{4,5},{5,4},{6,7},{7,6},{8,9},{9,8},{10,11... | collective-permute-start | bytes 393224 | tf_op jit(solution)/shard_map/ppermute | solution.py:469
  7.6 15.3 %collective-permute-start = (f32[3,16,8,128]{3,2,1,0:T(8,128)}, f32[3,16,8,128]{3,2,1,0:T(8,128)S(1)}, u32[]{:S(2)}, u32[]{:S(2)}) collective-permute-start(f32[3,16,8,128]{3,2,1,0:T(8,128)} %get-tuple-element.17), channel_id=1, source_target_pairs={{0,24},{4,28},{8,16},{12,20},{16,8},{20,12},{24,0},{28,4},{1,25},{... | collective-permute-start | bytes 589832 | tf_op jit(solution)/shard_map/ppermute | solution.py:465
  12.3 11.4 %collective-permute-start.1 = (f32[3,16,8,128]{3,2,1,0:T(8,128)}, f32[3,16,8,128]{3,2,1,0:T(8,128)S(1)}, u32[]{:S(2)}, u32[]{:S(2)}) collective-permute-start(f32[3,16,8,128]{3,2,1,0:T(8,128)} %get-tuple-element.18), channel_id=1, source_target_pairs={{0,28},{4,8},{8,4},{12,16},{16,12},{20,24},{24,20},{28,0},{1,29},{... | collective-permute-start | bytes 589832 | tf_op jit(solution)/shard_map/ppermute | solution.py:465
  13.5 13.1 %collective-permute-start.2 = (f32[3,16,8,128]{3,2,1,0:T(8,128)}, f32[3,16,8,128]{3,2,1,0:T(8,128)S(1)}, u32[]{:S(2)}, u32[]{:S(2)}) collective-permute-start(f32[3,16,8,128]{3,2,1,0:T(8,128)} %get-tuple-element.19), channel_id=1, source_target_pairs={{0,8},{4,12},{8,0},{12,4},{16,24},{20,28},{24,16},{28,20},{1,9},{5... | collective-permute-start | bytes 589832 | tf_op jit(solution)/shard_map/ppermute | solution.py:465
  15.3 11.3 %collective-permute-start.3 = (f32[3,16,8,128]{3,2,1,0:T(8,128)}, f32[3,16,8,128]{3,2,1,0:T(8,128)S(1)}, u32[]{:S(2)}, u32[]{:S(2)}) collective-permute-start(f32[3,16,8,128]{3,2,1,0:T(8,128)} %get-tuple-element.20), channel_id=1, source_target_pairs={{0,4},{4,0},{8,12},{12,8},{16,20},{20,16},{24,28},{28,24},{1,5},{5... | collective-permute-start | bytes 589832 | tf_op jit(solution)/shard_map/ppermute | solution.py:465
  15.3 0.8 %copy-start.3 = (s32[4,16,128]{2,1,0:T(8,128)S(1)}, s32[4,16,128]{2,1,0:T(8,128)}, u32[]{:S(2)}) copy-start(s32[4,16,128]{2,1,0:T(8,128)} %get-tuple-element.24.table_ref) | copy-start | bytes 98308
  16.1 1.1 %copy-start.6 = (f32[3,63,8,128]{3,2,1,0:T(8,128)S(1)}, f32[3,63,8,128]{3,2,1,0:T(8,128)}, u32[]{:S(2)}) copy-start(f32[3,63,8,128]{3,2,1,0:T(8,128)} %get-tuple-element.25) | copy-start | bytes 2322436
  17.2 1.2 %copy-start.12 = (f32[1,16,8,128]{3,2,1,0:T(8,128)S(1)}, f32[1,16,8,128]{3,2,1,0:T(8,128)}, u32[]{:S(2)}) copy-start(f32[1,16,8,128]{3,2,1,0:T(8,128)} %get-tuple-element.23) | copy-start | bytes 196612
  17.2 2.8 %copy-start = (f32[9,56,128]{2,1,0:T(8,128)S(1)}, f32[9,56,128]{2,1,0:T(8,128)}, u32[]{:S(2)}) copy-start(f32[9,56,128]{2,1,0:T(8,128)} %state_ref.1) | copy-start | bytes 774148
  17.2 2.8 %copy-start.1 = (f32[3,9,9,128]{3,0,2,1:T(4,128)S(1)}, f32[3,9,9,128]{3,0,2,1:T(4,128)}, u32[]{:S(2)}) copy-start(f32[3,9,9,128]{3,0,2,1:T(4,128)} %param.18) | copy-start | bytes 373252
  17.2 2.8 %copy-start.4 = (s32[4,16,128]{2,1,0:T(8,128)S(1)}, s32[4,16,128]{2,1,0:T(8,128)}, u32[]{:S(2)}) copy-start(s32[4,16,128]{2,1,0:T(8,128)} %get-tuple-element.24.table_ref) | copy-start | bytes 98308
  17.2 2.8 %copy-start.5 = (f32[4,12,56,56]{3,2,1,0:T(8,128)S(1)}, f32[4,12,56,56]{3,2,1,0:T(8,128)}, u32[]{:S(2)}) copy-start(f32[4,12,56,56]{3,2,1,0:T(8,128)} %neighbour_ref.1) | copy-start | bytes 1806340
  17.2 2.8 %copy-start.7 = (f32[3,63,8,128]{3,2,1,0:T(8,128)S(1)}, f32[3,63,8,128]{3,2,1,0:T(8,128)}, u32[]{:S(2)}) copy-start(f32[3,63,8,128]{3,2,1,0:T(8,128)} %get-tuple-element.25) | copy-start | bytes 2322436
  17.2 2.8 %copy-start.8 = (f32[4,9,9,128]{3,0,2,1:T(4,128)S(1)}, f32[4,9,9,128]{3,0,2,1:T(4,128)}, u32[]{:S(2)}) copy-start(f32[4,9,9,128]{3,0,2,1:T(4,128)} %param.19) | copy-start | bytes 497668
  17.2 2.8 %copy-start.9 = (f32[4,9,9,128]{3,0,2,1:T(4,128)S(1)}, f32[4,9,9,128]{3,0,2,1:T(4,128)}, u32[]{:S(2)}) copy-start(f32[4,9,9,128]{3,0,2,1:T(4,128)} %param.20) | copy-start | bytes 497668
  17.2 2.8 %copy-start.10 = (f32[4,56,56]{2,1,0:T(8,128)S(1)}, f32[4,56,56]{2,1,0:T(8,128)}, u32[]{:S(2)}) copy-start(f32[4,56,56]{2,1,0:T(8,128)} %local_ref.1) | copy-start | bytes 150532
  17.2 2.8 %copy-start.11 = (f32[3,56,56]{2,1,0:T(8,128)S(1)}, f32[3,56,56]{2,1,0:T(8,128)}, u32[]{:S(2)}) copy-start(f32[3,56,56]{2,1,0:T(8,128)} %volume_ref.1) | copy-start | bytes 112900
  18.4 8.2 %collective-permute-start.5 = (f32[2,16,8,128]{3,2,1,0:T(8,128)S(1)}, f32[2,16,8,128]{3,2,1,0:T(8,128)S(1)}, u32[]{:S(2)}, u32[]{:S(2)}) collective-permute-start(f32[2,16,8,128]{3,2,1,0:T(8,128)S(1)} %pad_maximum_fusion), channel_id=1, source_target_pairs={{0,2},{1,3},{2,0},{3,1},{4,6},{5,7},{6,4},{7,5},{8,10},{9,11},{10,... | collective-permute-start | bytes 393224 | tf_op jit(solution)/shard_map/ppermute | solution.py:469
  20.0 6.6 %copy-start.2 = (f32[16,8,128]{2,1,0:T(8,128)S(1)}, f32[16,8,128]{2,1,0:T(8,128)}, u32[]{:S(2)}) copy-start(f32[16,8,128]{2,1,0:T(8,128)} %get-tuple-element.21.first_ref) | copy-start | bytes 196612

commit v5 on v3

--- a/solution.py
+++ b/solution.py
@@ -76,9 +76,12 @@
 
 
 def pairing_blocks(region):
+    half = region // 4 % 2
     second = region // 2 % 2
     odd = region % 2
-    return [3 * second, 1 + odd, 3 - 3 * second, 2 - odd]
+    near, beside = 3 - 3 * second, 2 - odd
+    turn = half * (beside - near)
+    return [near + turn, 3 * second, 1 + odd, beside - turn]
 
 
 def predict_kernel(

time: 31 us -> 30.3 us (0.977)
  waiting for transfers between devices: 3.81 us -> 3.33 us
    ppermute x4, waiting for transfers between devices: 3.81 us -> 3.32 us  [paired(): return lax.ppermute(value, axis, pairs)]
  transfers between devices with their start and end apart: 6 -> 6, of which waited for: 2 -> 2; matrix products, arithmetic and copies ran while one was open for 0% -> 0% of each run, Pallas kernels for 12% -> 13%
where the time goes in v5:
time: 30.3 us; the launch traced here: 30.1 us
  Pallas kernels  15.1 us (50%)
  starting transfers between devices  9.52 us (31%)
  waiting for transfers between devices  3.33 us (11%)
  local copies, waits for them, and re-layouts  1.94 us (6%)
    ppermute x4, starting transfers between devices, paired(): return lax.ppermute(value, axis, pairs)  7.42 us
    pallas_call x1, Pallas kernels, local(): pl.pallas_call(predict_kernel, out_shape=(shape((clusters, count, 8, lane...  6.83 us
    pallas_call x1, Pallas kernels, local(): pl.pallas_call(neighbour_kernel, out_shape=shape((quants, modes, lanes),...  4.46 us
    ppermute x4, waiting for transfers between devices, paired(): return lax.ppermute(value, axis, pairs)  3.32 us
    pallas_call x1, Pallas kernels, local(): pl.pallas_call(own_kernel, out_shape=(shape((quants, modes, lanes), F32),...  2.76 us
    ppermute x2, starting transfers between devices, swapped(): lax.ppermute(value, axis, [(s, s ^ bit) for s in range(lax.axis_size(axis...  2.11 us
    unnamed x24, local copies, waits for them, and re-layouts  1.94 us
    pallas_call x1, Pallas kernels, local(): pl.pallas_call(near_kernel, out_shape=shape((faces, quants, modes, lanes)...  1.08 us
  transfers between devices with their start and end apart: 6, of which 2 were waited for; matrix products, arithmetic and copies ran while one was open for 0% of the time, Pallas kernels for 13%

profile of v5, /device:TPU:0, one launch (start us, length us, event | category | flops | bytes accessed | tf_op | source)
XLA Modules:
  0.0 30.1 jit_solution(13267160032592954801)
XLA Ops:
  0.0 6.8 %predict.1 = (f32[3,63,8,128]{3,2,1,0:T(8,128)}, s32[4,16,128]{2,1,0:T(8,128)}, f32[3,16,8,128]{3,2,1,0:T(8,128)}, f32[3,16,8,128]{3,2,1,0:T(8,128)}, f32[3,16,8...) custom-call(f32[9,56,128]{2,1,0:T(8,128)} %state_ref.1, ...), custom_call_target="tpu_custom_call" | custom-call | tf_op jit(solution)/shard_map/predict/pallas_call | solution.py:491
  6.8 0.5 %collective-permute-start.4 = (f32[2,16,8,128]{3,2,1,0:T(8,128)}, f32[2,16,8,128]{3,2,1,0:T(8,128)S(1)}, u32[]{:S(2)}, u32[]{:S(2)}) collective-permute-start(f32[2,16,8,128]{3,2,1,0:T(8,128)} %get-tuple-element.21), channel_id=1, source_target_pairs={{0,1},{1,0},{2,3},{3,2},{4,5},{5,4},{6,7},{7,6},{8,9},{9,8},{10,11... | collective-permute-start | bytes 393224 | tf_op jit(solution)/shard_map/ppermute | solution.py:454
  7.4 2.6 %collective-permute-start = (f32[3,16,8,128]{3,2,1,0:T(8,128)}, f32[3,16,8,128]{3,2,1,0:T(8,128)S(1)}, u32[]{:S(2)}, u32[]{:S(2)}) collective-permute-start(f32[3,16,8,128]{3,2,1,0:T(8,128)} %get-tuple-element.16), channel_id=1, source_target_pairs={{0,8},{4,12},{8,0},{12,4},{16,20},{20,16},{24,28},{28,24},{1,9},{5... | collective-permute-start | bytes 589832 | tf_op jit(solution)/shard_map/ppermute | solution.py:450
  10.0 3.5 %collective-permute-start.1 = (f32[3,16,8,128]{3,2,1,0:T(8,128)}, f32[3,16,8,128]{3,2,1,0:T(8,128)S(1)}, u32[]{:S(2)}, u32[]{:S(2)}) collective-permute-start(f32[3,16,8,128]{3,2,1,0:T(8,128)} %get-tuple-element.17), channel_id=1, source_target_pairs={{0,24},{4,28},{8,16},{12,20},{16,8},{20,12},{24,0},{28,4},{1,25},{... | collective-permute-start | bytes 589832 | tf_op jit(solution)/shard_map/ppermute | solution.py:450
  13.6 1.2 %collective-permute-start.2 = (f32[3,16,8,128]{3,2,1,0:T(8,128)}, f32[3,16,8,128]{3,2,1,0:T(8,128)S(1)}, u32[]{:S(2)}, u32[]{:S(2)}) collective-permute-start(f32[3,16,8,128]{3,2,1,0:T(8,128)} %get-tuple-element.18), channel_id=1, source_target_pairs={{0,28},{4,8},{8,4},{12,16},{16,12},{20,24},{24,20},{28,0},{1,29},{... | collective-permute-start | bytes 589832 | tf_op jit(solution)/shard_map/ppermute | solution.py:450
  14.8 0.0 collective-permute-start.3
  14.8 0.8 %copy-done.4 = s32[4,16,128]{2,1,0:T(8,128)S(1)} copy-done((s32[4,16,128]{2,1,0:T(8,128)S(1)}, s32[4,16,128]{2,1,0:T(8,128)}, u32[]{:S(2)}) %copy-start.4) | copy-done | bytes 32792
  15.5 1.1 %copy-done.7 = f32[3,63,8,128]{3,2,1,0:T(8,128)S(1)} copy-done((f32[3,63,8,128]{3,2,1,0:T(8,128)S(1)}, f32[3,63,8,128]{3,2,1,0:T(8,128)}, u32[]{:S(2)}) %copy-start.7) | copy-done | bytes 774168
  16.7 0.0 copy-start.6
  16.7 0.0 copy-start.8
  16.7 0.0 copy-start.9
  16.7 0.0 copy-start.10
  16.7 1.1 %near.1.near_ref = f32[4,9,56,128]{3,2,1,0:T(8,128)S(1)} custom-call(s32[4,16,128]{2,1,0:T(8,128)S(1)} %copy-done.4, f32[3,9,56,128]{3,2,1,0:T(8,128)S(1)} %bitcast.12), custom_call_target="tpu_custom_call" | custom-call | flops 4000000000 | bytes 8000000 | tf_op jit(solution)/shard_map/near/pallas_call | solution.py:540
  17.8 0.0 collective-permute-done.4.beside_ref
  17.9 1.6 %collective-permute-start.5 = (f32[2,16,8,128]{3,2,1,0:T(8,128)S(1)}, f32[2,16,8,128]{3,2,1,0:T(8,128)S(1)}, u32[]{:S(2)}, u32[]{:S(2)}) collective-permute-start(f32[2,16,8,128]{3,2,1,0:T(8,128)S(1)} %pad_maximum_fusion), channel_id=1, source_target_pairs={{0,2},{1,3},{2,0},{3,1},{4,6},{5,7},{6,4},{7,5},{8,10},{9,11},{10,... | collective-permute-start | bytes 393224 | tf_op jit(solution)/shard_map/ppermute | solution.py:454
  19.4 0.0 copy-done.2
  19.5 0.0 copy-start.1
  19.5 2.8 %own.1 = (f32[9,56,128]{2,1,0:T(8,128)S(1)}, bf16[4,672,176]{2,1,0:T(8,128)(2,1)S(1)}) custom-call(s32[4,16,128]{2,1,0:T(8,128)S(1)} %copy-done.5, f32[3,56,56]{2,1,0:T(8,128)S(1)} %copy-done.10, f32[4,56,56]{2,1,0:T(8,128)S(1)} %copy-done.9, f32[3,9,56,128]{3,2,1,0:T(8,128)S(1)} %bitcast.13, f32[9,56,128]{2,1,0:T(8,128)S(1)} %copy-done, ...), custom_call_target="tpu_custom_call" | custom-call | flops 4000000000 | bytes 8000000 | tf_op jit(solution)/shard_map/own/pallas_call | solution.py:552
  22.3 0.0 collective-permute-done.region_refs_0_
  22.3 0.0 collective-permute-done.1.region_refs_1_
  22.3 2.7 %collective-permute-done.2.region_refs_2_ = f32[3,16,8,128]{3,2,1,0:T(8,128)S(1)} collective-permute-done((f32[3,16,8,128]{3,2,1,0:T(8,128)}, f32[3,16,8,128]{3,2,1,0:T(8,128)S(1)}, u32[]{:S(2)}, u32[]{:S(2)}) %collective-permute-start.2) | collective-permute-done | bytes 196640 | tf_op jit(solution)/shard_map/ppermute | solution.py:450
  25.0 0.6 %collective-permute-done.3.region_refs_3_ = f32[3,16,8,128]{3,2,1,0:T(8,128)S(1)} collective-permute-done((f32[3,16,8,128]{3,2,1,0:T(8,128)}, f32[3,16,8,128]{3,2,1,0:T(8,128)S(1)}, u32[]{:S(2)}, u32[]{:S(2)}) %collective-permute-start.3) | collective-permute-done | bytes 196640 | tf_op jit(solution)/shard_map/ppermute | solution.py:450
  25.6 0.0 collective-permute-done.5.across_ref
  25.6 4.5 %neighbour.1 = f32[9,56,128]{2,1,0:T(8,128)} custom-call(f32[3,16,8,128]{3,2,1,0:T(8,128)S(1)} %collective-permute-done.region_refs_0_, f32[3,16,8,128]{3,2,1,0:T(8,128)S(1)} %collective-permute-done.1.region_refs_1_, f32[3,16,8,128]{3,2,1,0:T(8,128)S(1)} %collective-permute-done.2.region_refs_2_, ...), custom_call_target="tpu_custom_call" | custom-call | tf_op jit(solution)/shard_map/neighbour/pallas_call | solution.py:580
  (18 shorter events, 0.0 us)
Async XLA Ops:
  6.8 11.0 %collective-permute-start.4 = (f32[2,16,8,128]{3,2,1,0:T(8,128)}, f32[2,16,8,128]{3,2,1,0:T(8,128)S(1)}, u32[]{:S(2)}, u32[]{:S(2)}) collective-permute-start(f32[2,16,8,128]{3,2,1,0:T(8,128)} %get-tuple-element.21), channel_id=1, source_target_pairs={{0,1},{1,0},{2,3},{3,2},{4,5},{5,4},{6,7},{7,6},{8,9},{9,8},{10,11... | collective-permute-start | bytes 393224 | tf_op jit(solution)/shard_map/ppermute | solution.py:454
  7.4 14.9 %collective-permute-start = (f32[3,16,8,128]{3,2,1,0:T(8,128)}, f32[3,16,8,128]{3,2,1,0:T(8,128)S(1)}, u32[]{:S(2)}, u32[]{:S(2)}) collective-permute-start(f32[3,16,8,128]{3,2,1,0:T(8,128)} %get-tuple-element.16), channel_id=1, source_target_pairs={{0,8},{4,12},{8,0},{12,4},{16,20},{20,16},{24,28},{28,24},{1,9},{5... | collective-permute-start | bytes 589832 | tf_op jit(solution)/shard_map/ppermute | solution.py:450
  10.0 12.3 %collective-permute-start.1 = (f32[3,16,8,128]{3,2,1,0:T(8,128)}, f32[3,16,8,128]{3,2,1,0:T(8,128)S(1)}, u32[]{:S(2)}, u32[]{:S(2)}) collective-permute-start(f32[3,16,8,128]{3,2,1,0:T(8,128)} %get-tuple-element.17), channel_id=1, source_target_pairs={{0,24},{4,28},{8,16},{12,20},{16,8},{20,12},{24,0},{28,4},{1,25},{... | collective-permute-start | bytes 589832 | tf_op jit(solution)/shard_map/ppermute | solution.py:450
  13.6 11.4 %collective-permute-start.2 = (f32[3,16,8,128]{3,2,1,0:T(8,128)}, f32[3,16,8,128]{3,2,1,0:T(8,128)S(1)}, u32[]{:S(2)}, u32[]{:S(2)}) collective-permute-start(f32[3,16,8,128]{3,2,1,0:T(8,128)} %get-tuple-element.18), channel_id=1, source_target_pairs={{0,28},{4,8},{8,4},{12,16},{16,12},{20,24},{24,20},{28,0},{1,29},{... | collective-permute-start | bytes 589832 | tf_op jit(solution)/shard_map/ppermute | solution.py:450
  14.8 10.8 %collective-permute-start.3 = (f32[3,16,8,128]{3,2,1,0:T(8,128)}, f32[3,16,8,128]{3,2,1,0:T(8,128)S(1)}, u32[]{:S(2)}, u32[]{:S(2)}) collective-permute-start(f32[3,16,8,128]{3,2,1,0:T(8,128)} %get-tuple-element.19), channel_id=1, source_target_pairs={{0,4},{4,0},{8,12},{12,8},{16,24},{20,28},{24,16},{28,20},{1,5},{5... | collective-permute-start | bytes 589832 | tf_op jit(solution)/shard_map/ppermute | solution.py:450
  14.8 0.8 %copy-start.4 = (s32[4,16,128]{2,1,0:T(8,128)S(1)}, s32[4,16,128]{2,1,0:T(8,128)}, u32[]{:S(2)}) copy-start(s32[4,16,128]{2,1,0:T(8,128)} %get-tuple-element.23.table_ref) | copy-start | bytes 98308
  15.5 1.1 %copy-start.7 = (f32[3,63,8,128]{3,2,1,0:T(8,128)S(1)}, f32[3,63,8,128]{3,2,1,0:T(8,128)}, u32[]{:S(2)}) copy-start(f32[3,63,8,128]{3,2,1,0:T(8,128)} %get-tuple-element.24) | copy-start | bytes 2322436
  16.7 1.2 %copy-start.11 = (f32[1,16,8,128]{3,2,1,0:T(8,128)S(1)}, f32[1,16,8,128]{3,2,1,0:T(8,128)}, u32[]{:S(2)}) copy-start(f32[1,16,8,128]{3,2,1,0:T(8,128)} %get-tuple-element.22) | copy-start | bytes 196612
  16.7 2.8 %copy-start = (f32[9,56,128]{2,1,0:T(8,128)S(1)}, f32[9,56,128]{2,1,0:T(8,128)}, u32[]{:S(2)}) copy-start(f32[9,56,128]{2,1,0:T(8,128)} %state_ref.1) | copy-start | bytes 774148
  16.7 2.8 %copy-start.2 = (f32[3,9,9,128]{3,0,2,1:T(4,128)S(1)}, f32[3,9,9,128]{3,0,2,1:T(4,128)}, u32[]{:S(2)}) copy-start(f32[3,9,9,128]{3,0,2,1:T(4,128)} %param.18) | copy-start | bytes 373252
  16.7 2.8 %copy-start.5 = (s32[4,16,128]{2,1,0:T(8,128)S(1)}, s32[4,16,128]{2,1,0:T(8,128)}, u32[]{:S(2)}) copy-start(s32[4,16,128]{2,1,0:T(8,128)} %get-tuple-element.23.table_ref) | copy-start | bytes 98308
  16.7 2.8 %copy-start.6 = (f32[4,12,56,56]{3,2,1,0:T(8,128)S(1)}, f32[4,12,56,56]{3,2,1,0:T(8,128)}, u32[]{:S(2)}) copy-start(f32[4,12,56,56]{3,2,1,0:T(8,128)} %neighbour_ref.1) | copy-start | bytes 1806340
  16.7 2.8 %copy-start.8 = (f32[4,9,9,128]{3,0,2,1:T(4,128)S(1)}, f32[4,9,9,128]{3,0,2,1:T(4,128)}, u32[]{:S(2)}) copy-start(f32[4,9,9,128]{3,0,2,1:T(4,128)} %param.19) | copy-start | bytes 497668
  16.7 2.8 %copy-start.9 = (f32[4,56,56]{2,1,0:T(8,128)S(1)}, f32[4,56,56]{2,1,0:T(8,128)}, u32[]{:S(2)}) copy-start(f32[4,56,56]{2,1,0:T(8,128)} %local_ref.1) | copy-start | bytes 150532
  16.7 2.8 %copy-start.10 = (f32[3,56,56]{2,1,0:T(8,128)S(1)}, f32[3,56,56]{2,1,0:T(8,128)}, u32[]{:S(2)}) copy-start(f32[3,56,56]{2,1,0:T(8,128)} %volume_ref.1) | copy-start | bytes 112900
  17.9 7.8 %collective-permute-start.5 = (f32[2,16,8,128]{3,2,1,0:T(8,128)S(1)}, f32[2,16,8,128]{3,2,1,0:T(8,128)S(1)}, u32[]{:S(2)}, u32[]{:S(2)}) collective-permute-start(f32[2,16,8,128]{3,2,1,0:T(8,128)S(1)} %pad_maximum_fusion), channel_id=1, source_target_pairs={{0,2},{1,3},{2,0},{3,1},{4,6},{5,7},{6,4},{7,5},{8,10},{9,11},{10,... | collective-permute-start | bytes 393224 | tf_op jit(solution)/shard_map/ppermute | solution.py:454
  19.5 6.1 %copy-start.1 = (f32[4,9,9,128]{3,0,2,1:T(4,128)S(1)}, f32[4,9,9,128]{3,0,2,1:T(4,128)}, u32[]{:S(2)}) copy-start(f32[4,9,9,128]{3,0,2,1:T(4,128)} %param.20) | copy-start | bytes 497668
  19.5 6.1 %copy-start.3 = (f32[16,8,128]{2,1,0:T(8,128)S(1)}, f32[16,8,128]{2,1,0:T(8,128)}, u32[]{:S(2)}) copy-start(f32[16,8,128]{2,1,0:T(8,128)} %get-tuple-element.20.first_ref) | copy-start | bytes 196612

commit v6 on v3

--- a/solution.py
+++ b/solution.py
@@ -78,7 +78,7 @@
 def pairing_blocks(region):
     second = region // 2 % 2
     odd = region % 2
-    return [3 * second, 1 + odd, 3 - 3 * second, 2 - odd]
+    return [3 - 3 * second, 3 * second, 1 + odd, 2 - odd]
 
 
 def predict_kernel(

time: 31 us -> 32.1 us (1.035)
  waiting for transfers between devices: 3.81 us -> 5.14 us
    ppermute x4, waiting for transfers between devices: 3.81 us -> 5.13 us  [paired(): return lax.ppermute(value, axis, pairs)]
where the time goes in v6:
time: 32.1 us; the launch traced here: 31.9 us
  Pallas kernels  15.1 us (47%)
  starting transfers between devices  9.51 us (30%)
  waiting for transfers between devices  5.14 us (16%)
  local copies, waits for them, and re-layouts  1.94 us (6%)
    ppermute x4, starting transfers between devices, paired(): return lax.ppermute(value, axis, pairs)  7.43 us
    pallas_call x1, Pallas kernels, local(): pl.pallas_call(predict_kernel, out_shape=(shape((clusters, count, 8, lane...  6.84 us
    ppermute x4, waiting for transfers between devices, paired(): return lax.ppermute(value, axis, pairs)  5.13 us
    pallas_call x1, Pallas kernels, local(): pl.pallas_call(neighbour_kernel, out_shape=shape((quants, modes, lanes),...  4.46 us
    pallas_call x1, Pallas kernels, local(): pl.pallas_call(own_kernel, out_shape=(shape((quants, modes, lanes), F32),...  2.76 us
    ppermute x2, starting transfers between devices, swapped(): lax.ppermute(value, axis, [(s, s ^ bit) for s in range(lax.axis_size(axis...  2.08 us
    unnamed x24, local copies, waits for them, and re-layouts  1.94 us
    pallas_call x1, Pallas kernels, local(): pl.pallas_call(near_kernel, out_shape=shape((faces, quants, modes, lanes)...  1.08 us
  transfers between devices with their start and end apart: 6, of which 2 were waited for; matrix products, arithmetic and copies ran while one was open for 0% of the time, Pallas kernels for 12%

profile of v6, /device:TPU:0, one launch (start us, length us, event | category | flops | bytes accessed | tf_op | source)
XLA Modules:
  0.0 31.9 jit_solution(8019666665656085702)
XLA Ops:
  0.0 6.8 %predict.1 = (f32[3,63,8,128]{3,2,1,0:T(8,128)}, s32[4,16,128]{2,1,0:T(8,128)}, f32[3,16,8,128]{3,2,1,0:T(8,128)}, f32[3,16,8,128]{3,2,1,0:T(8,128)}, f32[3,16,8...) custom-call(f32[9,56,128]{2,1,0:T(8,128)} %state_ref.1, ...), custom_call_target="tpu_custom_call" | custom-call | tf_op jit(solution)/shard_map/predict/pallas_call | solution.py:488
  6.9 0.5 %collective-permute-start.4 = (f32[2,16,8,128]{3,2,1,0:T(8,128)}, f32[2,16,8,128]{3,2,1,0:T(8,128)S(1)}, u32[]{:S(2)}, u32[]{:S(2)}) collective-permute-start(f32[2,16,8,128]{3,2,1,0:T(8,128)} %get-tuple-element.21), channel_id=1, source_target_pairs={{0,1},{1,0},{2,3},{3,2},{4,5},{5,4},{6,7},{7,6},{8,9},{9,8},{10,11... | collective-permute-start | bytes 393224 | tf_op jit(solution)/shard_map/ppermute | solution.py:451
  7.4 2.6 %collective-permute-start = (f32[3,16,8,128]{3,2,1,0:T(8,128)}, f32[3,16,8,128]{3,2,1,0:T(8,128)S(1)}, u32[]{:S(2)}, u32[]{:S(2)}) collective-permute-start(f32[3,16,8,128]{3,2,1,0:T(8,128)} %get-tuple-element.16), channel_id=1, source_target_pairs={{0,8},{4,12},{8,0},{12,4},{16,24},{20,28},{24,16},{28,20},{1,9},{5... | collective-permute-start | bytes 589832 | tf_op jit(solution)/shard_map/ppermute | solution.py:447
  10.0 2.5 %collective-permute-start.1 = (f32[3,16,8,128]{3,2,1,0:T(8,128)}, f32[3,16,8,128]{3,2,1,0:T(8,128)S(1)}, u32[]{:S(2)}, u32[]{:S(2)}) collective-permute-start(f32[3,16,8,128]{3,2,1,0:T(8,128)} %get-tuple-element.17), channel_id=1, source_target_pairs={{0,24},{4,28},{8,16},{12,20},{16,8},{20,12},{24,0},{28,4},{1,25},{... | collective-permute-start | bytes 589832 | tf_op jit(solution)/shard_map/ppermute | solution.py:447
  12.5 2.3 %collective-permute-start.2 = (f32[3,16,8,128]{3,2,1,0:T(8,128)}, f32[3,16,8,128]{3,2,1,0:T(8,128)S(1)}, u32[]{:S(2)}, u32[]{:S(2)}) collective-permute-start(f32[3,16,8,128]{3,2,1,0:T(8,128)} %get-tuple-element.18), channel_id=1, source_target_pairs={{0,28},{4,8},{8,4},{12,16},{16,12},{20,24},{24,20},{28,0},{1,29},{... | collective-permute-start | bytes 589832 | tf_op jit(solution)/shard_map/ppermute | solution.py:447
  14.8 0.0 collective-permute-start.3
  14.8 0.8 %copy-done.4 = s32[4,16,128]{2,1,0:T(8,128)S(1)} copy-done((s32[4,16,128]{2,1,0:T(8,128)S(1)}, s32[4,16,128]{2,1,0:T(8,128)}, u32[]{:S(2)}) %copy-start.4) | copy-done | bytes 32792
  15.6 1.1 %copy-done.7 = f32[3,63,8,128]{3,2,1,0:T(8,128)S(1)} copy-done((f32[3,63,8,128]{3,2,1,0:T(8,128)S(1)}, f32[3,63,8,128]{3,2,1,0:T(8,128)}, u32[]{:S(2)}) %copy-start.7) | copy-done | bytes 774168
  16.7 0.0 copy-start.6
  16.7 0.0 copy-start.8
  16.7 0.0 copy-start.9
  16.7 0.0 copy-start.10
  16.8 1.1 %near.1.near_ref = f32[4,9,56,128]{3,2,1,0:T(8,128)S(1)} custom-call(s32[4,16,128]{2,1,0:T(8,128)S(1)} %copy-done.4, f32[3,9,56,128]{3,2,1,0:T(8,128)S(1)} %bitcast.12), custom_call_target="tpu_custom_call" | custom-call | flops 4000000000 | bytes 8000000 | tf_op jit(solution)/shard_map/near/pallas_call | solution.py:537
  17.8 0.0 collective-permute-done.4.beside_ref
  17.9 1.6 %collective-permute-start.5 = (f32[2,16,8,128]{3,2,1,0:T(8,128)S(1)}, f32[2,16,8,128]{3,2,1,0:T(8,128)S(1)}, u32[]{:S(2)}, u32[]{:S(2)}) collective-permute-start(f32[2,16,8,128]{3,2,1,0:T(8,128)S(1)} %pad_maximum_fusion), channel_id=1, source_target_pairs={{0,2},{1,3},{2,0},{3,1},{4,6},{5,7},{6,4},{7,5},{8,10},{9,11},{10,... | collective-permute-start | bytes 393224 | tf_op jit(solution)/shard_map/ppermute | solution.py:451
  19.5 0.0 copy-start.1
  19.5 2.8 %own.1 = (f32[9,56,128]{2,1,0:T(8,128)S(1)}, bf16[4,672,176]{2,1,0:T(8,128)(2,1)S(1)}) custom-call(s32[4,16,128]{2,1,0:T(8,128)S(1)} %copy-done.5, f32[3,56,56]{2,1,0:T(8,128)S(1)} %copy-done.10, f32[4,56,56]{2,1,0:T(8,128)S(1)} %copy-done.9, f32[3,9,56,128]{3,2,1,0:T(8,128)S(1)} %bitcast.13, f32[9,56,128]{2,1,0:T(8,128)S(1)} %copy-done, ...), custom_call_target="tpu_custom_call" | custom-call | flops 4000000000 | bytes 8000000 | tf_op jit(solution)/shard_map/own/pallas_call | solution.py:549
  22.3 0.0 collective-permute-done.region_refs_0_
  22.3 0.3 %collective-permute-done.1.region_refs_1_ = f32[3,16,8,128]{3,2,1,0:T(8,128)S(1)} collective-permute-done((f32[3,16,8,128]{3,2,1,0:T(8,128)}, f32[3,16,8,128]{3,2,1,0:T(8,128)S(1)}, u32[]{:S(2)}, u32[]{:S(2)}) %collective-permute-start.1) | collective-permute-done | bytes 196640 | tf_op jit(solution)/shard_map/ppermute | solution.py:447
  22.6 4.8 %collective-permute-done.2.region_refs_2_ = f32[3,16,8,128]{3,2,1,0:T(8,128)S(1)} collective-permute-done((f32[3,16,8,128]{3,2,1,0:T(8,128)}, f32[3,16,8,128]{3,2,1,0:T(8,128)S(1)}, u32[]{:S(2)}, u32[]{:S(2)}) %collective-permute-start.2) | collective-permute-done | bytes 196640 | tf_op jit(solution)/shard_map/ppermute | solution.py:447
  27.4 0.0 collective-permute-done.3.region_refs_3_
  27.4 0.0 collective-permute-done.5.across_ref
  27.4 0.0 copy-done.1
  27.4 4.5 %neighbour.1 = f32[9,56,128]{2,1,0:T(8,128)} custom-call(f32[3,16,8,128]{3,2,1,0:T(8,128)S(1)} %collective-permute-done.region_refs_0_, f32[3,16,8,128]{3,2,1,0:T(8,128)S(1)} %collective-permute-done.1.region_refs_1_, f32[3,16,8,128]{3,2,1,0:T(8,128)S(1)} %collective-permute-done.2.region_refs_2_, ...), custom_call_target="tpu_custom_call" | custom-call | tf_op jit(solution)/shard_map/neighbour/pallas_call | solution.py:577
  (18 shorter events, 0.0 us)
Async XLA Ops:
  6.9 11.0 %collective-permute-start.4 = (f32[2,16,8,128]{3,2,1,0:T(8,128)}, f32[2,16,8,128]{3,2,1,0:T(8,128)S(1)}, u32[]{:S(2)}, u32[]{:S(2)}) collective-permute-start(f32[2,16,8,128]{3,2,1,0:T(8,128)} %get-tuple-element.21), channel_id=1, source_target_pairs={{0,1},{1,0},{2,3},{3,2},{4,5},{5,4},{6,7},{7,6},{8,9},{9,8},{10,11... | collective-permute-start | bytes 393224 | tf_op jit(solution)/shard_map/ppermute | solution.py:451
  7.4 14.9 %collective-permute-start = (f32[3,16,8,128]{3,2,1,0:T(8,128)}, f32[3,16,8,128]{3,2,1,0:T(8,128)S(1)}, u32[]{:S(2)}, u32[]{:S(2)}) collective-permute-start(f32[3,16,8,128]{3,2,1,0:T(8,128)} %get-tuple-element.16), channel_id=1, source_target_pairs={{0,8},{4,12},{8,0},{12,4},{16,24},{20,28},{24,16},{28,20},{1,9},{5... | collective-permute-start | bytes 589832 | tf_op jit(solution)/shard_map/ppermute | solution.py:447
  10.0 12.6 %collective-permute-start.1 = (f32[3,16,8,128]{3,2,1,0:T(8,128)}, f32[3,16,8,128]{3,2,1,0:T(8,128)S(1)}, u32[]{:S(2)}, u32[]{:S(2)}) collective-permute-start(f32[3,16,8,128]{3,2,1,0:T(8,128)} %get-tuple-element.17), channel_id=1, source_target_pairs={{0,24},{4,28},{8,16},{12,20},{16,8},{20,12},{24,0},{28,4},{1,25},{... | collective-permute-start | bytes 589832 | tf_op jit(solution)/shard_map/ppermute | solution.py:447
  12.5 14.9 %collective-permute-start.2 = (f32[3,16,8,128]{3,2,1,0:T(8,128)}, f32[3,16,8,128]{3,2,1,0:T(8,128)S(1)}, u32[]{:S(2)}, u32[]{:S(2)}) collective-permute-start(f32[3,16,8,128]{3,2,1,0:T(8,128)} %get-tuple-element.18), channel_id=1, source_target_pairs={{0,28},{4,8},{8,4},{12,16},{16,12},{20,24},{24,20},{28,0},{1,29},{... | collective-permute-start | bytes 589832 | tf_op jit(solution)/shard_map/ppermute | solution.py:447
  14.8 12.6 %collective-permute-start.3 = (f32[3,16,8,128]{3,2,1,0:T(8,128)}, f32[3,16,8,128]{3,2,1,0:T(8,128)S(1)}, u32[]{:S(2)}, u32[]{:S(2)}) collective-permute-start(f32[3,16,8,128]{3,2,1,0:T(8,128)} %get-tuple-element.19), channel_id=1, source_target_pairs={{0,4},{4,0},{8,12},{12,8},{16,20},{20,16},{24,28},{28,24},{1,5},{5... | collective-permute-start | bytes 589832 | tf_op jit(solution)/shard_map/ppermute | solution.py:447
  14.8 0.8 %copy-start.4 = (s32[4,16,128]{2,1,0:T(8,128)S(1)}, s32[4,16,128]{2,1,0:T(8,128)}, u32[]{:S(2)}) copy-start(s32[4,16,128]{2,1,0:T(8,128)} %get-tuple-element.23.table_ref) | copy-start | bytes 98308
  15.6 1.1 %copy-start.7 = (f32[3,63,8,128]{3,2,1,0:T(8,128)S(1)}, f32[3,63,8,128]{3,2,1,0:T(8,128)}, u32[]{:S(2)}) copy-start(f32[3,63,8,128]{3,2,1,0:T(8,128)} %get-tuple-element.24) | copy-start | bytes 2322436
  16.7 1.2 %copy-start.11 = (f32[1,16,8,128]{3,2,1,0:T(8,128)S(1)}, f32[1,16,8,128]{3,2,1,0:T(8,128)}, u32[]{:S(2)}) copy-start(f32[1,16,8,128]{3,2,1,0:T(8,128)} %get-tuple-element.22) | copy-start | bytes 196612
  16.7 2.8 %copy-start = (f32[9,56,128]{2,1,0:T(8,128)S(1)}, f32[9,56,128]{2,1,0:T(8,128)}, u32[]{:S(2)}) copy-start(f32[9,56,128]{2,1,0:T(8,128)} %state_ref.1) | copy-start | bytes 774148
  16.7 2.8 %copy-start.2 = (f32[3,9,9,128]{3,0,2,1:T(4,128)S(1)}, f32[3,9,9,128]{3,0,2,1:T(4,128)}, u32[]{:S(2)}) copy-start(f32[3,9,9,128]{3,0,2,1:T(4,128)} %param.18) | copy-start | bytes 373252
  16.7 2.8 %copy-start.5 = (s32[4,16,128]{2,1,0:T(8,128)S(1)}, s32[4,16,128]{2,1,0:T(8,128)}, u32[]{:S(2)}) copy-start(s32[4,16,128]{2,1,0:T(8,128)} %get-tuple-element.23.table_ref) | copy-start | bytes 98308
  16.7 2.8 %copy-start.6 = (f32[4,12,56,56]{3,2,1,0:T(8,128)S(1)}, f32[4,12,56,56]{3,2,1,0:T(8,128)}, u32[]{:S(2)}) copy-start(f32[4,12,56,56]{3,2,1,0:T(8,128)} %neighbour_ref.1) | copy-start | bytes 1806340
  16.7 2.7 %copy-start.8 = (f32[4,9,9,128]{3,0,2,1:T(4,128)S(1)}, f32[4,9,9,128]{3,0,2,1:T(4,128)}, u32[]{:S(2)}) copy-start(f32[4,9,9,128]{3,0,2,1:T(4,128)} %param.19) | copy-start | bytes 497668
  16.7 2.7 %copy-start.9 = (f32[4,56,56]{2,1,0:T(8,128)S(1)}, f32[4,56,56]{2,1,0:T(8,128)}, u32[]{:S(2)}) copy-start(f32[4,56,56]{2,1,0:T(8,128)} %local_ref.1) | copy-start | bytes 150532
  16.7 2.7 %copy-start.10 = (f32[3,56,56]{2,1,0:T(8,128)S(1)}, f32[3,56,56]{2,1,0:T(8,128)}, u32[]{:S(2)}) copy-start(f32[3,56,56]{2,1,0:T(8,128)} %volume_ref.1) | copy-start | bytes 112900
  17.9 9.5 %collective-permute-start.5 = (f32[2,16,8,128]{3,2,1,0:T(8,128)S(1)}, f32[2,16,8,128]{3,2,1,0:T(8,128)S(1)}, u32[]{:S(2)}, u32[]{:S(2)}) collective-permute-start(f32[2,16,8,128]{3,2,1,0:T(8,128)S(1)} %pad_maximum_fusion), channel_id=1, source_target_pairs={{0,2},{1,3},{2,0},{3,1},{4,6},{5,7},{6,4},{7,5},{8,10},{9,11},{10,... | collective-permute-start | bytes 393224 | tf_op jit(solution)/shard_map/ppermute | solution.py:451
  19.5 7.9 %copy-start.1 = (f32[4,9,9,128]{3,0,2,1:T(4,128)S(1)}, f32[4,9,9,128]{3,0,2,1:T(4,128)}, u32[]{:S(2)}) copy-start(f32[4,9,9,128]{3,0,2,1:T(4,128)} %param.20) | copy-start | bytes 497668
  19.5 7.9 %copy-start.3 = (f32[16,8,128]{2,1,0:T(8,128)S(1)}, f32[16,8,128]{2,1,0:T(8,128)}, u32[]{:S(2)}) copy-start(f32[16,8,128]{2,1,0:T(8,128)} %get-tuple-element.20.first_ref) | copy-start | bytes 196612

commit v7 on v5

--- a/solution.py
+++ b/solution.py
@@ -369,7 +369,8 @@
 
     def unpack(group):
         for cluster in range(clusters):
-            pools = turned(odd, high, [region_refs[b][cluster, group] for b in range(BLOCKS)])
+            brought = [region_refs[b][cluster, group] for b in range(BLOCKS + 1)]
+            pools = turned(odd, high, [brought[0] + brought[BLOCKS], *brought[1:BLOCKS]])
             for member, pool in enumerate(pools):
                 if group * BLOCKS + member < count:
                     pool_ref[cluster, group * BLOCKS + member] = pool
@@ -441,12 +442,13 @@
     return [pl.BlockSpec(memory_space=pltpu.HBM) for _ in range(count)]
 
 
-def paired(value, axis, pairing):
+def paired(value, axis, pairing, halves=(0, 1)):
     count = lax.axis_size(axis)
     pairs = []
     for source in range(count):
-        offset = OFFSETS[pairing_blocks(source)[pairing]]
-        pairs.append((source, (source + offset) % count))
+        if source // 4 % 2 in halves:
+            offset = OFFSETS[pairing_blocks(source)[pairing]]
+            pairs.append((source, (source + offset) % count))
     return lax.ppermute(value, axis, pairs)
 
 
@@ -532,9 +534,12 @@
         here,
     )
 
-    arrived = [paired(packed[p], "region", p) for p in range(BLOCKS)]
+    early = paired(packed[0], "region", 0, (0,))
+    arrived = [paired(packed[p], "region", p) for p in range(1, BLOCKS)]
     first, beside, across = packed[BLOCKS:]
     beside = swapped(beside, "sub", 1)
+    last, beside = lax.optimization_barrier((packed[0], beside))
+    late = paired(last, "region", 0, (1,))
     across = swapped(jnp.concatenate([across, beside[1:]], axis=0), "sub", 2)
     integrals = integrals.reshape(clusters, quants, modes, lanes)
     near_partner = pl.pallas_call(
@@ -580,7 +585,7 @@
     return pl.pallas_call(
         neighbour_kernel,
         out_shape=shape((quants, modes, lanes), F32),
-        in_specs=[whole(BLOCKS), *whole(8)],
+        in_specs=[whole(BLOCKS + 1), *whole(8)],
         out_specs=whole(1)[0],
         scratch_shapes=[
             pltpu.VMEM((clusters, count, 8, lanes), F32),
@@ -589,7 +594,7 @@
         ],
         compiler_params=near_params,
         name="neighbour",
-    )(arrived, first, beside, across, table, near_partner, minus, flux, own)
+    )([early, *arrived, late], first, beside, across, table, near_partner, minus, flux, own)
 
 
 def solution(mesh):

time: 30.3 us -> 33.7 us (1.11)
  the two profiles are of different devices: /device:TPU:0 before, /device:TPU:29 now
where the time goes in v7:
time: 33.7 us; the launch traced here: 33.4 us
  Pallas kernels  15.2 us (45%)
  starting transfers between devices  8.52 us (25%)
  waiting for transfers between devices  7.6 us (23%)
  local copies, waits for them, and re-layouts  1.95 us (6%)
    ppermute x5, waiting for transfers between devices, paired(): return lax.ppermute(value, axis, pairs)  7.6 us
    pallas_call x1, Pallas kernels, local(): pl.pallas_call(predict_kernel, out_shape=(shape((clusters, count, 8, lane...  6.84 us
    ppermute x5, starting transfers between devices, paired(): return lax.ppermute(value, axis, pairs)  6.52 us
    pallas_call x1, Pallas kernels, local(): pl.pallas_call(neighbour_kernel, out_shape=shape((quants, modes, lanes),...  4.47 us
    pallas_call x1, Pallas kernels, local(): pl.pallas_call(own_kernel, out_shape=(shape((quants, modes, lanes), F32),...  2.76 us
    ppermute x2, starting transfers between devices, swapped(): lax.ppermute(value, axis, [(s, s ^ bit) for s in range(lax.axis_size(axis...  2 us
    unnamed x26, local copies, waits for them, and re-layouts  1.94 us
    pallas_call x1, Pallas kernels, local(): pl.pallas_call(near_kernel, out_shape=shape((faces, quants, modes, lanes)...  1.08 us
  transfers between devices with their start and end apart: 7, of which 3 were waited for; matrix products, arithmetic and copies ran while one was open for 0% of the time, Pallas kernels for 11%

profile of v7, /device:TPU:29, one launch (start us, length us, event | category | flops | bytes accessed | tf_op | source)
XLA Modules:
  0.0 33.4 jit_solution(18408193812879869782)
XLA Ops:
  0.0 6.8 %predict.1 = (f32[3,63,8,128]{3,2,1,0:T(8,128)}, s32[4,16,128]{2,1,0:T(8,128)}, f32[3,16,8,128]{3,2,1,0:T(8,128)}, f32[3,16,8,128]{3,2,1,0:T(8,128)}, f32[3,16,8...) custom-call(f32[9,56,128]{2,1,0:T(8,128)} %state_ref.1, ...), custom_call_target="tpu_custom_call" | custom-call | tf_op jit(solution)/shard_map/predict/pallas_call | solution.py:493
  6.8 0.7 %collective-permute-start.4 = (f32[2,16,8,128]{3,2,1,0:T(8,128)}, f32[2,16,8,128]{3,2,1,0:T(8,128)S(1)}, u32[]{:S(2)}, u32[]{:S(2)}) collective-permute-start(f32[2,16,8,128]{3,2,1,0:T(8,128)} %get-tuple-element.22), channel_id=1, source_target_pairs={{0,1},{1,0},{2,3},{3,2},{4,5},{5,4},{6,7},{7,6},{8,9},{9,8},{10,11... | collective-permute-start | bytes 393224 | tf_op jit(solution)/shard_map/ppermute | solution.py:456
  7.6 0.7 %collective-permute-start = (f32[3,16,8,128]{3,2,1,0:T(8,128)}, f32[3,16,8,128]{3,2,1,0:T(8,128)S(1)}, u32[]{:S(2)}, u32[]{:S(2)}) collective-permute-start(f32[3,16,8,128]{3,2,1,0:T(8,128)} %get-tuple-element.23), channel_id=1, source_target_pairs={{0,8},{4,12},{8,0},{12,4},{1,9},{5,13},{9,1},{13,5},{2,10},{6,14},... | collective-permute-start | bytes 589832 | tf_op jit(solution)/shard_map/ppermute | solution.py:452
  8.3 2.5 %collective-permute-start.1 = (f32[3,16,8,128]{3,2,1,0:T(8,128)}, f32[3,16,8,128]{3,2,1,0:T(8,128)S(1)}, u32[]{:S(2)}, u32[]{:S(2)}) collective-permute-start(f32[3,16,8,128]{3,2,1,0:T(8,128)} %get-tuple-element.19), channel_id=1, source_target_pairs={{0,24},{4,28},{8,16},{12,20},{16,8},{20,12},{24,0},{28,4},{1,25},{... | collective-permute-start | bytes 589832 | tf_op jit(solution)/shard_map/ppermute | solution.py:452
  10.8 0.7 %collective-permute-start.2 = (f32[3,16,8,128]{3,2,1,0:T(8,128)}, f32[3,16,8,128]{3,2,1,0:T(8,128)S(1)}, u32[]{:S(2)}, u32[]{:S(2)}) collective-permute-start(f32[3,16,8,128]{3,2,1,0:T(8,128)} %get-tuple-element.20), channel_id=1, source_target_pairs={{0,28},{4,8},{8,4},{12,16},{16,12},{20,24},{24,20},{28,0},{1,29},{... | collective-permute-start | bytes 589832 | tf_op jit(solution)/shard_map/ppermute | solution.py:452
  11.5 0.7 %collective-permute-start.3 = (f32[3,16,8,128]{3,2,1,0:T(8,128)}, f32[3,16,8,128]{3,2,1,0:T(8,128)S(1)}, u32[]{:S(2)}, u32[]{:S(2)}) collective-permute-start(f32[3,16,8,128]{3,2,1,0:T(8,128)} %get-tuple-element.21), channel_id=1, source_target_pairs={{0,4},{4,0},{8,12},{12,8},{16,24},{20,28},{24,16},{28,20},{1,5},{5... | collective-permute-start | bytes 589832 | tf_op jit(solution)/shard_map/ppermute | solution.py:452
  12.2 0.8 %copy-done.4 = s32[4,16,128]{2,1,0:T(8,128)S(1)} copy-done((s32[4,16,128]{2,1,0:T(8,128)S(1)}, s32[4,16,128]{2,1,0:T(8,128)}, u32[]{:S(2)}) %copy-start.4) | copy-done | bytes 32792
  13.0 1.1 %copy-done.7 = f32[3,63,8,128]{3,2,1,0:T(8,128)S(1)} copy-done((f32[3,63,8,128]{3,2,1,0:T(8,128)S(1)}, f32[3,63,8,128]{3,2,1,0:T(8,128)}, u32[]{:S(2)}) %copy-start.7) | copy-done | bytes 774168
  14.1 0.0 copy-start.6
  14.1 0.0 copy-start.8
  14.1 0.0 copy-start.9
  14.1 0.0 copy-start.10
  14.2 1.1 %near.1.near_ref = f32[4,9,56,128]{3,2,1,0:T(8,128)S(1)} custom-call(s32[4,16,128]{2,1,0:T(8,128)S(1)} %copy-done.4, f32[3,9,56,128]{3,2,1,0:T(8,128)S(1)} %bitcast.12), custom_call_target="tpu_custom_call" | custom-call | flops 4000000000 | bytes 8000000 | tf_op jit(solution)/shard_map/near/pallas_call | solution.py:545
  15.2 0.0 collective-permute-done.4.beside_ref
  15.3 1.3 %collective-permute-start.6 = (f32[2,16,8,128]{3,2,1,0:T(8,128)S(1)}, f32[2,16,8,128]{3,2,1,0:T(8,128)S(1)}, u32[]{:S(2)}, u32[]{:S(2)}) collective-permute-start(f32[2,16,8,128]{3,2,1,0:T(8,128)S(1)} %pad_maximum_fusion), channel_id=1, source_target_pairs={{0,2},{1,3},{2,0},{3,1},{4,6},{5,7},{6,4},{7,5},{8,10},{9,11},{10,... | collective-permute-start | bytes 393224 | tf_op jit(solution)/shard_map/ppermute | solution.py:456
  16.6 0.0 collective-permute-done.region_refs_0_
  16.6 1.9 %collective-permute-start.5 = (f32[3,16,8,128]{3,2,1,0:T(8,128)S(1)}, f32[3,16,8,128]{3,2,1,0:T(8,128)S(1)}, u32[]{:S(2)}, u32[]{:S(2)}) collective-permute-start(f32[3,16,8,128]{3,2,1,0:T(8,128)S(1)} %copy-done.12), channel_id=1, source_target_pairs={{16,20},{20,16},{24,28},{28,24},{17,21},{21,17},{25,29},{29,25},{1... | collective-permute-start | bytes 589832 | tf_op jit(solution)/shard_map/ppermute | solution.py:452
  18.6 0.0 copy-start.1
  18.6 2.8 %own.1 = (f32[9,56,128]{2,1,0:T(8,128)S(1)}, bf16[4,672,176]{2,1,0:T(8,128)(2,1)S(1)}) custom-call(s32[4,16,128]{2,1,0:T(8,128)S(1)} %copy-done.5, f32[3,56,56]{2,1,0:T(8,128)S(1)} %copy-done.10, f32[4,56,56]{2,1,0:T(8,128)S(1)} %copy-done.9, f32[3,9,56,128]{3,2,1,0:T(8,128)S(1)} %bitcast.13, f32[9,56,128]{2,1,0:T(8,128)S(1)} %copy-done, ...), custom_call_target="tpu_custom_call" | custom-call | flops 4000000000 | bytes 8000000 | tf_op jit(solution)/shard_map/own/pallas_call | solution.py:557
  21.3 0.0 collective-permute-done.1.region_refs_1_
  21.4 3.0 %collective-permute-done.2.region_refs_2_ = f32[3,16,8,128]{3,2,1,0:T(8,128)S(1)} collective-permute-done((f32[3,16,8,128]{3,2,1,0:T(8,128)}, f32[3,16,8,128]{3,2,1,0:T(8,128)S(1)}, u32[]{:S(2)}, u32[]{:S(2)}) %collective-permute-start.2) | collective-permute-done | bytes 196640 | tf_op jit(solution)/shard_map/ppermute | solution.py:452
  24.3 0.9 %collective-permute-done.3.region_refs_3_ = f32[3,16,8,128]{3,2,1,0:T(8,128)S(1)} collective-permute-done((f32[3,16,8,128]{3,2,1,0:T(8,128)}, f32[3,16,8,128]{3,2,1,0:T(8,128)S(1)}, u32[]{:S(2)}, u32[]{:S(2)}) %collective-permute-start.3) | collective-permute-done | bytes 196640 | tf_op jit(solution)/shard_map/ppermute | solution.py:452
  25.2 3.7 %collective-permute-done.5.region_refs_4_ = f32[3,16,8,128]{3,2,1,0:T(8,128)S(1)} collective-permute-done((f32[3,16,8,128]{3,2,1,0:T(8,128)S(1)}, f32[3,16,8,128]{3,2,1,0:T(8,128)S(1)}, u32[]{:S(2)}, u32[]{:S(2)}) %collective-permute-start.5) | collective-permute-done | bytes 196640 | tf_op jit(solution)/shard_map/ppermute | solution.py:452
  29.0 4.5 %neighbour.1 = f32[9,56,128]{2,1,0:T(8,128)} custom-call(f32[3,16,8,128]{3,2,1,0:T(8,128)S(1)} %collective-permute-done.region_refs_0_, f32[3,16,8,128]{3,2,1,0:T(8,128)S(1)} %collective-permute-done.1.region_refs_1_, f32[3,16,8,128]{3,2,1,0:T(8,128)S(1)} %collective-permute-done.2.region_refs_2_, ...), custom_call_target="tpu_custom_call" | custom-call | tf_op jit(solution)/shard_map/neighbour/pallas_call | solution.py:585
  (22 shorter events, 0.1 us)
Async XLA Ops:
  6.8 8.4 %collective-permute-start.4 = (f32[2,16,8,128]{3,2,1,0:T(8,128)}, f32[2,16,8,128]{3,2,1,0:T(8,128)S(1)}, u32[]{:S(2)}, u32[]{:S(2)}) collective-permute-start(f32[2,16,8,128]{3,2,1,0:T(8,128)} %get-tuple-element.22), channel_id=1, source_target_pairs={{0,1},{1,0},{2,3},{3,2},{4,5},{5,4},{6,7},{7,6},{8,9},{9,8},{10,11... | collective-permute-start | bytes 393224 | tf_op jit(solution)/shard_map/ppermute | solution.py:456
  7.6 9.0 %collective-permute-start = (f32[3,16,8,128]{3,2,1,0:T(8,128)}, f32[3,16,8,128]{3,2,1,0:T(8,128)S(1)}, u32[]{:S(2)}, u32[]{:S(2)}) collective-permute-start(f32[3,16,8,128]{3,2,1,0:T(8,128)} %get-tuple-element.23), channel_id=1, source_target_pairs={{0,8},{4,12},{8,0},{12,4},{1,9},{5,13},{9,1},{13,5},{2,10},{6,14},... | collective-permute-start | bytes 589832 | tf_op jit(solution)/shard_map/ppermute | solution.py:452
  8.3 13.1 %collective-permute-start.1 = (f32[3,16,8,128]{3,2,1,0:T(8,128)}, f32[3,16,8,128]{3,2,1,0:T(8,128)S(1)}, u32[]{:S(2)}, u32[]{:S(2)}) collective-permute-start(f32[3,16,8,128]{3,2,1,0:T(8,128)} %get-tuple-element.19), channel_id=1, source_target_pairs={{0,24},{4,28},{8,16},{12,20},{16,8},{20,12},{24,0},{28,4},{1,25},{... | collective-permute-start | bytes 589832 | tf_op jit(solution)/shard_map/ppermute | solution.py:452
  10.8 13.5 %collective-permute-start.2 = (f32[3,16,8,128]{3,2,1,0:T(8,128)}, f32[3,16,8,128]{3,2,1,0:T(8,128)S(1)}, u32[]{:S(2)}, u32[]{:S(2)}) collective-permute-start(f32[3,16,8,128]{3,2,1,0:T(8,128)} %get-tuple-element.20), channel_id=1, source_target_pairs={{0,28},{4,8},{8,4},{12,16},{16,12},{20,24},{24,20},{28,0},{1,29},{... | collective-permute-start | bytes 589832 | tf_op jit(solution)/shard_map/ppermute | solution.py:452
  11.5 13.7 %collective-permute-start.3 = (f32[3,16,8,128]{3,2,1,0:T(8,128)}, f32[3,16,8,128]{3,2,1,0:T(8,128)S(1)}, u32[]{:S(2)}, u32[]{:S(2)}) collective-permute-start(f32[3,16,8,128]{3,2,1,0:T(8,128)} %get-tuple-element.21), channel_id=1, source_target_pairs={{0,4},{4,0},{8,12},{12,8},{16,24},{20,28},{24,16},{28,20},{1,5},{5... | collective-permute-start | bytes 589832 | tf_op jit(solution)/shard_map/ppermute | solution.py:452
  12.2 0.8 %copy-start.4 = (s32[4,16,128]{2,1,0:T(8,128)S(1)}, s32[4,16,128]{2,1,0:T(8,128)}, u32[]{:S(2)}) copy-start(s32[4,16,128]{2,1,0:T(8,128)} %get-tuple-element.27.table_ref) | copy-start | bytes 98308
  13.0 1.1 %copy-start.7 = (f32[3,63,8,128]{3,2,1,0:T(8,128)S(1)}, f32[3,63,8,128]{3,2,1,0:T(8,128)}, u32[]{:S(2)}) copy-start(f32[3,63,8,128]{3,2,1,0:T(8,128)} %get-tuple-element.28) | copy-start | bytes 2322436
  14.1 1.2 %copy-start.11 = (f32[1,16,8,128]{3,2,1,0:T(8,128)S(1)}, f32[1,16,8,128]{3,2,1,0:T(8,128)}, u32[]{:S(2)}) copy-start(f32[1,16,8,128]{3,2,1,0:T(8,128)} %get-tuple-element.26) | copy-start | bytes 196612
  14.1 2.5 %copy-start.12 = (f32[3,16,8,128]{3,2,1,0:T(8,128)S(1)}, f32[3,16,8,128]{3,2,1,0:T(8,128)}, u32[]{:S(2)}) copy-start(f32[3,16,8,128]{3,2,1,0:T(8,128)} %get-tuple-element.23) | copy-start | bytes 589828
  14.1 4.4 %copy-start = (f32[9,56,128]{2,1,0:T(8,128)S(1)}, f32[9,56,128]{2,1,0:T(8,128)}, u32[]{:S(2)}) copy-start(f32[9,56,128]{2,1,0:T(8,128)} %state_ref.1) | copy-start | bytes 774148
  14.1 4.4 %copy-start.2 = (f32[3,9,9,128]{3,0,2,1:T(4,128)S(1)}, f32[3,9,9,128]{3,0,2,1:T(4,128)}, u32[]{:S(2)}) copy-start(f32[3,9,9,128]{3,0,2,1:T(4,128)} %param.18) | copy-start | bytes 373252
  14.1 4.4 %copy-start.5 = (s32[4,16,128]{2,1,0:T(8,128)S(1)}, s32[4,16,128]{2,1,0:T(8,128)}, u32[]{:S(2)}) copy-start(s32[4,16,128]{2,1,0:T(8,128)} %get-tuple-element.27.table_ref) | copy-start | bytes 98308
  14.1 4.4 %copy-start.6 = (f32[4,12,56,56]{3,2,1,0:T(8,128)S(1)}, f32[4,12,56,56]{3,2,1,0:T(8,128)}, u32[]{:S(2)}) copy-start(f32[4,12,56,56]{3,2,1,0:T(8,128)} %neighbour_ref.1) | copy-start | bytes 1806340
  14.1 4.4 %copy-start.8 = (f32[4,9,9,128]{3,0,2,1:T(4,128)S(1)}, f32[4,9,9,128]{3,0,2,1:T(4,128)}, u32[]{:S(2)}) copy-start(f32[4,9,9,128]{3,0,2,1:T(4,128)} %param.19) | copy-start | bytes 497668
  14.1 4.4 %copy-start.9 = (f32[4,56,56]{2,1,0:T(8,128)S(1)}, f32[4,56,56]{2,1,0:T(8,128)}, u32[]{:S(2)}) copy-start(f32[4,56,56]{2,1,0:T(8,128)} %local_ref.1) | copy-start | bytes 150532
  14.1 4.4 %copy-start.10 = (f32[3,56,56]{2,1,0:T(8,128)S(1)}, f32[3,56,56]{2,1,0:T(8,128)}, u32[]{:S(2)}) copy-start(f32[3,56,56]{2,1,0:T(8,128)} %volume_ref.1) | copy-start | bytes 112900
  15.3 9.9 %collective-permute-start.6 = (f32[2,16,8,128]{3,2,1,0:T(8,128)S(1)}, f32[2,16,8,128]{3,2,1,0:T(8,128)S(1)}, u32[]{:S(2)}, u32[]{:S(2)}) collective-permute-start(f32[2,16,8,128]{3,2,1,0:T(8,128)S(1)} %pad_maximum_fusion), channel_id=1, source_target_pairs={{0,2},{1,3},{2,0},{3,1},{4,6},{5,7},{6,4},{7,5},{8,10},{9,11},{10,... | collective-permute-start | bytes 393224 | tf_op jit(solution)/shard_map/ppermute | solution.py:456
  16.6 12.4 %collective-permute-start.5 = (f32[3,16,8,128]{3,2,1,0:T(8,128)S(1)}, f32[3,16,8,128]{3,2,1,0:T(8,128)S(1)}, u32[]{:S(2)}, u32[]{:S(2)}) collective-permute-start(f32[3,16,8,128]{3,2,1,0:T(8,128)S(1)} %copy-done.12), channel_id=1, source_target_pairs={{16,20},{20,16},{24,28},{28,24},{17,21},{21,17},{25,29},{29,25},{1... | collective-permute-start | bytes 589832 | tf_op jit(solution)/shard_map/ppermute | solution.py:452
  18.6 10.4 %copy-start.1 = (f32[4,9,9,128]{3,0,2,1:T(4,128)S(1)}, f32[4,9,9,128]{3,0,2,1:T(4,128)}, u32[]{:S(2)}) copy-start(f32[4,9,9,128]{3,0,2,1:T(4,128)} %param.20) | copy-start | bytes 497668
  18.6 10.4 %copy-start.3 = (f32[16,8,128]{2,1,0:T(8,128)S(1)}, f32[16,8,128]{2,1,0:T(8,128)}, u32[]{:S(2)}) copy-start(f32[16,8,128]{2,1,0:T(8,128)} %get-tuple-element.24.first_ref) | copy-start | bytes 196612

commit v8 on v5

--- a/solution.py
+++ b/solution.py
@@ -396,18 +396,18 @@
     block = 2
     blocks = [range(first, min(first + block, quants)) for first in range(0, quants, block)]
 
-    def flux(face, rows):
-        orient = spread(face, 2 * BLOCKS + 1)
-        masks = [orient == o for o in range(orients)]
+    def mix(face, rows):
         mixed = [None for _ in rows]
         for column in range(quants):
             value = partner_ref[face, column]
             for place, row in enumerate(rows):
                 term = minus_ref[row, column, pl.ds(face, 1), :] * value
                 mixed[place] = term if mixed[place] is None else mixed[place] + term
-        every = jnp.dot(
-            flux_ref[face], split_rows(jnp.concatenate(mixed, axis=1)), preferred_element_type=F32
-        )
+        return split_rows(jnp.concatenate(mixed, axis=1))
+
+    def select(face, rows, every):
+        orient = spread(face, 2 * BLOCKS + 1)
+        masks = [orient == o for o in range(orients)]
         for place, row in enumerate(rows):
             for first in range(0, modes, 8):
                 columns = slice(place * lanes, (place + 1) * lanes)
@@ -425,12 +425,17 @@
     for group in range(groups(count)):
         unpack(group)
     gather(0, range(count))
-    for face in range(faces):
-        step = (count + len(blocks) - 1) // len(blocks)
-        for place, rows in enumerate(blocks):
-            flux(face, rows)
-            if face + 1 < faces:
-                gather(face + 1, range(place * step, min((place + 1) * step, count)))
+    step = (count + len(blocks) - 1) // len(blocks)
+    steps = [(face, place) for face in range(faces) for place in range(len(blocks))]
+    ready = mix(0, blocks[0])
+    for at, (face, place) in enumerate(steps):
+        every = jnp.dot(flux_ref[face], ready, preferred_element_type=F32)
+        if face + 1 < faces:
+            gather(face + 1, range(place * step, min((place + 1) * step, count)))
+        if at + 1 < len(steps):
+            later, block = steps[at + 1]
+            ready = mix(later, blocks[block])
+        select(face, blocks[place], every)
 
 
 def whole(count):

time: 30.3 us -> 30.3 us (level)
  no operation moved by 1% of the time
where the time goes in v8:
time: 30.3 us; the launch traced here: 30.1 us
  Pallas kernels  15.1 us (50%)
  starting transfers between devices  9.52 us (31%)
  waiting for transfers between devices  3.33 us (11%)
  local copies, waits for them, and re-layouts  1.94 us (6%)
    ppermute x4, starting transfers between devices, paired(): return lax.ppermute(value, axis, pairs)  7.42 us
    pallas_call x1, Pallas kernels, local(): pl.pallas_call(predict_kernel, out_shape=(shape((clusters, count, 8, lane...  6.83 us
    pallas_call x1, Pallas kernels, local(): pl.pallas_call(neighbour_kernel, out_shape=shape((quants, modes, lanes),...  4.44 us
    ppermute x4, waiting for transfers between devices, paired(): return lax.ppermute(value, axis, pairs)  3.32 us
    pallas_call x1, Pallas kernels, local(): pl.pallas_call(own_kernel, out_shape=(shape((quants, modes, lanes), F32),...  2.76 us
    ppermute x2, starting transfers between devices, swapped(): lax.ppermute(value, axis, [(s, s ^ bit) for s in range(lax.axis_size(axis...  2.11 us
    unnamed x24, local copies, waits for them, and re-layouts  1.94 us
    pallas_call x1, Pallas kernels, local(): pl.pallas_call(near_kernel, out_shape=shape((faces, quants, modes, lanes)...  1.08 us
  transfers between devices with their start and end apart: 6, of which 2 were waited for; matrix products, arithmetic and copies ran while one was open for 0% of the time, Pallas kernels for 13%

profile of v8, /device:TPU:0, one launch (start us, length us, event | category | flops | bytes accessed | tf_op | source)
XLA Modules:
  0.0 30.1 jit_solution(5885506916700119610)
XLA Ops:
  0.0 6.8 %predict.1 = (f32[3,63,8,128]{3,2,1,0:T(8,128)}, s32[4,16,128]{2,1,0:T(8,128)}, f32[3,16,8,128]{3,2,1,0:T(8,128)}, f32[3,16,8,128]{3,2,1,0:T(8,128)}, f32[3,16,8...) custom-call(f32[9,56,128]{2,1,0:T(8,128)} %state_ref.1, ...), custom_call_target="tpu_custom_call" | custom-call | tf_op jit(solution)/shard_map/predict/pallas_call | solution.py:496
  6.8 0.5 %collective-permute-start.4 = (f32[2,16,8,128]{3,2,1,0:T(8,128)}, f32[2,16,8,128]{3,2,1,0:T(8,128)S(1)}, u32[]{:S(2)}, u32[]{:S(2)}) collective-permute-start(f32[2,16,8,128]{3,2,1,0:T(8,128)} %get-tuple-element.21), channel_id=1, source_target_pairs={{0,1},{1,0},{2,3},{3,2},{4,5},{5,4},{6,7},{7,6},{8,9},{9,8},{10,11... | collective-permute-start | bytes 393224 | tf_op jit(solution)/shard_map/ppermute | solution.py:459
  7.4 2.6 %collective-permute-start = (f32[3,16,8,128]{3,2,1,0:T(8,128)}, f32[3,16,8,128]{3,2,1,0:T(8,128)S(1)}, u32[]{:S(2)}, u32[]{:S(2)}) collective-permute-start(f32[3,16,8,128]{3,2,1,0:T(8,128)} %get-tuple-element.16), channel_id=1, source_target_pairs={{0,8},{4,12},{8,0},{12,4},{16,20},{20,16},{24,28},{28,24},{1,9},{5... | collective-permute-start | bytes 589832 | tf_op jit(solution)/shard_map/ppermute | solution.py:455
  10.0 3.5 %collective-permute-start.1 = (f32[3,16,8,128]{3,2,1,0:T(8,128)}, f32[3,16,8,128]{3,2,1,0:T(8,128)S(1)}, u32[]{:S(2)}, u32[]{:S(2)}) collective-permute-start(f32[3,16,8,128]{3,2,1,0:T(8,128)} %get-tuple-element.17), channel_id=1, source_target_pairs={{0,24},{4,28},{8,16},{12,20},{16,8},{20,12},{24,0},{28,4},{1,25},{... | collective-permute-start | bytes 589832 | tf_op jit(solution)/shard_map/ppermute | solution.py:455
  13.6 1.2 %collective-permute-start.2 = (f32[3,16,8,128]{3,2,1,0:T(8,128)}, f32[3,16,8,128]{3,2,1,0:T(8,128)S(1)}, u32[]{:S(2)}, u32[]{:S(2)}) collective-permute-start(f32[3,16,8,128]{3,2,1,0:T(8,128)} %get-tuple-element.18), channel_id=1, source_target_pairs={{0,28},{4,8},{8,4},{12,16},{16,12},{20,24},{24,20},{28,0},{1,29},{... | collective-permute-start | bytes 589832 | tf_op jit(solution)/shard_map/ppermute | solution.py:455
  14.8 0.0 collective-permute-start.3
  14.8 0.8 %copy-done.4 = s32[4,16,128]{2,1,0:T(8,128)S(1)} copy-done((s32[4,16,128]{2,1,0:T(8,128)S(1)}, s32[4,16,128]{2,1,0:T(8,128)}, u32[]{:S(2)}) %copy-start.4) | copy-done | bytes 32792
  15.5 1.1 %copy-done.7 = f32[3,63,8,128]{3,2,1,0:T(8,128)S(1)} copy-done((f32[3,63,8,128]{3,2,1,0:T(8,128)S(1)}, f32[3,63,8,128]{3,2,1,0:T(8,128)}, u32[]{:S(2)}) %copy-start.7) | copy-done | bytes 774168
  16.7 0.0 copy-start.6
  16.7 0.0 copy-start.8
  16.7 0.0 copy-start.9
  16.7 0.0 copy-start.10
  16.7 1.1 %near.1.near_ref = f32[4,9,56,128]{3,2,1,0:T(8,128)S(1)} custom-call(s32[4,16,128]{2,1,0:T(8,128)S(1)} %copy-done.4, f32[3,9,56,128]{3,2,1,0:T(8,128)S(1)} %bitcast.12), custom_call_target="tpu_custom_call" | custom-call | flops 4000000000 | bytes 8000000 | tf_op jit(solution)/shard_map/near/pallas_call | solution.py:545
  17.8 0.0 collective-permute-done.4.beside_ref
  17.9 1.6 %collective-permute-start.5 = (f32[2,16,8,128]{3,2,1,0:T(8,128)S(1)}, f32[2,16,8,128]{3,2,1,0:T(8,128)S(1)}, u32[]{:S(2)}, u32[]{:S(2)}) collective-permute-start(f32[2,16,8,128]{3,2,1,0:T(8,128)S(1)} %pad_maximum_fusion), channel_id=1, source_target_pairs={{0,2},{1,3},{2,0},{3,1},{4,6},{5,7},{6,4},{7,5},{8,10},{9,11},{10,... | collective-permute-start | bytes 393224 | tf_op jit(solution)/shard_map/ppermute | solution.py:459
  19.5 0.0 copy-done.5
  19.5 0.0 copy-start.1
  19.5 2.8 %own.1 = (f32[9,56,128]{2,1,0:T(8,128)S(1)}, bf16[4,672,176]{2,1,0:T(8,128)(2,1)S(1)}) custom-call(s32[4,16,128]{2,1,0:T(8,128)S(1)} %copy-done.5, f32[3,56,56]{2,1,0:T(8,128)S(1)} %copy-done.10, f32[4,56,56]{2,1,0:T(8,128)S(1)} %copy-done.9, f32[3,9,56,128]{3,2,1,0:T(8,128)S(1)} %bitcast.13, f32[9,56,128]{2,1,0:T(8,128)S(1)} %copy-done, ...), custom_call_target="tpu_custom_call" | custom-call | flops 4000000000 | bytes 8000000 | tf_op jit(solution)/shard_map/own/pallas_call | solution.py:557
  22.3 0.0 collective-permute-done.region_refs_0_
  22.3 0.0 collective-permute-done.1.region_refs_1_
  22.3 2.7 %collective-permute-done.2.region_refs_2_ = f32[3,16,8,128]{3,2,1,0:T(8,128)S(1)} collective-permute-done((f32[3,16,8,128]{3,2,1,0:T(8,128)}, f32[3,16,8,128]{3,2,1,0:T(8,128)S(1)}, u32[]{:S(2)}, u32[]{:S(2)}) %collective-permute-start.2) | collective-permute-done | bytes 196640 | tf_op jit(solution)/shard_map/ppermute | solution.py:455
  25.0 0.6 %collective-permute-done.3.region_refs_3_ = f32[3,16,8,128]{3,2,1,0:T(8,128)S(1)} collective-permute-done((f32[3,16,8,128]{3,2,1,0:T(8,128)}, f32[3,16,8,128]{3,2,1,0:T(8,128)S(1)}, u32[]{:S(2)}, u32[]{:S(2)}) %collective-permute-start.3) | collective-permute-done | bytes 196640 | tf_op jit(solution)/shard_map/ppermute | solution.py:455
  25.6 0.0 collective-permute-done.5.across_ref
  25.6 4.4 %neighbour.1 = f32[9,56,128]{2,1,0:T(8,128)} custom-call(f32[3,16,8,128]{3,2,1,0:T(8,128)S(1)} %collective-permute-done.region_refs_0_, f32[3,16,8,128]{3,2,1,0:T(8,128)S(1)} %collective-permute-done.1.region_refs_1_, f32[3,16,8,128]{3,2,1,0:T(8,128)S(1)} %collective-permute-done.2.region_refs_2_, ...), custom_call_target="tpu_custom_call" | custom-call | tf_op jit(solution)/shard_map/neighbour/pallas_call | solution.py:585
  (18 shorter events, 0.0 us)
Async XLA Ops:
  6.8 11.0 %collective-permute-start.4 = (f32[2,16,8,128]{3,2,1,0:T(8,128)}, f32[2,16,8,128]{3,2,1,0:T(8,128)S(1)}, u32[]{:S(2)}, u32[]{:S(2)}) collective-permute-start(f32[2,16,8,128]{3,2,1,0:T(8,128)} %get-tuple-element.21), channel_id=1, source_target_pairs={{0,1},{1,0},{2,3},{3,2},{4,5},{5,4},{6,7},{7,6},{8,9},{9,8},{10,11... | collective-permute-start | bytes 393224 | tf_op jit(solution)/shard_map/ppermute | solution.py:459
  7.4 14.9 %collective-permute-start = (f32[3,16,8,128]{3,2,1,0:T(8,128)}, f32[3,16,8,128]{3,2,1,0:T(8,128)S(1)}, u32[]{:S(2)}, u32[]{:S(2)}) collective-permute-start(f32[3,16,8,128]{3,2,1,0:T(8,128)} %get-tuple-element.16), channel_id=1, source_target_pairs={{0,8},{4,12},{8,0},{12,4},{16,20},{20,16},{24,28},{28,24},{1,9},{5... | collective-permute-start | bytes 589832 | tf_op jit(solution)/shard_map/ppermute | solution.py:455
  10.0 12.3 %collective-permute-start.1 = (f32[3,16,8,128]{3,2,1,0:T(8,128)}, f32[3,16,8,128]{3,2,1,0:T(8,128)S(1)}, u32[]{:S(2)}, u32[]{:S(2)}) collective-permute-start(f32[3,16,8,128]{3,2,1,0:T(8,128)} %get-tuple-element.17), channel_id=1, source_target_pairs={{0,24},{4,28},{8,16},{12,20},{16,8},{20,12},{24,0},{28,4},{1,25},{... | collective-permute-start | bytes 589832 | tf_op jit(solution)/shard_map/ppermute | solution.py:455
  13.6 11.4 %collective-permute-start.2 = (f32[3,16,8,128]{3,2,1,0:T(8,128)}, f32[3,16,8,128]{3,2,1,0:T(8,128)S(1)}, u32[]{:S(2)}, u32[]{:S(2)}) collective-permute-start(f32[3,16,8,128]{3,2,1,0:T(8,128)} %get-tuple-element.18), channel_id=1, source_target_pairs={{0,28},{4,8},{8,4},{12,16},{16,12},{20,24},{24,20},{28,0},{1,29},{... | collective-permute-start | bytes 589832 | tf_op jit(solution)/shard_map/ppermute | solution.py:455
  14.8 10.8 %collective-permute-start.3 = (f32[3,16,8,128]{3,2,1,0:T(8,128)}, f32[3,16,8,128]{3,2,1,0:T(8,128)S(1)}, u32[]{:S(2)}, u32[]{:S(2)}) collective-permute-start(f32[3,16,8,128]{3,2,1,0:T(8,128)} %get-tuple-element.19), channel_id=1, source_target_pairs={{0,4},{4,0},{8,12},{12,8},{16,24},{20,28},{24,16},{28,20},{1,5},{5... | collective-permute-start | bytes 589832 | tf_op jit(solution)/shard_map/ppermute | solution.py:455
  14.8 0.8 %copy-start.4 = (s32[4,16,128]{2,1,0:T(8,128)S(1)}, s32[4,16,128]{2,1,0:T(8,128)}, u32[]{:S(2)}) copy-start(s32[4,16,128]{2,1,0:T(8,128)} %get-tuple-element.23.table_ref) | copy-start | bytes 98308
  15.5 1.1 %copy-start.7 = (f32[3,63,8,128]{3,2,1,0:T(8,128)S(1)}, f32[3,63,8,128]{3,2,1,0:T(8,128)}, u32[]{:S(2)}) copy-start(f32[3,63,8,128]{3,2,1,0:T(8,128)} %get-tuple-element.24) | copy-start | bytes 2322436
  16.7 1.2 %copy-start.11 = (f32[1,16,8,128]{3,2,1,0:T(8,128)S(1)}, f32[1,16,8,128]{3,2,1,0:T(8,128)}, u32[]{:S(2)}) copy-start(f32[1,16,8,128]{3,2,1,0:T(8,128)} %get-tuple-element.22) | copy-start | bytes 196612
  16.7 2.8 %copy-start = (f32[9,56,128]{2,1,0:T(8,128)S(1)}, f32[9,56,128]{2,1,0:T(8,128)}, u32[]{:S(2)}) copy-start(f32[9,56,128]{2,1,0:T(8,128)} %state_ref.1) | copy-start | bytes 774148
  16.7 2.8 %copy-start.2 = (f32[3,9,9,128]{3,0,2,1:T(4,128)S(1)}, f32[3,9,9,128]{3,0,2,1:T(4,128)}, u32[]{:S(2)}) copy-start(f32[3,9,9,128]{3,0,2,1:T(4,128)} %param.18) | copy-start | bytes 373252
  16.7 2.8 %copy-start.5 = (s32[4,16,128]{2,1,0:T(8,128)S(1)}, s32[4,16,128]{2,1,0:T(8,128)}, u32[]{:S(2)}) copy-start(s32[4,16,128]{2,1,0:T(8,128)} %get-tuple-element.23.table_ref) | copy-start | bytes 98308
  16.7 2.8 %copy-start.6 = (f32[4,12,56,56]{3,2,1,0:T(8,128)S(1)}, f32[4,12,56,56]{3,2,1,0:T(8,128)}, u32[]{:S(2)}) copy-start(f32[4,12,56,56]{3,2,1,0:T(8,128)} %neighbour_ref.1) | copy-start | bytes 1806340
  16.7 2.8 %copy-start.8 = (f32[4,9,9,128]{3,0,2,1:T(4,128)S(1)}, f32[4,9,9,128]{3,0,2,1:T(4,128)}, u32[]{:S(2)}) copy-start(f32[4,9,9,128]{3,0,2,1:T(4,128)} %param.19) | copy-start | bytes 497668
  16.7 2.8 %copy-start.9 = (f32[4,56,56]{2,1,0:T(8,128)S(1)}, f32[4,56,56]{2,1,0:T(8,128)}, u32[]{:S(2)}) copy-start(f32[4,56,56]{2,1,0:T(8,128)} %local_ref.1) | copy-start | bytes 150532
  16.7 2.8 %copy-start.10 = (f32[3,56,56]{2,1,0:T(8,128)S(1)}, f32[3,56,56]{2,1,0:T(8,128)}, u32[]{:S(2)}) copy-start(f32[3,56,56]{2,1,0:T(8,128)} %volume_ref.1) | copy-start | bytes 112900
  17.9 7.8 %collective-permute-start.5 = (f32[2,16,8,128]{3,2,1,0:T(8,128)S(1)}, f32[2,16,8,128]{3,2,1,0:T(8,128)S(1)}, u32[]{:S(2)}, u32[]{:S(2)}) collective-permute-start(f32[2,16,8,128]{3,2,1,0:T(8,128)S(1)} %pad_maximum_fusion), channel_id=1, source_target_pairs={{0,2},{1,3},{2,0},{3,1},{4,6},{5,7},{6,4},{7,5},{8,10},{9,11},{10,... | collective-permute-start | bytes 393224 | tf_op jit(solution)/shard_map/ppermute | solution.py:459
  19.5 6.1 %copy-start.1 = (f32[4,9,9,128]{3,0,2,1:T(4,128)S(1)}, f32[4,9,9,128]{3,0,2,1:T(4,128)}, u32[]{:S(2)}) copy-start(f32[4,9,9,128]{3,0,2,1:T(4,128)} %param.20) | copy-start | bytes 497668
  19.5 6.1 %copy-start.3 = (f32[16,8,128]{2,1,0:T(8,128)S(1)}, f32[16,8,128]{2,1,0:T(8,128)}, u32[]{:S(2)}) copy-start(f32[16,8,128]{2,1,0:T(8,128)} %get-tuple-element.20.first_ref) | copy-start | bytes 196612

commit v9 on v5

--- a/solution.py
+++ b/solution.py
@@ -393,7 +393,7 @@
             other = lane_gather(sub_pool_ref[at], sub_index[at % BLOCKS])
             partner_ref[face, at // per_quant, rows, :] = jnp.where(hits[clusters], other, total)
 
-    block = 2
+    block = 4
     blocks = [range(first, min(first + block, quants)) for first in range(0, quants, block)]
 
     def flux(face, rows):

time: 30.3 us -> 30.3 us (level)
  no operation moved by 1% of the time
where the time goes in v9:
time: 30.3 us; the launch traced here: 30.1 us
  Pallas kernels  15.1 us (50%)
  starting transfers between devices  9.52 us (31%)
  waiting for transfers between devices  3.33 us (11%)
  local copies, waits for them, and re-layouts  1.94 us (6%)
    ppermute x4, starting transfers between devices, paired(): return lax.ppermute(value, axis, pairs)  7.42 us
    pallas_call x1, Pallas kernels, local(): pl.pallas_call(predict_kernel, out_shape=(shape((clusters, count, 8, lane...  6.83 us
    pallas_call x1, Pallas kernels, local(): pl.pallas_call(neighbour_kernel, out_shape=shape((quants, modes, lanes),...  4.43 us
    ppermute x4, waiting for transfers between devices, paired(): return lax.ppermute(value, axis, pairs)  3.32 us
    pallas_call x1, Pallas kernels, local(): pl.pallas_call(own_kernel, out_shape=(shape((quants, modes, lanes), F32),...  2.76 us
    ppermute x2, starting transfers between devices, swapped(): lax.ppermute(value, axis, [(s, s ^ bit) for s in range(lax.axis_size(axis...  2.11 us
    unnamed x24, local copies, waits for them, and re-layouts  1.94 us
    pallas_call x1, Pallas kernels, local(): pl.pallas_call(near_kernel, out_shape=shape((faces, quants, modes, lanes)...  1.08 us
  transfers between devices with their start and end apart: 6, of which 2 were waited for; matrix products, arithmetic and copies ran while one was open for 0% of the time, Pallas kernels for 13%

profile of v9, /device:TPU:0, one launch (start us, length us, event | category | flops | bytes accessed | tf_op | source)
XLA Modules:
  0.0 30.1 jit_solution(2411531726103908369)
XLA Ops:
  0.0 6.8 %predict.1 = (f32[3,63,8,128]{3,2,1,0:T(8,128)}, s32[4,16,128]{2,1,0:T(8,128)}, f32[3,16,8,128]{3,2,1,0:T(8,128)}, f32[3,16,8,128]{3,2,1,0:T(8,128)}, f32[3,16,8...) custom-call(f32[9,56,128]{2,1,0:T(8,128)} %state_ref.1, ...), custom_call_target="tpu_custom_call" | custom-call | tf_op jit(solution)/shard_map/predict/pallas_call | solution.py:491
  6.8 0.5 %collective-permute-start.4 = (f32[2,16,8,128]{3,2,1,0:T(8,128)}, f32[2,16,8,128]{3,2,1,0:T(8,128)S(1)}, u32[]{:S(2)}, u32[]{:S(2)}) collective-permute-start(f32[2,16,8,128]{3,2,1,0:T(8,128)} %get-tuple-element.21), channel_id=1, source_target_pairs={{0,1},{1,0},{2,3},{3,2},{4,5},{5,4},{6,7},{7,6},{8,9},{9,8},{10,11... | collective-permute-start | bytes 393224 | tf_op jit(solution)/shard_map/ppermute | solution.py:454
  7.4 2.6 %collective-permute-start = (f32[3,16,8,128]{3,2,1,0:T(8,128)}, f32[3,16,8,128]{3,2,1,0:T(8,128)S(1)}, u32[]{:S(2)}, u32[]{:S(2)}) collective-permute-start(f32[3,16,8,128]{3,2,1,0:T(8,128)} %get-tuple-element.16), channel_id=1, source_target_pairs={{0,8},{4,12},{8,0},{12,4},{16,20},{20,16},{24,28},{28,24},{1,9},{5... | collective-permute-start | bytes 589832 | tf_op jit(solution)/shard_map/ppermute | solution.py:450
  10.0 3.5 %collective-permute-start.1 = (f32[3,16,8,128]{3,2,1,0:T(8,128)}, f32[3,16,8,128]{3,2,1,0:T(8,128)S(1)}, u32[]{:S(2)}, u32[]{:S(2)}) collective-permute-start(f32[3,16,8,128]{3,2,1,0:T(8,128)} %get-tuple-element.17), channel_id=1, source_target_pairs={{0,24},{4,28},{8,16},{12,20},{16,8},{20,12},{24,0},{28,4},{1,25},{... | collective-permute-start | bytes 589832 | tf_op jit(solution)/shard_map/ppermute | solution.py:450
  13.6 1.2 %collective-permute-start.2 = (f32[3,16,8,128]{3,2,1,0:T(8,128)}, f32[3,16,8,128]{3,2,1,0:T(8,128)S(1)}, u32[]{:S(2)}, u32[]{:S(2)}) collective-permute-start(f32[3,16,8,128]{3,2,1,0:T(8,128)} %get-tuple-element.18), channel_id=1, source_target_pairs={{0,28},{4,8},{8,4},{12,16},{16,12},{20,24},{24,20},{28,0},{1,29},{... | collective-permute-start | bytes 589832 | tf_op jit(solution)/shard_map/ppermute | solution.py:450
  14.8 0.0 collective-permute-start.3
  14.8 0.8 %copy-done.4 = s32[4,16,128]{2,1,0:T(8,128)S(1)} copy-done((s32[4,16,128]{2,1,0:T(8,128)S(1)}, s32[4,16,128]{2,1,0:T(8,128)}, u32[]{:S(2)}) %copy-start.4) | copy-done | bytes 32792
  15.5 1.1 %copy-done.7 = f32[3,63,8,128]{3,2,1,0:T(8,128)S(1)} copy-done((f32[3,63,8,128]{3,2,1,0:T(8,128)S(1)}, f32[3,63,8,128]{3,2,1,0:T(8,128)}, u32[]{:S(2)}) %copy-start.7) | copy-done | bytes 774168
  16.7 0.0 copy-start.6
  16.7 0.0 copy-start.8
  16.7 0.0 copy-start.9
  16.7 0.0 copy-start.10
  16.7 1.1 %near.1.near_ref = f32[4,9,56,128]{3,2,1,0:T(8,128)S(1)} custom-call(s32[4,16,128]{2,1,0:T(8,128)S(1)} %copy-done.4, f32[3,9,56,128]{3,2,1,0:T(8,128)S(1)} %bitcast.12), custom_call_target="tpu_custom_call" | custom-call | flops 4000000000 | bytes 8000000 | tf_op jit(solution)/shard_map/near/pallas_call | solution.py:540
  17.8 0.0 collective-permute-done.4.beside_ref
  17.9 1.6 %collective-permute-start.5 = (f32[2,16,8,128]{3,2,1,0:T(8,128)S(1)}, f32[2,16,8,128]{3,2,1,0:T(8,128)S(1)}, u32[]{:S(2)}, u32[]{:S(2)}) collective-permute-start(f32[2,16,8,128]{3,2,1,0:T(8,128)S(1)} %pad_maximum_fusion), channel_id=1, source_target_pairs={{0,2},{1,3},{2,0},{3,1},{4,6},{5,7},{6,4},{7,5},{8,10},{9,11},{10,... | collective-permute-start | bytes 393224 | tf_op jit(solution)/shard_map/ppermute | solution.py:454
  19.4 0.0 copy-done
  19.5 0.0 copy-start.1
  19.5 2.8 %own.1 = (f32[9,56,128]{2,1,0:T(8,128)S(1)}, bf16[4,672,176]{2,1,0:T(8,128)(2,1)S(1)}) custom-call(s32[4,16,128]{2,1,0:T(8,128)S(1)} %copy-done.5, f32[3,56,56]{2,1,0:T(8,128)S(1)} %copy-done.10, f32[4,56,56]{2,1,0:T(8,128)S(1)} %copy-done.9, f32[3,9,56,128]{3,2,1,0:T(8,128)S(1)} %bitcast.13, f32[9,56,128]{2,1,0:T(8,128)S(1)} %copy-done, ...), custom_call_target="tpu_custom_call" | custom-call | flops 4000000000 | bytes 8000000 | tf_op jit(solution)/shard_map/own/pallas_call | solution.py:552
  22.3 0.0 collective-permute-done.region_refs_0_
  22.3 0.0 collective-permute-done.1.region_refs_1_
  22.3 2.7 %collective-permute-done.2.region_refs_2_ = f32[3,16,8,128]{3,2,1,0:T(8,128)S(1)} collective-permute-done((f32[3,16,8,128]{3,2,1,0:T(8,128)}, f32[3,16,8,128]{3,2,1,0:T(8,128)S(1)}, u32[]{:S(2)}, u32[]{:S(2)}) %collective-permute-start.2) | collective-permute-done | bytes 196640 | tf_op jit(solution)/shard_map/ppermute | solution.py:450
  25.0 0.6 %collective-permute-done.3.region_refs_3_ = f32[3,16,8,128]{3,2,1,0:T(8,128)S(1)} collective-permute-done((f32[3,16,8,128]{3,2,1,0:T(8,128)}, f32[3,16,8,128]{3,2,1,0:T(8,128)S(1)}, u32[]{:S(2)}, u32[]{:S(2)}) %collective-permute-start.3) | collective-permute-done | bytes 196640 | tf_op jit(solution)/shard_map/ppermute | solution.py:450
  25.6 0.0 collective-permute-done.5.across_ref
  25.6 4.4 %neighbour.1 = f32[9,56,128]{2,1,0:T(8,128)} custom-call(f32[3,16,8,128]{3,2,1,0:T(8,128)S(1)} %collective-permute-done.region_refs_0_, f32[3,16,8,128]{3,2,1,0:T(8,128)S(1)} %collective-permute-done.1.region_refs_1_, f32[3,16,8,128]{3,2,1,0:T(8,128)S(1)} %collective-permute-done.2.region_refs_2_, ...), custom_call_target="tpu_custom_call" | custom-call | tf_op jit(solution)/shard_map/neighbour/pallas_call | solution.py:580
  (18 shorter events, 0.0 us)
Async XLA Ops:
  6.8 11.0 %collective-permute-start.4 = (f32[2,16,8,128]{3,2,1,0:T(8,128)}, f32[2,16,8,128]{3,2,1,0:T(8,128)S(1)}, u32[]{:S(2)}, u32[]{:S(2)}) collective-permute-start(f32[2,16,8,128]{3,2,1,0:T(8,128)} %get-tuple-element.21), channel_id=1, source_target_pairs={{0,1},{1,0},{2,3},{3,2},{4,5},{5,4},{6,7},{7,6},{8,9},{9,8},{10,11... | collective-permute-start | bytes 393224 | tf_op jit(solution)/shard_map/ppermute | solution.py:454
  7.4 14.9 %collective-permute-start = (f32[3,16,8,128]{3,2,1,0:T(8,128)}, f32[3,16,8,128]{3,2,1,0:T(8,128)S(1)}, u32[]{:S(2)}, u32[]{:S(2)}) collective-permute-start(f32[3,16,8,128]{3,2,1,0:T(8,128)} %get-tuple-element.16), channel_id=1, source_target_pairs={{0,8},{4,12},{8,0},{12,4},{16,20},{20,16},{24,28},{28,24},{1,9},{5... | collective-permute-start | bytes 589832 | tf_op jit(solution)/shard_map/ppermute | solution.py:450
  10.0 12.3 %collective-permute-start.1 = (f32[3,16,8,128]{3,2,1,0:T(8,128)}, f32[3,16,8,128]{3,2,1,0:T(8,128)S(1)}, u32[]{:S(2)}, u32[]{:S(2)}) collective-permute-start(f32[3,16,8,128]{3,2,1,0:T(8,128)} %get-tuple-element.17), channel_id=1, source_target_pairs={{0,24},{4,28},{8,16},{12,20},{16,8},{20,12},{24,0},{28,4},{1,25},{... | collective-permute-start | bytes 589832 | tf_op jit(solution)/shard_map/ppermute | solution.py:450
  13.6 11.4 %collective-permute-start.2 = (f32[3,16,8,128]{3,2,1,0:T(8,128)}, f32[3,16,8,128]{3,2,1,0:T(8,128)S(1)}, u32[]{:S(2)}, u32[]{:S(2)}) collective-permute-start(f32[3,16,8,128]{3,2,1,0:T(8,128)} %get-tuple-element.18), channel_id=1, source_target_pairs={{0,28},{4,8},{8,4},{12,16},{16,12},{20,24},{24,20},{28,0},{1,29},{... | collective-permute-start | bytes 589832 | tf_op jit(solution)/shard_map/ppermute | solution.py:450
  14.8 10.8 %collective-permute-start.3 = (f32[3,16,8,128]{3,2,1,0:T(8,128)}, f32[3,16,8,128]{3,2,1,0:T(8,128)S(1)}, u32[]{:S(2)}, u32[]{:S(2)}) collective-permute-start(f32[3,16,8,128]{3,2,1,0:T(8,128)} %get-tuple-element.19), channel_id=1, source_target_pairs={{0,4},{4,0},{8,12},{12,8},{16,24},{20,28},{24,16},{28,20},{1,5},{5... | collective-permute-start | bytes 589832 | tf_op jit(solution)/shard_map/ppermute | solution.py:450
  14.8 0.8 %copy-start.4 = (s32[4,16,128]{2,1,0:T(8,128)S(1)}, s32[4,16,128]{2,1,0:T(8,128)}, u32[]{:S(2)}) copy-start(s32[4,16,128]{2,1,0:T(8,128)} %get-tuple-element.23.table_ref) | copy-start | bytes 98308
  15.5 1.1 %copy-start.7 = (f32[3,63,8,128]{3,2,1,0:T(8,128)S(1)}, f32[3,63,8,128]{3,2,1,0:T(8,128)}, u32[]{:S(2)}) copy-start(f32[3,63,8,128]{3,2,1,0:T(8,128)} %get-tuple-element.24) | copy-start | bytes 2322436
  16.7 1.2 %copy-start.11 = (f32[1,16,8,128]{3,2,1,0:T(8,128)S(1)}, f32[1,16,8,128]{3,2,1,0:T(8,128)}, u32[]{:S(2)}) copy-start(f32[1,16,8,128]{3,2,1,0:T(8,128)} %get-tuple-element.22) | copy-start | bytes 196612
  16.7 2.8 %copy-start = (f32[9,56,128]{2,1,0:T(8,128)S(1)}, f32[9,56,128]{2,1,0:T(8,128)}, u32[]{:S(2)}) copy-start(f32[9,56,128]{2,1,0:T(8,128)} %state_ref.1) | copy-start | bytes 774148
  16.7 2.8 %copy-start.2 = (f32[3,9,9,128]{3,0,2,1:T(4,128)S(1)}, f32[3,9,9,128]{3,0,2,1:T(4,128)}, u32[]{:S(2)}) copy-start(f32[3,9,9,128]{3,0,2,1:T(4,128)} %param.18) | copy-start | bytes 373252
  16.7 2.8 %copy-start.5 = (s32[4,16,128]{2,1,0:T(8,128)S(1)}, s32[4,16,128]{2,1,0:T(8,128)}, u32[]{:S(2)}) copy-start(s32[4,16,128]{2,1,0:T(8,128)} %get-tuple-element.23.table_ref) | copy-start | bytes 98308
  16.7 2.8 %copy-start.6 = (f32[4,12,56,56]{3,2,1,0:T(8,128)S(1)}, f32[4,12,56,56]{3,2,1,0:T(8,128)}, u32[]{:S(2)}) copy-start(f32[4,12,56,56]{3,2,1,0:T(8,128)} %neighbour_ref.1) | copy-start | bytes 1806340
  16.7 2.8 %copy-start.8 = (f32[4,9,9,128]{3,0,2,1:T(4,128)S(1)}, f32[4,9,9,128]{3,0,2,1:T(4,128)}, u32[]{:S(2)}) copy-start(f32[4,9,9,128]{3,0,2,1:T(4,128)} %param.19) | copy-start | bytes 497668
  16.7 2.8 %copy-start.9 = (f32[4,56,56]{2,1,0:T(8,128)S(1)}, f32[4,56,56]{2,1,0:T(8,128)}, u32[]{:S(2)}) copy-start(f32[4,56,56]{2,1,0:T(8,128)} %local_ref.1) | copy-start | bytes 150532
  16.7 2.8 %copy-start.10 = (f32[3,56,56]{2,1,0:T(8,128)S(1)}, f32[3,56,56]{2,1,0:T(8,128)}, u32[]{:S(2)}) copy-start(f32[3,56,56]{2,1,0:T(8,128)} %volume_ref.1) | copy-start | bytes 112900
  17.9 7.8 %collective-permute-start.5 = (f32[2,16,8,128]{3,2,1,0:T(8,128)S(1)}, f32[2,16,8,128]{3,2,1,0:T(8,128)S(1)}, u32[]{:S(2)}, u32[]{:S(2)}) collective-permute-start(f32[2,16,8,128]{3,2,1,0:T(8,128)S(1)} %pad_maximum_fusion), channel_id=1, source_target_pairs={{0,2},{1,3},{2,0},{3,1},{4,6},{5,7},{6,4},{7,5},{8,10},{9,11},{10,... | collective-permute-start | bytes 393224 | tf_op jit(solution)/shard_map/ppermute | solution.py:454
  19.5 6.1 %copy-start.1 = (f32[4,9,9,128]{3,0,2,1:T(4,128)S(1)}, f32[4,9,9,128]{3,0,2,1:T(4,128)}, u32[]{:S(2)}) copy-start(f32[4,9,9,128]{3,0,2,1:T(4,128)} %param.20) | copy-start | bytes 497668
  19.5 6.1 %copy-start.3 = (f32[16,8,128]{2,1,0:T(8,128)S(1)}, f32[16,8,128]{2,1,0:T(8,128)}, u32[]{:S(2)}) copy-start(f32[16,8,128]{2,1,0:T(8,128)} %get-tuple-element.20.first_ref) | copy-start | bytes 196612

commit v10 on v9

--- a/solution.py
+++ b/solution.py
@@ -81,7 +81,7 @@
     odd = region % 2
     near, beside = 3 - 3 * second, 2 - odd
     turn = half * (beside - near)
-    return [near + turn, 3 * second, 1 + odd, beside - turn]
+    return [near + turn, 1 + odd, 3 * second, beside - turn]
 
 
 def predict_kernel(

time: 30.3 us -> 31.6 us (1.043)
  the two profiles are of different devices: /device:TPU:0 before, /device:TPU:25 now
where the time goes in v10:
time: 31.6 us; the launch traced here: 31.4 us
  Pallas kernels  15.1 us (48%)
  waiting for transfers between devices  7.69 us (24%)
  starting transfers between devices  6.48 us (21%)
  local copies, waits for them, and re-layouts  1.94 us (6%)
    ppermute x4, waiting for transfers between devices, paired(): return lax.ppermute(value, axis, pairs)  7.69 us
    pallas_call x1, Pallas kernels, local(): pl.pallas_call(predict_kernel, out_shape=(shape((clusters, count, 8, lane...  6.84 us
    ppermute x4, starting transfers between devices, paired(): return lax.ppermute(value, axis, pairs)  4.46 us
    pallas_call x1, Pallas kernels, local(): pl.pallas_call(neighbour_kernel, out_shape=shape((quants, modes, lanes),...  4.43 us
    pallas_call x1, Pallas kernels, local(): pl.pallas_call(own_kernel, out_shape=(shape((quants, modes, lanes), F32),...  2.76 us
    ppermute x2, starting transfers between devices, swapped(): lax.ppermute(value, axis, [(s, s ^ bit) for s in range(lax.axis_size(axis...  2.01 us
    unnamed x24, local copies, waits for them, and re-layouts  1.94 us
    pallas_call x1, Pallas kernels, local(): pl.pallas_call(near_kernel, out_shape=shape((faces, quants, modes, lanes)...  1.08 us
  transfers between devices with their start and end apart: 6, of which 2 were waited for; matrix products, arithmetic and copies ran while one was open for 0% of the time, Pallas kernels for 12%

profile of v10, /device:TPU:25, one launch (start us, length us, event | category | flops | bytes accessed | tf_op | source)
XLA Modules:
  0.0 31.4 jit_solution(13317831354646322606)
XLA Ops:
  0.0 6.8 %predict.1 = (f32[3,63,8,128]{3,2,1,0:T(8,128)}, s32[4,16,128]{2,1,0:T(8,128)}, f32[3,16,8,128]{3,2,1,0:T(8,128)}, f32[3,16,8,128]{3,2,1,0:T(8,128)}, f32[3,16,8...) custom-call(f32[9,56,128]{2,1,0:T(8,128)} %state_ref.1, ...), custom_call_target="tpu_custom_call" | custom-call | tf_op jit(solution)/shard_map/predict/pallas_call | solution.py:491
  6.8 0.7 %collective-permute-start.4 = (f32[2,16,8,128]{3,2,1,0:T(8,128)}, f32[2,16,8,128]{3,2,1,0:T(8,128)S(1)}, u32[]{:S(2)}, u32[]{:S(2)}) collective-permute-start(f32[2,16,8,128]{3,2,1,0:T(8,128)} %get-tuple-element.21), channel_id=1, source_target_pairs={{0,1},{1,0},{2,3},{3,2},{4,5},{5,4},{6,7},{7,6},{8,9},{9,8},{10,11... | collective-permute-start | bytes 393224 | tf_op jit(solution)/shard_map/ppermute | solution.py:454
  7.6 1.3 %collective-permute-start = (f32[3,16,8,128]{3,2,1,0:T(8,128)}, f32[3,16,8,128]{3,2,1,0:T(8,128)S(1)}, u32[]{:S(2)}, u32[]{:S(2)}) collective-permute-start(f32[3,16,8,128]{3,2,1,0:T(8,128)} %get-tuple-element.16), channel_id=1, source_target_pairs={{0,8},{4,12},{8,0},{12,4},{16,20},{20,16},{24,28},{28,24},{1,9},{5... | collective-permute-start | bytes 589832 | tf_op jit(solution)/shard_map/ppermute | solution.py:450
  8.8 0.1 collective-permute-start.1
  9.0 3.1 %collective-permute-start.2 = (f32[3,16,8,128]{3,2,1,0:T(8,128)}, f32[3,16,8,128]{3,2,1,0:T(8,128)S(1)}, u32[]{:S(2)}, u32[]{:S(2)}) collective-permute-start(f32[3,16,8,128]{3,2,1,0:T(8,128)} %get-tuple-element.18), channel_id=1, source_target_pairs={{0,24},{4,28},{8,16},{12,20},{16,8},{20,12},{24,0},{28,4},{1,25},{... | collective-permute-start | bytes 589832 | tf_op jit(solution)/shard_map/ppermute | solution.py:450
  12.0 0.0 collective-permute-start.3
  12.1 0.8 %copy-done.4 = s32[4,16,128]{2,1,0:T(8,128)S(1)} copy-done((s32[4,16,128]{2,1,0:T(8,128)S(1)}, s32[4,16,128]{2,1,0:T(8,128)}, u32[]{:S(2)}) %copy-start.4) | copy-done | bytes 32792
  12.8 1.1 %copy-done.7 = f32[3,63,8,128]{3,2,1,0:T(8,128)S(1)} copy-done((f32[3,63,8,128]{3,2,1,0:T(8,128)S(1)}, f32[3,63,8,128]{3,2,1,0:T(8,128)}, u32[]{:S(2)}) %copy-start.7) | copy-done | bytes 774168
  14.0 0.0 copy-start.6
  14.0 0.0 copy-start.8
  14.0 0.0 copy-start.9
  14.0 0.0 copy-start.10
  14.0 1.1 %near.1.near_ref = f32[4,9,56,128]{3,2,1,0:T(8,128)S(1)} custom-call(s32[4,16,128]{2,1,0:T(8,128)S(1)} %copy-done.4, f32[3,9,56,128]{3,2,1,0:T(8,128)S(1)} %bitcast.12), custom_call_target="tpu_custom_call" | custom-call | flops 4000000000 | bytes 8000000 | tf_op jit(solution)/shard_map/near/pallas_call | solution.py:540
  15.1 0.0 collective-permute-done.4.beside_ref
  15.1 0.0 copy-done.11
  15.1 1.3 %collective-permute-start.5 = (f32[2,16,8,128]{3,2,1,0:T(8,128)S(1)}, f32[2,16,8,128]{3,2,1,0:T(8,128)S(1)}, u32[]{:S(2)}, u32[]{:S(2)}) collective-permute-start(f32[2,16,8,128]{3,2,1,0:T(8,128)S(1)} %pad_maximum_fusion), channel_id=1, source_target_pairs={{0,2},{1,3},{2,0},{3,1},{4,6},{5,7},{6,4},{7,5},{8,10},{9,11},{10,... | collective-permute-start | bytes 393224 | tf_op jit(solution)/shard_map/ppermute | solution.py:454
  16.5 0.0 copy-start.1
  16.5 2.8 %own.1 = (f32[9,56,128]{2,1,0:T(8,128)S(1)}, bf16[4,672,176]{2,1,0:T(8,128)(2,1)S(1)}) custom-call(s32[4,16,128]{2,1,0:T(8,128)S(1)} %copy-done.5, f32[3,56,56]{2,1,0:T(8,128)S(1)} %copy-done.10, f32[4,56,56]{2,1,0:T(8,128)S(1)} %copy-done.9, f32[3,9,56,128]{3,2,1,0:T(8,128)S(1)} %bitcast.13, f32[9,56,128]{2,1,0:T(8,128)S(1)} %copy-done, ...), custom_call_target="tpu_custom_call" | custom-call | flops 4000000000 | bytes 8000000 | tf_op jit(solution)/shard_map/own/pallas_call | solution.py:552
  19.2 0.0 collective-permute-done.region_refs_0_
  19.3 0.0 collective-permute-done.1.region_refs_1_
  19.3 3.3 %collective-permute-done.2.region_refs_2_ = f32[3,16,8,128]{3,2,1,0:T(8,128)S(1)} collective-permute-done((f32[3,16,8,128]{3,2,1,0:T(8,128)}, f32[3,16,8,128]{3,2,1,0:T(8,128)S(1)}, u32[]{:S(2)}, u32[]{:S(2)}) %collective-permute-start.2) | collective-permute-done | bytes 196640 | tf_op jit(solution)/shard_map/ppermute | solution.py:450
  22.6 4.4 %collective-permute-done.3.region_refs_3_ = f32[3,16,8,128]{3,2,1,0:T(8,128)S(1)} collective-permute-done((f32[3,16,8,128]{3,2,1,0:T(8,128)}, f32[3,16,8,128]{3,2,1,0:T(8,128)S(1)}, u32[]{:S(2)}, u32[]{:S(2)}) %collective-permute-start.3) | collective-permute-done | bytes 196640 | tf_op jit(solution)/shard_map/ppermute | solution.py:450
  27.0 0.0 collective-permute-done.5.across_ref
  27.0 4.4 %neighbour.1 = f32[9,56,128]{2,1,0:T(8,128)} custom-call(f32[3,16,8,128]{3,2,1,0:T(8,128)S(1)} %collective-permute-done.region_refs_0_, f32[3,16,8,128]{3,2,1,0:T(8,128)S(1)} %collective-permute-done.1.region_refs_1_, f32[3,16,8,128]{3,2,1,0:T(8,128)S(1)} %collective-permute-done.2.region_refs_2_, ...), custom_call_target="tpu_custom_call" | custom-call | tf_op jit(solution)/shard_map/neighbour/pallas_call | solution.py:580
  (18 shorter events, 0.0 us)
Async XLA Ops:
  6.8 8.2 %collective-permute-start.4 = (f32[2,16,8,128]{3,2,1,0:T(8,128)}, f32[2,16,8,128]{3,2,1,0:T(8,128)S(1)}, u32[]{:S(2)}, u32[]{:S(2)}) collective-permute-start(f32[2,16,8,128]{3,2,1,0:T(8,128)} %get-tuple-element.21), channel_id=1, source_target_pairs={{0,1},{1,0},{2,3},{3,2},{4,5},{5,4},{6,7},{7,6},{8,9},{9,8},{10,11... | collective-permute-start | bytes 393224 | tf_op jit(solution)/shard_map/ppermute | solution.py:454
  7.6 11.7 %collective-permute-start = (f32[3,16,8,128]{3,2,1,0:T(8,128)}, f32[3,16,8,128]{3,2,1,0:T(8,128)S(1)}, u32[]{:S(2)}, u32[]{:S(2)}) collective-permute-start(f32[3,16,8,128]{3,2,1,0:T(8,128)} %get-tuple-element.16), channel_id=1, source_target_pairs={{0,8},{4,12},{8,0},{12,4},{16,20},{20,16},{24,28},{28,24},{1,9},{5... | collective-permute-start | bytes 589832 | tf_op jit(solution)/shard_map/ppermute | solution.py:450
  8.8 10.4 %collective-permute-start.1 = (f32[3,16,8,128]{3,2,1,0:T(8,128)}, f32[3,16,8,128]{3,2,1,0:T(8,128)S(1)}, u32[]{:S(2)}, u32[]{:S(2)}) collective-permute-start(f32[3,16,8,128]{3,2,1,0:T(8,128)} %get-tuple-element.17), channel_id=1, source_target_pairs={{0,28},{4,8},{8,4},{12,16},{16,12},{20,24},{24,20},{28,0},{1,29},{... | collective-permute-start | bytes 589832 | tf_op jit(solution)/shard_map/ppermute | solution.py:450
  9.0 13.6 %collective-permute-start.2 = (f32[3,16,8,128]{3,2,1,0:T(8,128)}, f32[3,16,8,128]{3,2,1,0:T(8,128)S(1)}, u32[]{:S(2)}, u32[]{:S(2)}) collective-permute-start(f32[3,16,8,128]{3,2,1,0:T(8,128)} %get-tuple-element.18), channel_id=1, source_target_pairs={{0,24},{4,28},{8,16},{12,20},{16,8},{20,12},{24,0},{28,4},{1,25},{... | collective-permute-start | bytes 589832 | tf_op jit(solution)/shard_map/ppermute | solution.py:450
  12.0 14.9 %collective-permute-start.3 = (f32[3,16,8,128]{3,2,1,0:T(8,128)}, f32[3,16,8,128]{3,2,1,0:T(8,128)S(1)}, u32[]{:S(2)}, u32[]{:S(2)}) collective-permute-start(f32[3,16,8,128]{3,2,1,0:T(8,128)} %get-tuple-element.19), channel_id=1, source_target_pairs={{0,4},{4,0},{8,12},{12,8},{16,24},{20,28},{24,16},{28,20},{1,5},{5... | collective-permute-start | bytes 589832 | tf_op jit(solution)/shard_map/ppermute | solution.py:450
  12.1 0.8 %copy-start.4 = (s32[4,16,128]{2,1,0:T(8,128)S(1)}, s32[4,16,128]{2,1,0:T(8,128)}, u32[]{:S(2)}) copy-start(s32[4,16,128]{2,1,0:T(8,128)} %get-tuple-element.23.table_ref) | copy-start | bytes 98308
  12.8 1.1 %copy-start.7 = (f32[3,63,8,128]{3,2,1,0:T(8,128)S(1)}, f32[3,63,8,128]{3,2,1,0:T(8,128)}, u32[]{:S(2)}) copy-start(f32[3,63,8,128]{3,2,1,0:T(8,128)} %get-tuple-element.24) | copy-start | bytes 2322436
  13.9 1.2 %copy-start.11 = (f32[1,16,8,128]{3,2,1,0:T(8,128)S(1)}, f32[1,16,8,128]{3,2,1,0:T(8,128)}, u32[]{:S(2)}) copy-start(f32[1,16,8,128]{3,2,1,0:T(8,128)} %get-tuple-element.22) | copy-start | bytes 196612
  13.9 2.5 %copy-start = (f32[9,56,128]{2,1,0:T(8,128)S(1)}, f32[9,56,128]{2,1,0:T(8,128)}, u32[]{:S(2)}) copy-start(f32[9,56,128]{2,1,0:T(8,128)} %state_ref.1) | copy-start | bytes 774148
  13.9 2.5 %copy-start.2 = (f32[3,9,9,128]{3,0,2,1:T(4,128)S(1)}, f32[3,9,9,128]{3,0,2,1:T(4,128)}, u32[]{:S(2)}) copy-start(f32[3,9,9,128]{3,0,2,1:T(4,128)} %param.18) | copy-start | bytes 373252
  13.9 2.5 %copy-start.5 = (s32[4,16,128]{2,1,0:T(8,128)S(1)}, s32[4,16,128]{2,1,0:T(8,128)}, u32[]{:S(2)}) copy-start(s32[4,16,128]{2,1,0:T(8,128)} %get-tuple-element.23.table_ref) | copy-start | bytes 98308
  14.0 2.5 %copy-start.6 = (f32[4,12,56,56]{3,2,1,0:T(8,128)S(1)}, f32[4,12,56,56]{3,2,1,0:T(8,128)}, u32[]{:S(2)}) copy-start(f32[4,12,56,56]{3,2,1,0:T(8,128)} %neighbour_ref.1) | copy-start | bytes 1806340
  14.0 2.5 %copy-start.8 = (f32[4,9,9,128]{3,0,2,1:T(4,128)S(1)}, f32[4,9,9,128]{3,0,2,1:T(4,128)}, u32[]{:S(2)}) copy-start(f32[4,9,9,128]{3,0,2,1:T(4,128)} %param.19) | copy-start | bytes 497668
  14.0 2.5 %copy-start.9 = (f32[4,56,56]{2,1,0:T(8,128)S(1)}, f32[4,56,56]{2,1,0:T(8,128)}, u32[]{:S(2)}) copy-start(f32[4,56,56]{2,1,0:T(8,128)} %local_ref.1) | copy-start | bytes 150532
  14.0 2.5 %copy-start.10 = (f32[3,56,56]{2,1,0:T(8,128)S(1)}, f32[3,56,56]{2,1,0:T(8,128)}, u32[]{:S(2)}) copy-start(f32[3,56,56]{2,1,0:T(8,128)} %volume_ref.1) | copy-start | bytes 112900
  15.1 11.8 %collective-permute-start.5 = (f32[2,16,8,128]{3,2,1,0:T(8,128)S(1)}, f32[2,16,8,128]{3,2,1,0:T(8,128)S(1)}, u32[]{:S(2)}, u32[]{:S(2)}) collective-permute-start(f32[2,16,8,128]{3,2,1,0:T(8,128)S(1)} %pad_maximum_fusion), channel_id=1, source_target_pairs={{0,2},{1,3},{2,0},{3,1},{4,6},{5,7},{6,4},{7,5},{8,10},{9,11},{10,... | collective-permute-start | bytes 393224 | tf_op jit(solution)/shard_map/ppermute | solution.py:454
  16.5 10.5 %copy-start.1 = (f32[4,9,9,128]{3,0,2,1:T(4,128)S(1)}, f32[4,9,9,128]{3,0,2,1:T(4,128)}, u32[]{:S(2)}) copy-start(f32[4,9,9,128]{3,0,2,1:T(4,128)} %param.20) | copy-start | bytes 497668
  16.5 10.5 %copy-start.3 = (f32[16,8,128]{2,1,0:T(8,128)S(1)}, f32[16,8,128]{2,1,0:T(8,128)}, u32[]{:S(2)}) copy-start(f32[16,8,128]{2,1,0:T(8,128)} %get-tuple-element.20.first_ref) | copy-start | bytes 196612

commit v11 on v10

--- a/solution.py
+++ b/solution.py
@@ -75,13 +75,15 @@
     return factors
 
 
-def pairing_blocks(region):
+def pairing_blocks(region, sub):
     half = region // 4 % 2
     second = region // 2 % 2
     odd = region % 2
     near, beside = 3 - 3 * second, 2 - odd
     turn = half * (beside - near)
-    return [near + turn, 1 + odd, 3 * second, beside - turn]
+    far_side, side = 3 * second, 1 + odd
+    swap = sub % 2 * (side - far_side)
+    return [near + turn, far_side + swap, side - swap, beside - turn]
 
 
 def predict_kernel(
@@ -178,7 +180,7 @@
     per_quant = modes // 8
     count = quants * per_quant
     odd, high = odd_and_high((8, lanes))
-    lists = pairing_blocks(region_index_ref[0])
+    lists = pairing_blocks(region_index_ref[0], sub_index_ref[0])
     index = []
     for cluster in range(clusters):
         base = jnp.concatenate(
@@ -199,7 +201,7 @@
         leaving[-1].start()
 
     here = sub_index_ref[0]
-    brought = pairing_blocks(region_index_ref[0])
+    brought = pairing_blocks(region_index_ref[0], sub_index_ref[0])
     cluster_row = cluster_ref[...]
     for face in range(face_ref.shape[0]):
         entry = face_ref[pl.ds(face, 1), :]
@@ -441,13 +443,14 @@
     return [pl.BlockSpec(memory_space=pltpu.HBM) for _ in range(count)]
 
 
-def paired(value, axis, pairing):
-    count = lax.axis_size(axis)
+def paired(value, place):
+    regions, subs = lax.axis_size("region"), lax.axis_size("sub")
     pairs = []
-    for source in range(count):
-        offset = OFFSETS[pairing_blocks(source)[pairing]]
-        pairs.append((source, (source + offset) % count))
-    return lax.ppermute(value, axis, pairs)
+    for region in range(regions):
+        for sub in range(subs):
+            offset = OFFSETS[pairing_blocks(region, sub)[place]]
+            pairs.append((region * subs + sub, (region + offset) % regions * subs + sub))
+    return lax.ppermute(value, ("region", "sub"), pairs)
 
 
 def swapped(value, axis, bit):
@@ -532,7 +535,7 @@
         here,
     )
 
-    arrived = [paired(packed[p], "region", p) for p in range(BLOCKS)]
+    arrived = [paired(packed[p], p) for p in range(BLOCKS)]
     first, beside, across = packed[BLOCKS:]
     beside = swapped(beside, "sub", 1)
     across = swapped(jnp.concatenate([across, beside[1:]], axis=0), "sub", 2)

time: 31.6 us -> 30.4 us (0.962)
  waiting for transfers between devices: 7.69 us -> 6.43 us
    ppermute x4, waiting for transfers between devices: 7.69 us -> 6.42 us  [paired(): return lax.ppermute(value, ('region', 'sub'), pairs)]
  transfers between devices with their start and end apart: 6 -> 6, of which waited for: 2 -> 2; matrix products, arithmetic and copies ran while one was open for 0% -> 0% of each run, Pallas kernels for 12% -> 13%
where the time goes in v11:
time: 30.4 us; the launch traced here: 30.1 us
  Pallas kernels  15.1 us (50%)
  starting transfers between devices  6.48 us (21%)
  waiting for transfers between devices  6.43 us (21%)
  local copies, waits for them, and re-layouts  1.94 us (6%)
    pallas_call x1, Pallas kernels, local(): pl.pallas_call(predict_kernel, out_shape=(shape((clusters, count, 8, lane...  6.84 us
    ppermute x4, waiting for transfers between devices, paired(): return lax.ppermute(value, ('region', 'sub'), pairs)  6.42 us
    ppermute x4, starting transfers between devices, paired(): return lax.ppermute(value, ('region', 'sub'), pairs)  4.46 us
    pallas_call x1, Pallas kernels, local(): pl.pallas_call(neighbour_kernel, out_shape=shape((quants, modes, lanes),...  4.43 us
    pallas_call x1, Pallas kernels, local(): pl.pallas_call(own_kernel, out_shape=(shape((quants, modes, lanes), F32),...  2.76 us
    ppermute x2, starting transfers between devices, swapped(): lax.ppermute(value, axis, [(s, s ^ bit) for s in range(lax.axis_size(axis...  2.01 us
    unnamed x24, local copies, waits for them, and re-layouts  1.94 us
    pallas_call x1, Pallas kernels, local(): pl.pallas_call(near_kernel, out_shape=shape((faces, quants, modes, lanes)...  1.08 us
  transfers between devices with their start and end apart: 6, of which 2 were waited for; matrix products, arithmetic and copies ran while one was open for 0% of the time, Pallas kernels for 13%

profile of v11, /device:TPU:25, one launch (start us, length us, event | category | flops | bytes accessed | tf_op | source)
XLA Modules:
  0.0 30.1 jit_solution(2908121676039938330)
XLA Ops:
  0.0 6.8 %predict.1 = (f32[3,63,8,128]{3,2,1,0:T(8,128)}, s32[4,16,128]{2,1,0:T(8,128)}, f32[3,16,8,128]{3,2,1,0:T(8,128)}, f32[3,16,8,128]{3,2,1,0:T(8,128)}, f32[3,16,8...) custom-call(f32[9,56,128]{2,1,0:T(8,128)} %state_ref.1, ...), custom_call_target="tpu_custom_call" | custom-call | tf_op jit(solution)/shard_map/predict/pallas_call | solution.py:494
  6.9 0.7 %collective-permute-start.4 = (f32[2,16,8,128]{3,2,1,0:T(8,128)}, f32[2,16,8,128]{3,2,1,0:T(8,128)S(1)}, u32[]{:S(2)}, u32[]{:S(2)}) collective-permute-start(f32[2,16,8,128]{3,2,1,0:T(8,128)} %get-tuple-element.21), channel_id=1, source_target_pairs={{0,1},{1,0},{2,3},{3,2},{4,5},{5,4},{6,7},{7,6},{8,9},{9,8},{10,11... | collective-permute-start | bytes 393224 | tf_op jit(solution)/shard_map/ppermute | solution.py:457
  7.6 1.3 %collective-permute-start = (f32[3,16,8,128]{3,2,1,0:T(8,128)}, f32[3,16,8,128]{3,2,1,0:T(8,128)S(1)}, u32[]{:S(2)}, u32[]{:S(2)}) collective-permute-start(f32[3,16,8,128]{3,2,1,0:T(8,128)} %get-tuple-element.16), channel_id=1, source_target_pairs={{0,8},{1,9},{2,10},{3,11},{4,12},{5,13},{6,14},{7,15},{8,0},{9,1},... | collective-permute-start | bytes 589832 | tf_op jit(solution)/shard_map/ppermute | solution.py:453
  8.8 0.1 collective-permute-start.1
  9.0 3.1 %collective-permute-start.2 = (f32[3,16,8,128]{3,2,1,0:T(8,128)}, f32[3,16,8,128]{3,2,1,0:T(8,128)S(1)}, u32[]{:S(2)}, u32[]{:S(2)}) collective-permute-start(f32[3,16,8,128]{3,2,1,0:T(8,128)} %get-tuple-element.18), channel_id=1, source_target_pairs={{0,28},{1,25},{2,30},{3,27},{4,8},{5,29},{6,10},{7,31},{8,4},{9,17... | collective-permute-start | bytes 589832 | tf_op jit(solution)/shard_map/ppermute | solution.py:453
  12.1 0.0 collective-permute-start.3
  12.1 0.8 %copy-done.4 = s32[4,16,128]{2,1,0:T(8,128)S(1)} copy-done((s32[4,16,128]{2,1,0:T(8,128)S(1)}, s32[4,16,128]{2,1,0:T(8,128)}, u32[]{:S(2)}) %copy-start.4) | copy-done | bytes 32792
  12.8 1.1 %copy-done.7 = f32[3,63,8,128]{3,2,1,0:T(8,128)S(1)} copy-done((f32[3,63,8,128]{3,2,1,0:T(8,128)S(1)}, f32[3,63,8,128]{3,2,1,0:T(8,128)}, u32[]{:S(2)}) %copy-start.7) | copy-done | bytes 774168
  14.0 0.0 copy-start.6
  14.0 0.0 copy-start.8
  14.0 0.0 copy-start.9
  14.0 0.0 copy-start.10
  14.0 1.1 %near.1.near_ref = f32[4,9,56,128]{3,2,1,0:T(8,128)S(1)} custom-call(s32[4,16,128]{2,1,0:T(8,128)S(1)} %copy-done.4, f32[3,9,56,128]{3,2,1,0:T(8,128)S(1)} %bitcast.12), custom_call_target="tpu_custom_call" | custom-call | flops 4000000000 | bytes 8000000 | tf_op jit(solution)/shard_map/near/pallas_call | solution.py:543
  15.1 0.0 collective-permute-done.4.beside_ref
  15.1 0.0 copy-done.11
  15.1 1.3 %collective-permute-start.5 = (f32[2,16,8,128]{3,2,1,0:T(8,128)S(1)}, f32[2,16,8,128]{3,2,1,0:T(8,128)S(1)}, u32[]{:S(2)}, u32[]{:S(2)}) collective-permute-start(f32[2,16,8,128]{3,2,1,0:T(8,128)S(1)} %pad_maximum_fusion), channel_id=1, source_target_pairs={{0,2},{1,3},{2,0},{3,1},{4,6},{5,7},{6,4},{7,5},{8,10},{9,11},{10,... | collective-permute-start | bytes 393224 | tf_op jit(solution)/shard_map/ppermute | solution.py:457
  16.5 0.0 copy-start.1
  16.5 2.8 %own.1 = (f32[9,56,128]{2,1,0:T(8,128)S(1)}, bf16[4,672,176]{2,1,0:T(8,128)(2,1)S(1)}) custom-call(s32[4,16,128]{2,1,0:T(8,128)S(1)} %copy-done.5, f32[3,56,56]{2,1,0:T(8,128)S(1)} %copy-done.10, f32[4,56,56]{2,1,0:T(8,128)S(1)} %copy-done.9, f32[3,9,56,128]{3,2,1,0:T(8,128)S(1)} %bitcast.13, f32[9,56,128]{2,1,0:T(8,128)S(1)} %copy-done, ...), custom_call_target="tpu_custom_call" | custom-call | flops 4000000000 | bytes 8000000 | tf_op jit(solution)/shard_map/own/pallas_call | solution.py:555
  19.3 0.0 collective-permute-done.region_refs_0_
  19.3 0.0 collective-permute-done.1.region_refs_1_
  19.3 3.1 %collective-permute-done.2.region_refs_2_ = f32[3,16,8,128]{3,2,1,0:T(8,128)S(1)} collective-permute-done((f32[3,16,8,128]{3,2,1,0:T(8,128)}, f32[3,16,8,128]{3,2,1,0:T(8,128)S(1)}, u32[]{:S(2)}, u32[]{:S(2)}) %collective-permute-start.2) | collective-permute-done | bytes 196640 | tf_op jit(solution)/shard_map/ppermute | solution.py:453
  22.3 3.4 %collective-permute-done.3.region_refs_3_ = f32[3,16,8,128]{3,2,1,0:T(8,128)S(1)} collective-permute-done((f32[3,16,8,128]{3,2,1,0:T(8,128)}, f32[3,16,8,128]{3,2,1,0:T(8,128)S(1)}, u32[]{:S(2)}, u32[]{:S(2)}) %collective-permute-start.3) | collective-permute-done | bytes 196640 | tf_op jit(solution)/shard_map/ppermute | solution.py:453
  25.7 0.0 collective-permute-done.5.across_ref
  25.7 4.4 %neighbour.1 = f32[9,56,128]{2,1,0:T(8,128)} custom-call(f32[3,16,8,128]{3,2,1,0:T(8,128)S(1)} %collective-permute-done.region_refs_0_, f32[3,16,8,128]{3,2,1,0:T(8,128)S(1)} %collective-permute-done.1.region_refs_1_, f32[3,16,8,128]{3,2,1,0:T(8,128)S(1)} %collective-permute-done.2.region_refs_2_, ...), custom_call_target="tpu_custom_call" | custom-call | tf_op jit(solution)/shard_map/neighbour/pallas_call | solution.py:583
  (18 shorter events, 0.0 us)
Async XLA Ops:
  6.9 8.2 %collective-permute-start.4 = (f32[2,16,8,128]{3,2,1,0:T(8,128)}, f32[2,16,8,128]{3,2,1,0:T(8,128)S(1)}, u32[]{:S(2)}, u32[]{:S(2)}) collective-permute-start(f32[2,16,8,128]{3,2,1,0:T(8,128)} %get-tuple-element.21), channel_id=1, source_target_pairs={{0,1},{1,0},{2,3},{3,2},{4,5},{5,4},{6,7},{7,6},{8,9},{9,8},{10,11... | collective-permute-start | bytes 393224 | tf_op jit(solution)/shard_map/ppermute | solution.py:457
  7.6 11.7 %collective-permute-start = (f32[3,16,8,128]{3,2,1,0:T(8,128)}, f32[3,16,8,128]{3,2,1,0:T(8,128)S(1)}, u32[]{:S(2)}, u32[]{:S(2)}) collective-permute-start(f32[3,16,8,128]{3,2,1,0:T(8,128)} %get-tuple-element.16), channel_id=1, source_target_pairs={{0,8},{1,9},{2,10},{3,11},{4,12},{5,13},{6,14},{7,15},{8,0},{9,1},... | collective-permute-start | bytes 589832 | tf_op jit(solution)/shard_map/ppermute | solution.py:453
  8.8 10.4 %collective-permute-start.1 = (f32[3,16,8,128]{3,2,1,0:T(8,128)}, f32[3,16,8,128]{3,2,1,0:T(8,128)S(1)}, u32[]{:S(2)}, u32[]{:S(2)}) collective-permute-start(f32[3,16,8,128]{3,2,1,0:T(8,128)} %get-tuple-element.17), channel_id=1, source_target_pairs={{0,24},{1,29},{2,26},{3,31},{4,28},{5,9},{6,30},{7,11},{8,16},{9,5... | collective-permute-start | bytes 589832 | tf_op jit(solution)/shard_map/ppermute | solution.py:453
  9.0 13.4 %collective-permute-start.2 = (f32[3,16,8,128]{3,2,1,0:T(8,128)}, f32[3,16,8,128]{3,2,1,0:T(8,128)S(1)}, u32[]{:S(2)}, u32[]{:S(2)}) collective-permute-start(f32[3,16,8,128]{3,2,1,0:T(8,128)} %get-tuple-element.18), channel_id=1, source_target_pairs={{0,28},{1,25},{2,30},{3,27},{4,8},{5,29},{6,10},{7,31},{8,4},{9,17... | collective-permute-start | bytes 589832 | tf_op jit(solution)/shard_map/ppermute | solution.py:453
  12.1 13.6 %collective-permute-start.3 = (f32[3,16,8,128]{3,2,1,0:T(8,128)}, f32[3,16,8,128]{3,2,1,0:T(8,128)S(1)}, u32[]{:S(2)}, u32[]{:S(2)}) collective-permute-start(f32[3,16,8,128]{3,2,1,0:T(8,128)} %get-tuple-element.19), channel_id=1, source_target_pairs={{0,4},{1,5},{2,6},{3,7},{4,0},{5,1},{6,2},{7,3},{8,12},{9,13},{10,... | collective-permute-start | bytes 589832 | tf_op jit(solution)/shard_map/ppermute | solution.py:453
  12.1 0.8 %copy-start.4 = (s32[4,16,128]{2,1,0:T(8,128)S(1)}, s32[4,16,128]{2,1,0:T(8,128)}, u32[]{:S(2)}) copy-start(s32[4,16,128]{2,1,0:T(8,128)} %get-tuple-element.23.table_ref) | copy-start | bytes 98308
  12.8 1.1 %copy-start.7 = (f32[3,63,8,128]{3,2,1,0:T(8,128)S(1)}, f32[3,63,8,128]{3,2,1,0:T(8,128)}, u32[]{:S(2)}) copy-start(f32[3,63,8,128]{3,2,1,0:T(8,128)} %get-tuple-element.24) | copy-start | bytes 2322436
  13.9 1.2 %copy-start.11 = (f32[1,16,8,128]{3,2,1,0:T(8,128)S(1)}, f32[1,16,8,128]{3,2,1,0:T(8,128)}, u32[]{:S(2)}) copy-start(f32[1,16,8,128]{3,2,1,0:T(8,128)} %get-tuple-element.22) | copy-start | bytes 196612
  13.9 2.5 %copy-start = (f32[9,56,128]{2,1,0:T(8,128)S(1)}, f32[9,56,128]{2,1,0:T(8,128)}, u32[]{:S(2)}) copy-start(f32[9,56,128]{2,1,0:T(8,128)} %state_ref.1) | copy-start | bytes 774148
  13.9 2.5 %copy-start.2 = (f32[3,9,9,128]{3,0,2,1:T(4,128)S(1)}, f32[3,9,9,128]{3,0,2,1:T(4,128)}, u32[]{:S(2)}) copy-start(f32[3,9,9,128]{3,0,2,1:T(4,128)} %param.18) | copy-start | bytes 373252
  13.9 2.5 %copy-start.5 = (s32[4,16,128]{2,1,0:T(8,128)S(1)}, s32[4,16,128]{2,1,0:T(8,128)}, u32[]{:S(2)}) copy-start(s32[4,16,128]{2,1,0:T(8,128)} %get-tuple-element.23.table_ref) | copy-start | bytes 98308
  14.0 2.5 %copy-start.6 = (f32[4,12,56,56]{3,2,1,0:T(8,128)S(1)}, f32[4,12,56,56]{3,2,1,0:T(8,128)}, u32[]{:S(2)}) copy-start(f32[4,12,56,56]{3,2,1,0:T(8,128)} %neighbour_ref.1) | copy-start | bytes 1806340
  14.0 2.5 %copy-start.8 = (f32[4,9,9,128]{3,0,2,1:T(4,128)S(1)}, f32[4,9,9,128]{3,0,2,1:T(4,128)}, u32[]{:S(2)}) copy-start(f32[4,9,9,128]{3,0,2,1:T(4,128)} %param.19) | copy-start | bytes 497668
  14.0 2.5 %copy-start.9 = (f32[4,56,56]{2,1,0:T(8,128)S(1)}, f32[4,56,56]{2,1,0:T(8,128)}, u32[]{:S(2)}) copy-start(f32[4,56,56]{2,1,0:T(8,128)} %local_ref.1) | copy-start | bytes 150532
  14.0 2.5 %copy-start.10 = (f32[3,56,56]{2,1,0:T(8,128)S(1)}, f32[3,56,56]{2,1,0:T(8,128)}, u32[]{:S(2)}) copy-start(f32[3,56,56]{2,1,0:T(8,128)} %volume_ref.1) | copy-start | bytes 112900
  15.1 10.5 %collective-permute-start.5 = (f32[2,16,8,128]{3,2,1,0:T(8,128)S(1)}, f32[2,16,8,128]{3,2,1,0:T(8,128)S(1)}, u32[]{:S(2)}, u32[]{:S(2)}) collective-permute-start(f32[2,16,8,128]{3,2,1,0:T(8,128)S(1)} %pad_maximum_fusion), channel_id=1, source_target_pairs={{0,2},{1,3},{2,0},{3,1},{4,6},{5,7},{6,4},{7,5},{8,10},{9,11},{10,... | collective-permute-start | bytes 393224 | tf_op jit(solution)/shard_map/ppermute | solution.py:457
  16.5 9.2 %copy-start.1 = (f32[4,9,9,128]{3,0,2,1:T(4,128)S(1)}, f32[4,9,9,128]{3,0,2,1:T(4,128)}, u32[]{:S(2)}) copy-start(f32[4,9,9,128]{3,0,2,1:T(4,128)} %param.20) | copy-start | bytes 497668
  16.5 9.2 %copy-start.3 = (f32[16,8,128]{2,1,0:T(8,128)S(1)}, f32[16,8,128]{2,1,0:T(8,128)}, u32[]{:S(2)}) copy-start(f32[16,8,128]{2,1,0:T(8,128)} %get-tuple-element.20.first_ref) | copy-start | bytes 196612
